TPU v7x, 32 devices: a whole 2x2x4 slice. The times are simulated.
32 devices in a mesh: head: 4 (over x, core), tok: 8 (over z, y).
Axes of the slice: x: 2, y: 2, z: 4, core: 2. Of those that a mesh axis runs over, the one named last changes fastest.
Arguments:
- residual_in: bfloat16 [4096, 768], P('tok', 'head')
- cotangent: bfloat16 [4096, 768], P('tok', 'head'), may hold values from -6 to 6
- w_qkv: bfloat16 [2, 768, 3, 768], P(None, None, None, 'head'), may hold values from -0.21875 to 0.21875
- b_qv: bfloat16 [2, 2, 768], P(None, None, 'head'), may hold values from -2 to 2
- w_out: bfloat16 [2, 768, 768], P(None, 'head'), may hold values from -0.875 to 0.875
- b_out: bfloat16 [2, 768], P(None, 'head'), may hold values from -2 to 2
- w_up: bfloat16 [2, 768, 3072], P(None, None, 'head')
- b_up: bfloat16 [2, 3072], P(None, 'head'), may hold values from -2 to 2
- w_down: bfloat16 [2, 3072, 768], P(None, 'head'), may hold values from -0.109375 to 0.109375
- b_down: bfloat16 [2, 768], P(None, 'head'), may hold values from -2 to 2
- ln_gain: bfloat16 [2, 2, 768], P(None, None, 'head'), may hold values from 0.5 to 1.5
- ln_bias: bfloat16 [2, 2, 768], P(None, None, 'head'), may hold values from -1.1953125 to 1.1953125
- selection: int32 [12, 64, 4], P('head'), may hold values from 0 to 255, as said below
- lengths: int32 [2], replicated, may hold values from 128 to 3968, as said below
- valid: int32 [4096], replicated, may hold values 0 or 1
Outputs:
- residual_out: bfloat16 [4096, 768], P('tok', 'head')
- grad_residual: bfloat16 [4096, 768], P('tok', 'head')
- grad_w_qkv: float32 [2, 768, 3, 768], P(None, None, None, 'head')
- grad_b_qv: float32 [2, 2, 768], P(None, None, 'head')
- grad_w_out: float32 [2, 768, 768], P(None, 'head')
- grad_b_out: float32 [2, 768], P(None, 'head')
- grad_w_up: float32 [2, 768, 3072], P(None, None, 'head')
- grad_b_up: float32 [2, 3072], P(None, 'head')
- grad_w_down: float32 [2, 3072, 768], P(None, 'head')
- grad_b_down: float32 [2, 768], P(None, 'head')
- grad_ln_gain: float32 [2, 2, 768], P(None, None, 'head')
- grad_ln_bias: float32 [2, 2, 768], P(None, None, 'head')
- statistics: float32 [2, 3], replicated
Inputs may be any that keep to these rules, and one draw needn't show every extreme that they name: `lengths`: two sequences laid end to end that fill all 4096 tokens, in either order; the shorter has 128 tokens. `selection`: where a query block has usable blocks in its sequence ending 64 or more tokens before it, each slot names one of them, and slot 0 names one of the 8 latest of them; otherwise the slot holds 255.
All inputs are finite; a program needn't handle non-finite values.
Results may differ from a plain program's by a relative error of at most 0.03.
Values may be sent and summed in bfloat16 or wider, within the bound.
No kernel may reach another device: no remote copies, remote signals or barrier semaphores. Data moves between devices by JAX's collectives and lax.ppermute only.
A program may use at most 256 MiB of HBM per device.

v0:
```python
import jax
import jax.numpy as jnp
from jax import lax
from jax.sharding import PartitionSpec as P

D = 768
HD = 64
LAYERS = 2
WINDOW = 64
KB = 16
SEL = 4
QB = 64


epsilon = 1e-05
negative = -1e30
highest = lax.Precision.HIGHEST


def passed_along(value, axis, steps):
    count = lax.axis_size(axis)
    first, last = (max(0, -steps), min(count, count - steps))
    return lax.ppermute(value, axis, [(source, source + steps) for source in range(first, last)])


def layer_norm_forward(rounded, gain, shift):
    average = jnp.mean(rounded, axis=-1, keepdims=True)
    centred = rounded - average
    spread = jnp.mean(centred * centred, axis=-1, keepdims=True)
    inverse = lax.rsqrt(spread + epsilon)
    unit_vec = centred * inverse
    return (unit_vec * gain + shift, unit_vec, inverse)


def layer_norm_backward(grad_out, unit_vec, inverse, gain):
    grad_unit = grad_out * gain
    first_mean = jnp.mean(grad_unit, axis=-1, keepdims=True)
    second_mean = jnp.mean(grad_unit * unit_vec, axis=-1, keepdims=True)
    grad_in = inverse * (grad_unit - first_mean - unit_vec * second_mean)
    return (grad_in, jnp.sum(grad_out * unit_vec, axis=0), jnp.sum(grad_out, axis=0))


def gather_norm_input(residual, gain, shift):
    rounded = residual.astype(jnp.bfloat16)
    gathered, gain_all, shift_all = (
        lax.all_gather(rounded, "head", axis=1, tiled=True),
        lax.all_gather(gain, "head", axis=0, tiled=True),
        lax.all_gather(shift, "head", axis=0, tiled=True),
    )
    gain_wide = gain_all.astype(jnp.float32)
    normed, unit_vec, inverse = layer_norm_forward(
        gathered.astype(jnp.float32), gain_wide, shift_all.astype(jnp.float32)
    )
    return (normed.astype(jnp.bfloat16), unit_vec, inverse, gain_wide)


def head_sum(partial_sum):
    return lax.psum_scatter(
        partial_sum.astype(jnp.bfloat16), "head", scatter_dimension=1, tiled=True
    ).astype(jnp.float32)


def gather_branch_grad(grad_low):
    return lax.all_gather(grad_low, "head", axis=1, tiled=True)


def scatter_norm_grad(grad_rounded, grad_gain, grad_shift):
    return (
        lax.psum_scatter(
            grad_rounded.astype(jnp.bfloat16), "head", scatter_dimension=1, tiled=True
        ).astype(jnp.float32),
        lax.psum_scatter(
            grad_gain.astype(jnp.bfloat16), "head", scatter_dimension=0, tiled=True
        ).astype(jnp.float32),
        lax.psum_scatter(
            grad_shift.astype(jnp.bfloat16), "head", scatter_dimension=0, tiled=True
        ).astype(jnp.float32),
    )


def gelu_tanh(value):
    return jax.nn.gelu(value, approximate=True)


def gelu_backward(inner_act, grad_hidden):
    return jax.vjp(gelu_tanh, inner_act)[1](grad_hidden)[0]


def attention_masks(chosen, valid, boundary, first_row, row_count):
    head_count, block_count, pick_count = chosen.shape
    query_pos = first_row + jnp.arange(row_count, dtype=jnp.int32)
    key_pos = first_row - WINDOW + jnp.arange(row_count + WINDOW, dtype=jnp.int32)
    padded_valid = jnp.concatenate([jnp.zeros((WINDOW,), jnp.int32), valid])
    key_valid = lax.dynamic_slice_in_dim(padded_valid, first_row, row_count + WINDOW) > 0
    query_seq = query_pos >= boundary
    key_seq = key_pos >= boundary
    query_col = query_pos[:, None]
    key_line = key_pos[None, :]
    window_ok = (key_line <= query_col) & (key_line > query_col - WINDOW) & (key_line >= 0)
    window_ok = (
        window_ok
        & (key_seq[None, :] == query_seq[:, None])
        & (key_valid[None, :] | (key_line == query_col))
    )
    token_index = (chosen[..., None] * KB + jnp.arange(KB, dtype=jnp.int32)).reshape(
        head_count, block_count, pick_count * KB
    )
    block_first = first_row + QB * jnp.arange(block_count, dtype=jnp.int32)
    early = chosen[..., None] * KB + KB <= block_first[None, :, None, None] - WINDOW
    early = jnp.broadcast_to(early, (head_count, block_count, pick_count, KB)).reshape(
        head_count, block_count, pick_count * KB
    )
    picked_valid = jnp.take(valid, token_index) > 0
    picked_seq = token_index >= boundary
    query_blocks = query_seq.reshape(block_count, QB)
    picked_ok = (
        early[:, :, None, :]
        & picked_valid[:, :, None, :]
        & (picked_seq[:, :, None, :] == query_blocks[None, :, :, None])
    )
    return (window_ok, picked_ok.reshape(head_count, row_count, pick_count * KB))


def attention_scores(queries, window_kv, picked_kv, window_ok, picked_ok):
    row_count, head_count, head_size = queries.shape
    block_count = picked_kv.shape[1]
    near = jnp.einsum(
        "qhd,khd->hqk", queries, window_kv[..., :head_size], preferred_element_type=jnp.float32
    )
    grouped = queries.reshape(block_count, QB, head_count, head_size)
    far = jnp.einsum(
        "bqhd,hbjd->hbqj", grouped, picked_kv[..., :head_size], preferred_element_type=jnp.float32
    )
    joined = jnp.concatenate([near, far.reshape(head_count, row_count, -1)], axis=-1)
    allowed = jnp.concatenate(
        [jnp.broadcast_to(window_ok, (head_count,) + window_ok.shape), picked_ok], axis=-1
    )
    return jnp.where(allowed, joined, negative)


def attention_output(weights, window_kv, picked_kv):
    head_count = weights.shape[0]
    row_count = weights.shape[1]
    width = window_kv.shape[0]
    head_size = window_kv.shape[-1] // 2
    block_count = picked_kv.shape[1]
    near_out = jnp.einsum(
        "hqk,khd->qhd",
        weights[..., :width],
        window_kv[..., head_size:],
        preferred_element_type=jnp.float32,
    )
    far_weights = weights[..., width:].reshape(head_count, block_count, QB, -1)
    far_out = jnp.einsum(
        "hbqj,hbjd->bqhd",
        far_weights,
        picked_kv[..., head_size:],
        preferred_element_type=jnp.float32,
    )
    return near_out + far_out.reshape(row_count, head_count, head_size)


def attention_backward(queries, window_kv, picked_kv, window_ok, picked_ok, log_total, grad_out):
    row_count, head_count, head_size = queries.shape
    block_count = picked_kv.shape[1]
    width = window_kv.shape[0]
    masked = attention_scores(queries, window_kv, picked_kv, window_ok, picked_ok)
    probs_exact = jnp.exp(masked - log_total)
    probs_low = probs_exact.astype(jnp.bfloat16)
    grad_grouped = grad_out.reshape(block_count, QB, head_count, head_size)
    near_grad = jnp.einsum(
        "qhd,khd->hqk", grad_out, window_kv[..., head_size:], preferred_element_type=jnp.float32
    )
    far_grad = jnp.einsum(
        "bqhd,hbjd->hbqj",
        grad_grouped,
        picked_kv[..., head_size:],
        preferred_element_type=jnp.float32,
    )
    grad_probs = jnp.concatenate([near_grad, far_grad.reshape(head_count, row_count, -1)], axis=-1)
    inner_sum = jnp.sum(probs_exact * grad_probs, axis=-1, keepdims=True)
    grad_scores = (probs_exact * (grad_probs - inner_sum)).astype(jnp.bfloat16)
    near_scores = grad_scores[..., :width]
    far_scores = grad_scores[..., width:].reshape(head_count, block_count, QB, -1)
    far_probs = probs_low[..., width:].reshape(head_count, block_count, QB, -1)
    grouped = queries.reshape(block_count, QB, head_count, head_size)
    grad_query = jnp.einsum(
        "hqk,khd->qhd", near_scores, window_kv[..., :head_size], preferred_element_type=jnp.float32
    )
    far_query = jnp.einsum(
        "hbqj,hbjd->bqhd",
        far_scores,
        picked_kv[..., :head_size],
        preferred_element_type=jnp.float32,
    )
    grad_query = grad_query + far_query.reshape(row_count, head_count, head_size)
    near_keys = jnp.einsum("hqk,qhd->khd", near_scores, queries, preferred_element_type=jnp.float32)
    near_values = jnp.einsum(
        "hqk,qhd->khd", probs_low[..., :width], grad_out, preferred_element_type=jnp.float32
    )
    far_keys = jnp.einsum(
        "hbqj,bqhd->hbjd", far_scores, grouped, preferred_element_type=jnp.float32
    )
    far_values = jnp.einsum(
        "hbqj,bqhd->hbjd", far_probs, grad_grouped, preferred_element_type=jnp.float32
    )
    return (
        grad_query,
        jnp.concatenate([near_keys, near_values], axis=-1),
        jnp.concatenate([far_keys, far_values], axis=-1),
        inner_sum,
    )


def on_device(
    residual_in,
    cotangent,
    w_qkv,
    b_qv,
    w_out,
    b_out,
    w_up,
    b_up,
    w_down,
    b_down,
    ln_gain,
    ln_bias,
    selection,
    lengths,
    valid,
):
    row_count = residual_in.shape[0]
    head_count = selection.shape[0]
    head_size = HD
    scale = HD ** (-0.5)
    block_count = row_count // QB
    kv_blocks = row_count // KB
    position = lax.axis_index("tok")
    first_row = position * row_count
    chosen = lax.dynamic_slice_in_dim(selection, position * block_count, block_count, 1)
    boundary = lengths[0]
    window_ok, picked_ok = attention_masks(chosen, valid, boundary, first_row, row_count)
    mine_valid = lax.dynamic_slice_in_dim(valid, first_row, row_count).astype(jnp.float32)[:, None]
    residual = residual_in.astype(jnp.float32)
    kept_state = []
    local_squares = []
    for layer_index in range(LAYERS):
        normed, unit_first, inverse_first, gain_first = gather_norm_input(
            residual, ln_gain[layer_index, 0], ln_bias[layer_index, 0]
        )
        projected = jnp.dot(
            normed, w_qkv[layer_index].reshape(D, -1), preferred_element_type=jnp.float32
        ).reshape(row_count, 3, -1)
        queries = (
            ((projected[:, 0] + b_qv[layer_index, 0]) * scale)
            .astype(jnp.bfloat16)
            .reshape(row_count, head_count, head_size)
        )
        key_rows = projected[:, 1].astype(jnp.bfloat16).reshape(row_count, head_count, head_size)
        value_rows = (
            (projected[:, 2] + b_qv[layer_index, 1])
            .astype(jnp.bfloat16)
            .reshape(row_count, head_count, head_size)
        )
        own_kv = jnp.concatenate([key_rows, value_rows], axis=-1)
        halo_kv = passed_along(own_kv[row_count - WINDOW :], "tok", 1)
        window_kv = jnp.concatenate([halo_kv, own_kv], axis=0)
        own_blocks = own_kv.reshape(kv_blocks, KB, head_count, 2 * head_size)
        shard_piece = lax.all_gather(own_blocks, "tok", axis=0, tiled=True)
        piece_blocks = shard_piece.shape[0]
        onehot = (chosen[..., None] == jnp.arange(piece_blocks, dtype=jnp.int32)).astype(
            jnp.bfloat16
        )
        collected = jnp.einsum(
            "hbsc,ckhe->hbske", onehot, shard_piece, preferred_element_type=jnp.float32
        )
        picked_kv = collected.astype(jnp.bfloat16).reshape(
            head_count, block_count, SEL * KB, 2 * head_size
        )
        masked = attention_scores(queries, window_kv, picked_kv, window_ok, picked_ok)
        maximum = jnp.max(masked, axis=-1, keepdims=True)
        exponent = jnp.exp(masked - maximum)
        denominator = jnp.sum(exponent, axis=-1, keepdims=True)
        weights = (exponent / denominator).astype(jnp.bfloat16)
        log_total = maximum + jnp.log(denominator)
        mixed_heads = (
            attention_output(weights, window_kv, picked_kv)
            .reshape(row_count, -1)
            .astype(jnp.bfloat16)
        )
        branch = (
            head_sum(jnp.dot(mixed_heads, w_out[layer_index], preferred_element_type=jnp.float32))
            + b_out[layer_index]
        )
        residual = residual + branch
        normed_second, unit_second, inverse_second, gain_second = gather_norm_input(
            residual, ln_gain[layer_index, 1], ln_bias[layer_index, 1]
        )
        inner_act = (
            jnp.dot(normed_second, w_up[layer_index], preferred_element_type=jnp.float32)
            + b_up[layer_index]
        )
        hidden = gelu_tanh(inner_act).astype(jnp.bfloat16)
        second = (
            head_sum(jnp.dot(hidden, w_down[layer_index], preferred_element_type=jnp.float32))
            + b_down[layer_index]
        )
        residual = residual + second
        local_squares.append(
            jnp.stack(
                [
                    jnp.sum(mine_valid * residual * residual),
                    jnp.sum(mine_valid * branch * branch),
                    jnp.sum(mine_valid * second * second),
                ]
            )
        )
        kept_state.append(
            (
                normed,
                unit_first,
                inverse_first,
                gain_first,
                queries,
                window_kv,
                picked_kv,
                log_total,
                mixed_heads,
                normed_second,
                unit_second,
                inverse_second,
                gain_second,
                inner_act,
                hidden,
            )
        )
    residual_out = residual.astype(jnp.bfloat16)
    square_sums = lax.psum(jnp.stack(local_squares), ("head", "tok"))
    valid_count = jnp.maximum(jnp.sum(valid.astype(jnp.float32)), 1.0)
    statistics = jnp.sqrt(square_sums / (valid_count * D))
    gradient = cotangent.astype(jnp.float32)
    layer_grads = [None] * LAYERS
    for layer_index in reversed(range(LAYERS)):
        (
            normed,
            unit_first,
            inverse_first,
            gain_first,
            queries,
            window_kv,
            picked_kv,
            log_total,
            mixed_heads,
            normed_second,
            unit_second,
            inverse_second,
            gain_second,
            inner_act,
            hidden,
        ) = kept_state[layer_index]
        second_low = gradient.astype(jnp.bfloat16)
        second_full = gather_branch_grad(second_low)
        grad_b_down = jnp.sum(second_low.astype(jnp.float32), axis=0)
        grad_w_down = jnp.einsum(
            "tf,td->fd", hidden, second_full, preferred_element_type=jnp.float32
        )
        grad_hidden = jnp.einsum(
            "td,fd->tf", second_full, w_down[layer_index], preferred_element_type=jnp.float32
        )
        grad_inner = gelu_backward(inner_act, grad_hidden).astype(jnp.bfloat16)
        grad_b_up = jnp.sum(grad_inner.astype(jnp.float32), axis=0)
        grad_w_up = jnp.einsum(
            "td,tf->df", normed_second, grad_inner, preferred_element_type=jnp.float32
        )
        grad_normed = jnp.einsum(
            "tf,df->td", grad_inner, w_up[layer_index], preferred_element_type=jnp.float32
        )
        grad_rounded, gain_part, shift_part = layer_norm_backward(
            grad_normed, unit_second, inverse_second, gain_second
        )
        back_rows, gain_second_sum, shift_second_sum = scatter_norm_grad(
            grad_rounded, gain_part, shift_part
        )
        gradient = gradient + back_rows
        branch_low = gradient.astype(jnp.bfloat16)
        branch_full = gather_branch_grad(branch_low)
        grad_b_out = jnp.sum(branch_low.astype(jnp.float32), axis=0)
        grad_w_out = jnp.einsum(
            "tc,td->cd", mixed_heads, branch_full, preferred_element_type=jnp.float32
        )
        grad_mixed = jnp.einsum(
            "td,cd->tc", branch_full, w_out[layer_index], preferred_element_type=jnp.float32
        )
        grad_mixed = grad_mixed.astype(jnp.bfloat16).reshape(row_count, head_count, head_size)
        grad_query, grad_window, grad_picked, inner_sum = attention_backward(
            queries, window_kv, picked_kv, window_ok, picked_ok, log_total, grad_mixed
        )
        halo_grad = passed_along(grad_window[:WINDOW].astype(jnp.bfloat16), "tok", -1).astype(
            jnp.float32
        )
        own_grad = grad_window[WINDOW:] + jnp.pad(
            halo_grad, ((row_count - WINDOW, 0), (0, 0), (0, 0))
        )
        picked_grad = grad_picked.reshape(head_count, block_count, SEL, KB, 2 * head_size)
        spread_onehot = (
            chosen[..., None] == jnp.arange(row_count * lax.axis_size("tok") // KB, dtype=jnp.int32)
        ).astype(jnp.float32)
        term = jnp.einsum(
            "hbsc,hbske->ckhe",
            spread_onehot,
            picked_grad,
            precision=highest,
            preferred_element_type=jnp.float32,
        )
        returned = lax.psum_scatter(
            term.reshape(row_count * lax.axis_size("tok"), head_count, 2 * head_size),
            "tok",
            scatter_dimension=0,
            tiled=True,
        )
        own_grad = own_grad + returned
        grad_keys = own_grad[..., :head_size].astype(jnp.bfloat16).reshape(row_count, -1)
        grad_values = own_grad[..., head_size:].astype(jnp.bfloat16).reshape(row_count, -1)
        grad_queries = (grad_query.astype(jnp.bfloat16) * scale).reshape(row_count, -1)
        grad_projected = jnp.concatenate([grad_queries, grad_keys, grad_values], axis=1)
        grad_w_qkv = jnp.einsum(
            "td,tc->dc", normed, grad_projected, preferred_element_type=jnp.float32
        ).reshape(D, 3, -1)
        grad_b_qv = jnp.stack(
            [
                jnp.sum(grad_queries.astype(jnp.float32), axis=0),
                jnp.sum(grad_values.astype(jnp.float32), axis=0),
            ]
        )
        grad_normed = jnp.einsum(
            "tc,dc->td",
            grad_projected,
            w_qkv[layer_index].reshape(D, -1),
            preferred_element_type=jnp.float32,
        )
        grad_rounded, gain_part, shift_part = layer_norm_backward(
            grad_normed, unit_first, inverse_first, gain_first
        )
        back_rows, gain_first_sum, shift_first_sum = scatter_norm_grad(
            grad_rounded, gain_part, shift_part
        )
        gradient = gradient + back_rows
        gain_pair = jnp.stack([gain_first_sum, gain_second_sum])
        shift_pair = jnp.stack([shift_first_sum, shift_second_sum])
        layer_grads[layer_index] = (
            grad_w_qkv,
            grad_b_qv,
            grad_w_out,
            grad_b_out,
            grad_w_up,
            grad_b_up,
            grad_w_down,
            grad_b_down,
            gain_pair,
            shift_pair,
        )
    stacked = [
        jnp.stack([layer_grads[layer_index][member] for layer_index in range(LAYERS)])
        for member in range(10)
    ]
    summed = lax.psum(
        (
            stacked[0],
            stacked[1],
            stacked[2],
            stacked[3],
            stacked[4],
            stacked[5],
            stacked[6],
            stacked[7],
            stacked[8],
            stacked[9],
        ),
        "tok",
    )
    return (
        residual_out,
        gradient.astype(jnp.bfloat16),
        summed[0],
        summed[1],
        summed[2],
        summed[3],
        summed[4],
        summed[5],
        summed[6],
        summed[7],
        summed[8],
        summed[9],
        statistics,
    )


def solution(mesh):
    in_specs = (
        P("tok", "head"),
        P("tok", "head"),
        P(None, None, None, "head"),
        P(None, None, "head"),
        P(None, "head", None),
        P(None, "head"),
        P(None, None, "head"),
        P(None, "head"),
        P(None, "head", None),
        P(None, "head"),
        P(None, None, "head"),
        P(None, None, "head"),
        P("head", None, None),
        P(),
        P(),
    )
    out_specs = (
        P("tok", "head"),
        P("tok", "head"),
        P(None, None, None, "head"),
        P(None, None, "head"),
        P(None, "head", None),
        P(None, "head"),
        P(None, None, "head"),
        P(None, "head"),
        P(None, "head", None),
        P(None, "head"),
        P(None, None, "head"),
        P(None, None, "head"),
        P(),
    )
    return jax.shard_map(
        on_device, mesh=mesh, in_specs=in_specs, out_specs=out_specs, check_vma=False
    )
```

profile of v0, /device:TPU:0, one launch (start us, length us, event | category | flops | bytes accessed | tf_op | source)
XLA Modules:
  0.0 1320.3 jit_solution(18356486946366307057)
XLA Ops:
  12.6 13.3 %all-reduce.22 = (bf16[768]{0:T(1024)(128)(2,1)S(1)}, bf16[768]{0:T(1024)(128)(2,1)S(1)}, bf16[768]{0:T(1024)(128)(2,1)}, bf16[768]{0:T(1024)(128)(2,1)}, bf16[7...) all-reduce(bf16[768]{0:T(1024)(128)(2,1)S(1)} %dynamic-update-slice, ...), channel_id=3, replica_groups=mesh['head'=4,'tok'=8] {'head'}, use_global_device_ids=true, to_apply=%add.4 | all-reduce | flops 6144 | bytes 24576
  25.9 7.7 all_gather.54
  43.8 8.4 gather_fusion
  60.5 43.0 %all-gather.11.cloned.1.call-done = bf16[256,16,3,128]{3,0,1,2:T(8,128)(2,1)} async-done(((bf16[32,16,3,128]{3,0,1,2:T(8,128)(2,1)}), bf16[256,16,3,128]{3,0,1,2:T(8,128)(2,1)}) %all-gather.11.cloned.1.call-update) | async-done | bytes 3145744 | tf_op jit(solution)/shard_map/all_gather | solution.py:269
  135.1 16.8 %reduce-scatter.11.cloned.1.call-done = bf16[512,192]{0,1:T(8,128)(2,1)} async-done(((bf16[512,768]{0,1:T(8,128)(2,1)}), bf16[512,192]{0,1:T(8,128)(2,1)}) %reduce-scatter.11.cloned.1.call-update) | async-done | bytes 196624 | tf_op jit(solution)/shard_map/reduce_scatter | solution.py:58
  153.3 8.2 all_gather.58
  171.8 18.7 %reduce-scatter.13.cloned.1.call-done = bf16[512,192]{0,1:T(8,128)(2,1)} async-done(((bf16[512,768]{0,1:T(8,128)(2,1)}), bf16[512,192]{0,1:T(8,128)(2,1)}) %reduce-scatter.13.cloned.1.call-update) | async-done | bytes 196624 | tf_op jit(solution)/shard_map/reduce_scatter | solution.py:58
  192.7 8.3 all_gather.61
  234.1 45.6 %all-gather.13.cloned.1.call-done = bf16[256,16,3,128]{3,0,1,2:T(8,128)(2,1)} async-done(((bf16[32,16,3,128]{3,0,1,2:T(8,128)(2,1)}), bf16[256,16,3,128]{3,0,1,2:T(8,128)(2,1)}) %all-gather.13.cloned.1.call-update) | async-done | bytes 3145744 | tf_op jit(solution)/shard_map/all_gather | solution.py:269
  309.6 9.8 all_gather.68
  319.4 9.3 reduce-scatter.15.cloned.1.call-done
  330.0 8.2 all_gather.65
  357.0 20.2 %reduce-scatter.19.cloned.1.call-done = bf16[512,192]{0,1:T(8,128)(2,1)} async-done(((bf16[512,768]{0,1:T(8,128)(2,1)}), bf16[512,192]{0,1:T(8,128)(2,1)}) %reduce-scatter.19.cloned.1.call-update) | async-done | bytes 196624 | tf_op jit(solution)/shard_map/reduce_scatter | solution.py:69
  379.0 8.3 all_gather.69
  401.2 7.4 multiply_convert_fusion.1
  419.4 6.7 copy.171
  426.1 6.6 copy.172
  446.0 6.5 collective-permute-done.2
  452.5 99.5 %reduce-scatter.21.cloned.1.call-done = f32[512,3,128]{0,2,1:T(8,128)} async-done(((f32[4096,3,128]{0,2,1:T(8,128)}), f32[512,3,128]{0,2,1:T(8,128)}) %reduce-scatter.21.cloned.1.call-update) | async-done | bytes 786448 | tf_op jit(solution)/shard_map/reduce_scatter | solution.py:415
  564.0 22.5 %reduce-scatter.23.cloned.1.call-done = bf16[512,192]{0,1:T(8,128)(2,1)} async-done(((bf16[512,768]{0,1:T(8,128)(2,1)}), bf16[512,192]{0,1:T(8,128)(2,1)}) %reduce-scatter.23.cloned.1.call-update) | async-done | bytes 196624 | tf_op jit(solution)/shard_map/reduce_scatter | solution.py:69
  588.5 8.4 all_gather.70
  614.2 20.2 %reduce-scatter.25.cloned.1.call-done = bf16[512,192]{0,1:T(8,128)(2,1)} async-done(((bf16[512,768]{0,1:T(8,128)(2,1)}), bf16[512,192]{0,1:T(8,128)(2,1)}) %reduce-scatter.25.cloned.1.call-update) | async-done | bytes 196624 | tf_op jit(solution)/shard_map/reduce_scatter | solution.py:69
  636.5 8.2 all_gather.71
  658.4 5.7 multiply_convert_fusion
  667.5 4.7 convolution_bitcast_fusion
  672.3 6.7 copy.185
  678.9 6.6 copy.186
  708.1 96.8 %reduce-scatter.27.cloned.1.call-done = f32[512,3,128]{0,2,1:T(8,128)} async-done(((f32[4096,3,128]{0,2,1:T(8,128)}), f32[512,3,128]{0,2,1:T(8,128)}) %reduce-scatter.27.cloned.1.call-update) | async-done | bytes 786448 | tf_op jit(solution)/shard_map/reduce_scatter | solution.py:415
  837.8 39.9 %psum.87 = f32[2,3]{1,0:T(2,128)S(1)} all-reduce(f32[2,3]{1,0:T(2,128)S(1)} %pad_maximum_fusion.26), channel_id=1, replica_groups=mesh['head'=4,'tok'=8] {'head','tok'}, use_global_device_ids=true, to_apply=%region_74.75 | all-reduce | flops 6 | bytes 48 | tf_op jit(solution)/shard_map/psum | solution.py:338
  878.9 10.9 all-reduce.21
  890.8 39.8 %all-reduce.19 = (f32[2,2,192]{2,1,0:T(2,128)}, f32[2,192]{1,0:T(2,128)}, f32[2,768]{1,0:T(2,128)}, f32[2,192]{1,0:T(2,128)}, f32[2,2,192]{2,1,0:T(2,128)}, /*index=5*/f32[2,2,192]{2,1,0:T(2,128)}) all-reduce(f32[2,2,192]{2,1,0:T(2,128)S(1)} %pad_maximum_fusion.23, ...), channel_id=1, replica_groups=mesh['head'=4,'tok'=8] {'tok'}, use_global_device_ids=true, to_apply=%region_37.38 | all-reduce | flops 4608 | bytes 36864 | tf_op jit(solution)/shard_map/psum | solution.py:466
  932.4 370.1 %all-reduce.25.cloned.1.call-done = (f32[2,768,3,192]{1,3,2,0:T(8,128)}, f32[2,192,768]{2,1,0:T(8,128)}, f32[2,768,768]{2,1,0:T(8,128)}, f32[2,768,768]{2,1,0:T(8,128)}) async-done(((f32[2,768,3,192]{1,3,2,0:T(8,128)}, f32[2,192,768]{2,1,0:T(8,128)}, f32[2,768,768]{2,1,0:T(8,128)}, f32[2,768,768]{2,1,0:T(8,128)}), (f32[2,768,3,192]{1,3,2,0:T(8,128)}, f32[2,192,768]{2,1,0:T(8,128)}, ...) | async-done | bytes 14155792 | tf_op jit(solution)/shard_map/psum | solution.py:466
  (688 shorter events, 308.9 us)
Async XLA Ops:
  7.2 96.3 %all-gather.11.cloned.1.call-start = ((), (), s32[]{:S(2)}) async-start(), calls=%async_computation.10 | async-start | bytes 3538944 | tf_op jit(solution)/shard_map/all_gather | solution.py:269
  38.9 113.1 %reduce-scatter.11.cloned.1.call-start = ((), (), s32[]{:S(2)}) async-start(), calls=%async_computation.11 | async-start | bytes 983040 | tf_op jit(solution)/shard_map/reduce_scatter | solution.py:58
  39.1 18.6 %collective-permute-start = (bf16[64,3,128]{0,2,1:T(8,128)(2,1)S(1)}, bf16[64,3,128]{0,2,1:T(8,128)(2,1)S(1)}, u32[]{:S(2)}, u32[]{:S(2)}) collective-permute-start(bf16[64,3,128]{0,2,1:T(8,128)(2,1)S(1)} %pad_maximum_fusion.21), channel_id=1, source_target_pairs={{0,1},{1,2},{2,3},{3,4},{4,5},{5,6},{6,7},{8,9},{9,10},{10,11},{11... | collective-permute-start | bytes 147464 | tf_op jit(solution)/shard_map/ppermute | solution.py:23
  130.4 60.2 %reduce-scatter.13.cloned.1.call-start = ((), (), s32[]{:S(2)}) async-start(), calls=%async_computation.12 | async-start | bytes 983040 | tf_op jit(solution)/shard_map/reduce_scatter | solution.py:58
  166.7 113.0 %all-gather.13.cloned.1.call-start = ((), (), s32[]{:S(2)}) async-start(), calls=%async_computation.13 | async-start | bytes 3538944 | tf_op jit(solution)/shard_map/all_gather | solution.py:269
  216.1 112.6 %reduce-scatter.15.cloned.1.call-start = ((), (), s32[]{:S(2)}) async-start(), calls=%async_computation.14 | async-start | bytes 983040 | tf_op jit(solution)/shard_map/reduce_scatter | solution.py:58
  219.4 9.1 collective-permute-start.1
  307.0 70.2 %reduce-scatter.19.cloned.1.call-start = ((), (), s32[]{:S(2)}) async-start(), calls=%async_computation.16 | async-start | bytes 983040 | tf_op jit(solution)/shard_map/reduce_scatter | solution.py:69
  353.4 198.7 %reduce-scatter.21.cloned.1.call-start = ((), (), s32[]{:S(2)}) async-start(), calls=%async_computation.17 | async-start | bytes 7077888 | tf_op jit(solution)/shard_map/reduce_scatter | solution.py:415
  432.7 153.8 %reduce-scatter.23.cloned.1.call-start = ((), (), s32[]{:S(2)}) async-start(), calls=%async_computation.18 | async-start | bytes 983040 | tf_op jit(solution)/shard_map/reduce_scatter | solution.py:69
  443.0 9.5 collective-permute-start.2
  563.9 70.5 %reduce-scatter.25.cloned.1.call-start = ((), (), s32[]{:S(2)}) async-start(), calls=%async_computation.19 | async-start | bytes 983040 | tf_op jit(solution)/shard_map/reduce_scatter | solution.py:69
  610.6 194.3 %reduce-scatter.27.cloned.1.call-start = ((), (), s32[]{:S(2)}) async-start(), calls=%async_computation.20 | async-start | bytes 7077888 | tf_op jit(solution)/shard_map/reduce_scatter | solution.py:415
  685.6 145.7 %reduce-scatter.17.cloned.1.call-start = ((), (), s32[]{:S(2)}) async-start(), calls=%async_computation.15 | async-start | bytes 983040 | tf_op jit(solution)/shard_map/reduce_scatter | solution.py:58
  693.9 236.8 %reduce-scatter.29.cloned.1.call-start = ((), (), s32[]{:S(2)}) async-start(), calls=%async_computation.21 | async-start | bytes 983040 | tf_op jit(solution)/shard_map/reduce_scatter | solution.py:69
  701.1 7.0 collective-permute-start.3
  705.6 100.8 %copy-start.78 = (bf16[1,768,3,192]{1,3,2,0:T(8,128)(2,1)S(1)}, bf16[1,768,3,192]{1,3,2,0:T(8,128)(2,1)}, u32[]{:S(2)}) copy-start(bf16[1,768,3,192]{1,3,2,0:T(8,128)(2,1)} %get-tuple-element.86) | copy-start | bytes 2654212
  705.6 100.8 %copy-start.170 = (bf16[512,3,64]{0,2,1:T(8,128)(2,1)S(1)}, bf16[512,3,64]{0,2,1:T(8,128)(2,1)}, u32[]{:S(2)}) copy-start(bf16[512,3,64]{0,2,1:T(8,128)(2,1)} %get-tuple-element.112) | copy-start | bytes 589828
  813.5 488.9 %all-reduce.25.cloned.1.call-start = ((), (), s32[]{:S(2)}) async-start(), calls=%async_computation.22 | async-start | bytes 28311552 | tf_op jit(solution)/shard_map/psum | solution.py:466
  828.7 50.1 %copy-start.141 = (f32[192]{0:T(256)S(1)}, f32[192]{0:T(256)}, u32[]{:S(2)}) copy-start(f32[192]{0:T(256)} %get-tuple-element.71) | copy-start | bytes 2308
  828.7 50.1 %copy-start.133 = (bf16[768]{0:T(1024)(128)(2,1)S(1)}, bf16[768]{0:T(1024)(128)(2,1)}, u32[]{:S(2)}) copy-start(bf16[768]{0:T(1024)(128)(2,1)} %get-tuple-element.19) | copy-start | bytes 4612
  828.8 50.1 %copy-start.134 = (bf16[768]{0:T(1024)(128)(2,1)S(1)}, bf16[768]{0:T(1024)(128)(2,1)}, u32[]{:S(2)}) copy-start(bf16[768]{0:T(1024)(128)(2,1)} %get-tuple-element.17) | copy-start | bytes 4612
  828.8 50.1 %copy-start.135 = (bf16[768]{0:T(1024)(128)(2,1)S(1)}, bf16[768]{0:T(1024)(128)(2,1)}, u32[]{:S(2)}) copy-start(bf16[768]{0:T(1024)(128)(2,1)} %get-tuple-element.15) | copy-start | bytes 4612
  828.8 50.1 %copy-start.136 = (bf16[768]{0:T(1024)(128)(2,1)S(1)}, bf16[768]{0:T(1024)(128)(2,1)}, u32[]{:S(2)}) copy-start(bf16[768]{0:T(1024)(128)(2,1)} %get-tuple-element.13) | copy-start | bytes 4612
  828.8 50.1 %copy-start.158 = (bf16[768]{0:T(1024)(128)(2,1)S(1)}, bf16[768]{0:T(1024)(128)(2,1)}, u32[]{:S(2)}) copy-start(bf16[768]{0:T(1024)(128)(2,1)} %get-tuple-element.117) | copy-start | bytes 4612
  828.8 50.1 %copy-start.159 = (bf16[768]{0:T(1024)(128)(2,1)S(1)}, bf16[768]{0:T(1024)(128)(2,1)}, u32[]{:S(2)}) copy-start(bf16[768]{0:T(1024)(128)(2,1)} %get-tuple-element.119) | copy-start | bytes 4612
  828.8 50.1 %copy-start.160 = (bf16[768]{0:T(1024)(128)(2,1)S(1)}, bf16[768]{0:T(1024)(128)(2,1)}, u32[]{:S(2)}) copy-start(bf16[768]{0:T(1024)(128)(2,1)} %get-tuple-element.121) | copy-start | bytes 4612
  828.8 50.1 %copy-start.161 = (bf16[768]{0:T(1024)(128)(2,1)S(1)}, bf16[768]{0:T(1024)(128)(2,1)}, u32[]{:S(2)}) copy-start(bf16[768]{0:T(1024)(128)(2,1)} %get-tuple-element.123) | copy-start | bytes 4612
  828.8 101.8 %copy-start.33 = (bf16[512,192]{0,1:T(8,128)(2,1)S(1)}, bf16[512,192]{0,1:T(8,128)(2,1)}, u32[]{:S(2)}) copy-start(bf16[512,192]{0,1:T(8,128)(2,1)} %param.16) | copy-start | bytes 589828
  828.8 101.8 %copy-start.48 = (bf16[512,192]{0,1:T(8,128)(2,1)S(1)}, bf16[512,192]{0,1:T(8,128)(2,1)}, u32[]{:S(2)}) copy-start(bf16[512,192]{0,1:T(8,128)(2,1)} %reduce-scatter.19.cloned.1.call-done) | copy-start | bytes 589828
  828.8 101.8 %copy-start.73 = (bf16[512,192]{0,1:T(8,128)(2,1)S(1)}, bf16[512,192]{0,1:T(8,128)(2,1)}, u32[]{:S(2)}) copy-start(bf16[512,192]{0,1:T(8,128)(2,1)} %reduce-scatter.23.cloned.1.call-done) | copy-start | bytes 589828
  828.9 101.8 %copy-start.85 = (bf16[512,192]{0,1:T(8,128)(2,1)S(1)}, bf16[512,192]{0,1:T(8,128)(2,1)}, u32[]{:S(2)}) copy-start(bf16[512,192]{0,1:T(8,128)(2,1)} %reduce-scatter.25.cloned.1.call-done) | copy-start | bytes 589828
  (167 other events, 923.1 us)
Sparse Core Ops, SparseCore 0:
  39.0 64.4 all-gather.10
  130.5 21.4 reduce-scatter.10
  166.9 23.6 reduce-scatter.12
  216.2 63.4 all-gather.12
  307.2 21.4 reduce-scatter.14
  353.5 23.6 reduce-scatter.18
  432.8 119.2 reduce-scatter.20
  564.0 22.4 reduce-scatter.22
  610.7 23.6 reduce-scatter.24
  685.7 119.1 reduce-scatter.26
  807.5 22.3 reduce-scatter.16
  832.5 23.4 reduce-scatter.28
  861.8 440.6 all-reduce.24
where the time goes:
time: 1330 us; the launch traced here: 1320 us
  waiting for transfers between devices  772 us (58%)
  blocking collectives  171 us (13%)
  local copies, waits for them, and re-layouts  155 us (12%)
  other arithmetic  96.9 us (7%)
  matrix products  95.3 us (7%)
  between operations  18.2 us (1%)
    psum x1, waiting for transfers between devices, on_device(): lax.psum((stacked[0], stacked[1], stacked[2], stacked[3], stacked[4], sta...  370 us
    reduce_scatter x2, waiting for transfers between devices, on_device(): lax.psum_scatter(term.reshape(row_count * lax.axis_size('tok'), head_coun...  196 us
    all_gather x2, waiting for transfers between devices, on_device(): shard_piece = lax.all_gather(own_blocks, 'tok', axis=0, tiled=True)  88.6 us
    reduce_scatter x4, waiting for transfers between devices, scatter_norm_grad(): lax.psum_scatter(grad_rounded.astype(jnp.bfloat16), 'head', scatter_dimen...  63 us
    reduce_scatter x4, waiting for transfers between devices, head_sum(): lax.psum_scatter(partial_sum.astype(jnp.bfloat16), 'head', scatter_dimens...  44.9 us
    psum x1, blocking collectives, on_device(): square_sums = lax.psum(jnp.stack(local_squares), ('head', 'tok'))  39.9 us
    psum x1, blocking collectives, on_device(): lax.psum((stacked[0], stacked[1], stacked[2], stacked[3], stacked[4], sta...  39.8 us
    unnamed x393, local copies, waits for them, and re-layouts  35.9 us
  transfers between devices with their start and end apart: 17, of which 13 were waited for; matrix products, arithmetic and copies ran while one was open for 8% of the time, Pallas kernels for 0%

commit v1 on v0

v1 whole, which is shorter than its diff:
```python
import functools

import jax
import jax.numpy as jnp
from jax import lax
from jax.experimental import pallas as pl
from jax.experimental.pallas import tpu as pltpu
from jax.sharding import PartitionSpec as P

D = 768
HD = 64
LAYERS = 2
WINDOW = 64
KB = 16
SEL = 4
QB = 64
WIDE = 2 * HD

epsilon = 1e-05
negative = -1e30
scale = HD ** (-0.5)
bf16 = jnp.bfloat16
f32 = jnp.float32

STEPS = (0, 2, 1, 3)
GAIN, SHIFT, B_OUT, B_DOWN, PARAM_ROWS = 0, 4, 8, 10, 16


def params(megabytes):
    return pltpu.CompilerParams(vmem_limit_bytes=megabytes * 2**20)


def cost(flops, moved, special=0):
    return pl.CostEstimate(flops=int(flops), bytes_accessed=int(moved), transcendentals=int(special))


def swap(value, axis, step):
    return lax.ppermute(value, axis, [(i, i ^ step) for i in range(lax.axis_size(axis))])


def shift_by(value, axis, step):
    count = lax.axis_size(axis)
    return lax.ppermute(
        value, axis, [(i, i + step) for i in range(count) if 0 <= i + step < count]
    )


def share_quarters(own):
    across = swap(own, "head", 2)
    beside = swap(own, "head", 1)
    both = swap(across, "head", 1)
    return own, across, beside, both


def sum_quarters(pieces):
    own, across, beside, both = pieces
    first = swap(both, "head", 1)
    onward = (across.astype(f32) + first.astype(f32)).astype(bf16)
    second = swap(beside, "head", 1)
    third = swap(onward, "head", 2)
    return own, second, third


def small_sum(value, axes):
    for axis in axes:
        step = 1
        while step < lax.axis_size(axis):
            value = value + swap(value, axis, step)
            step *= 2
    return value


def block_sum(value):
    count = lax.axis_size("tok")
    position = lax.axis_index("tok")
    columns = value.shape[1]
    steps = []
    step = 1
    while step < count:
        steps.append(step)
        step *= 2
    for step in steps:
        bit = (position // step) % 2
        half = value.shape[0] // 2
        pair = value.reshape(2, half, columns)
        give = lax.dynamic_index_in_dim(pair, 1 - bit, 0, keepdims=False)
        keep = lax.dynamic_index_in_dim(pair, bit, 0, keepdims=False)
        value = (keep.astype(f32) + swap(give, "tok", step).astype(f32)).astype(bf16)
    for step in reversed(steps):
        bit = (position // step) % 2
        other = swap(value, "tok", step)
        value = jnp.concatenate(
            [jnp.where(bit == 0, value, other), jnp.where(bit == 0, other, value)], axis=0
        )
    return value.astype(f32)


def ring_form(count):
    return count == 8


def gather_blocks(own):
    count = lax.axis_size("tok")
    if not ring_form(count):
        return [lax.all_gather(own, "tok")]
    current = own
    parts = []
    for hop in range(count // 2):
        other = swap(current, "tok", 1)
        if hop < count // 2 - 1:
            after = shift_by(current, "tok", 2)
            current, other, after = lax.optimization_barrier((current, other, after))
        parts += [current, other]
        current = after
    return parts


def return_blocks(parts):
    count = lax.axis_size("tok")
    if not ring_form(count):
        return [lax.psum_scatter(parts[0], "tok", scatter_dimension=0, tiled=False)]
    running = None
    for d in range(count // 2 - 1, 0, -1):
        got = swap(parts[2 * d + 1], "tok", 1)
        total = parts[2 * d].astype(f32) + got.astype(f32)
        if running is not None:
            total = total + running.astype(f32)
        running = shift_by(total.astype(bf16), "tok", -2)
    return [parts[0], swap(parts[1], "tok", 1), running]


def slot_of(block, tok, count):
    if not ring_form(count):
        return block
    away = (tok >> 1) - (block >> 1)
    return 2 * jnp.maximum(away, 0) + ((tok ^ block) & 1)


def normalise(rows):
    average = jnp.mean(rows, axis=-1, keepdims=True)
    centred = rows - average
    spread = jnp.mean(centred * centred, axis=-1, keepdims=True)
    inverse = lax.rsqrt(spread + epsilon)
    return centred * inverse, inverse


def row(ref, index):
    return ref[index : index + 1, :].astype(f32)


def piece_rows(place, step, size):
    return pl.ds(pl.multiple_of((place[0] ^ step) * size, size), size)


def project_kernel(place, *refs, heads, first):
    if first:
        rows_ref, param_ref, w_ref, bias_ref, normed_ref, q_ref, kv_ref = refs
    else:
        own, across, beside, both, w_ref, bias_ref, normed_ref, q_ref, kv_ref = refs
    size = normed_ref.shape[0] // 4
    for k in range(4):
        if first:
            rows = pl.ds(k * size, size)
            unit, _ = normalise(rows_ref[rows, :].astype(f32))
            normed = (unit * row(param_ref, GAIN) + row(param_ref, SHIFT)).astype(bf16)
        else:
            rows = piece_rows(place, STEPS[k], size)
            normed = (own, across, beside, both)[k][...]
        normed_ref[rows, :] = normed
        projected = jnp.dot(normed, w_ref[...], preferred_element_type=f32) + bias_ref[...]
        for h in range(heads):
            q_ref[h, rows, :] = (projected[:, h * WIDE : (h + 1) * WIDE] * scale).astype(bf16)
            at = (heads + h) * WIDE
            kv_ref[h, rows, :] = projected[:, at : at + WIDE].astype(bf16)


def whole(shape):
    return pl.BlockSpec(shape, lambda *_: (0,) * len(shape))


def param_spec(rows):
    return pl.BlockSpec((PARAM_ROWS, D), lambda *_: (rows // PARAM_ROWS, 0))


def project(place, source, gathered, w_all, bias_all, rows, heads):
    first = source is None
    quarter = rows // 4
    columns = w_all.shape[1]
    if first:
        arrays = (gathered, gathered)
        specs = [whole((rows, D)), param_spec(rows)]
    else:
        arrays = tuple(source)
        specs = [whole((quarter, D))] * 4
    return pl.pallas_call(
        functools.partial(project_kernel, heads=heads, first=first),
        grid_spec=pltpu.PrefetchScalarGridSpec(
            num_scalar_prefetch=1,
            grid=(1,),
            in_specs=specs + [whole(w_all.shape), whole(bias_all.shape)],
            out_specs=[whole((rows, D)), whole((heads, rows, WIDE)), whole((heads, rows, WIDE))],
        ),
        out_shape=[
            jax.ShapeDtypeStruct((rows, D), bf16),
            jax.ShapeDtypeStruct((heads, rows, WIDE), bf16),
            jax.ShapeDtypeStruct((heads, rows, WIDE), bf16),
        ],
        compiler_params=params(32),
        cost_estimate=cost(2 * rows * D * columns, 2 * D * columns + 8 * rows * D),
        name="project",
    )(place, *arrays, w_all, bias_all)


def copies(parts, scratch, sems, head, buffer, rows):
    if len(parts) == 1:
        count = parts[0].shape[0]
        return [
            pltpu.make_async_copy(
                parts[0].at[slot, head],
                scratch.at[buffer, pl.ds(slot * rows, rows), :],
                sems.at[buffer, slot],
            )
            for slot in range(count)
        ]
    return [
        pltpu.make_async_copy(
            part.at[head], scratch.at[buffer, pl.ds(slot * rows, rows), :], sems.at[buffer, slot]
        )
        for slot, part in enumerate(parts)
    ]


def bring_blocks(parts, scratch, sems, heads, rows):
    head = pl.program_id(0)
    buffer = lax.rem(head, 2)

    @pl.when(head == 0)
    def _():
        for copy in copies(parts, scratch, sems, 0, 0, rows):
            copy.start()

    @pl.when(head + 1 < heads)
    def _():
        for copy in copies(parts, scratch, sems, head + 1, 1 - buffer, rows):
            copy.start()

    for copy in copies(parts, scratch, sems, head, buffer, rows):
        copy.wait()
    return head, buffer


class Listed:
    def __init__(self, place, chosen, keys, near_valid, far_valid, rows, count):
        self.place, self.chosen, self.keys = place, chosen, keys
        self.near_valid, self.far_valid = near_valid, far_valid
        self.rows, self.count = rows, count
        self.tok = place[1]
        self.boundary = place[2]
        self.own = slot_of(self.tok, self.tok, count) * rows
        self.before = slot_of(jnp.maximum(self.tok - 1, 0), self.tok, count) * rows
        line = lax.broadcasted_iota(jnp.int32, (QB, 2 * WINDOW), 1)
        column = lax.broadcasted_iota(jnp.int32, (QB, 2 * WINDOW), 0)
        self.band = (line > column) & (line <= column + WINDOW)
        self.diagonal = line == column + WINDOW

    def near_starts(self, b):
        if b == 0:
            return [
                (pl.multiple_of(self.before + self.rows - WINDOW, WINDOW), WINDOW),
                (pl.multiple_of(self.own, WINDOW), WINDOW),
            ]
        return [(pl.multiple_of(self.own + (b - 1) * QB, WINDOW), 2 * WINDOW)]

    def far_start(self, head, b, s):
        block = self.chosen[head, b * SEL + s]
        per_device = self.rows // KB
        device = lax.div(block, per_device)
        at = slot_of(device, self.tok, self.count) * self.rows + lax.rem(block, per_device) * KB
        return pl.multiple_of(at, KB)

    def load(self, buffer, starts):
        loaded = [self.keys[buffer, pl.ds(start, size), :] for start, size in starts]
        return loaded[0] if len(loaded) == 1 else jnp.concatenate(loaded, axis=0)

    def masks(self, head, b):
        first = self.tok * self.rows + b * QB
        in_second = lambda position: jnp.where(position >= self.boundary, 1, 0)
        query = first + lax.broadcasted_iota(jnp.int32, (QB, 1), 0)
        query_seq = in_second(query)
        key = first - WINDOW + lax.broadcasted_iota(jnp.int32, (1, 2 * WINDOW), 1)
        valid = self.near_valid[b : b + 1, :] > 0.0
        near = self.band & (self.diagonal | valid) & (in_second(key) == query_seq)
        lane = lax.broadcasted_iota(jnp.int32, (1, SEL * KB), 1)
        usable = jnp.zeros((1, SEL * KB), f32)
        token = lane & (KB - 1)
        for s in range(SEL):
            block = self.chosen[head, b * SEL + s]
            here = (lane >= s * KB) & (lane < (s + 1) * KB)
            early = block * KB + KB <= first - WINDOW
            here_usable = here & early
            usable = jnp.where(here_usable, self.far_valid[pl.ds(block, 1), :], usable)
            token = token + jnp.where(here, block * KB, 0)
        far = (usable > 0.0) & (in_second(token) == query_seq)
        return near, far


def softmax(queries, near_kv, far_kv, near_ok, far_ok):
    transposed = (((1,), (1,)), ((), ()))
    near = lax.dot_general(queries, near_kv, transposed, preferred_element_type=f32)
    far = lax.dot_general(queries, far_kv, transposed, preferred_element_type=f32)
    near = jnp.where(near_ok, near, negative)
    far = jnp.where(far_ok, far, negative)
    top = jnp.maximum(
        jnp.max(near, axis=-1, keepdims=True), jnp.max(far, axis=-1, keepdims=True)
    )
    near = jnp.exp(near - top)
    far = jnp.exp(far - top)
    total = jnp.sum(near, axis=-1, keepdims=True) + jnp.sum(far, axis=-1, keepdims=True)
    part = 1.0 / total
    return near * part, far * part


def attend_kernel(place, chosen, *refs, heads, count, blocks, parts):
    q_ref, w_ref, near_valid, far_valid = refs[:4]
    kv_parts = refs[4 : 4 + parts]
    mixed_ref = refs[4 + parts]
    outs = refs[5 + parts : 9 + parts]
    keys, gathered, sems = refs[9 + parts :]
    rows = blocks * QB
    head, buffer = bring_blocks(kv_parts, keys, sems, heads, rows)
    listed = Listed(place, chosen, keys, near_valid, far_valid, rows, count)
    for b in range(blocks):
        at = pl.ds(b * QB, QB)
        near_kv = listed.load(buffer, listed.near_starts(b))
        far_kv = listed.load(buffer, [(listed.far_start(head, b, s), KB) for s in range(SEL)])
        near_ok, far_ok = listed.masks(head, b)
        near, far = softmax(q_ref[0, at, :], near_kv, far_kv, near_ok, far_ok)
        out = jnp.dot(near.astype(bf16), near_kv, preferred_element_type=f32)
        out = out + jnp.dot(far.astype(bf16), far_kv, preferred_element_type=f32)
        out = out.astype(bf16)
        mixed_ref[0, at, :] = out
        gathered[head, at, :] = out

    @pl.when(head == heads - 1)
    def _():
        size = rows // 4
        for k in range(4):
            at = piece_rows(place, STEPS[k], size)
            mixed = jnp.concatenate([gathered[h, at, :] for h in range(heads)], axis=1)
            outs[k][...] = jnp.dot(mixed, w_ref[...], preferred_element_type=f32).astype(bf16)


def attend(place, chosen, queries, w_out, near_valid, far_valid, parts, count):
    heads, rows, _ = queries.shape
    blocks = rows // QB
    quarter = rows // 4
    per_head = pl.BlockSpec((1, rows, WIDE), lambda h, *_: (h, 0, 0))
    slots = count if len(parts) == 1 else len(parts)
    return pl.pallas_call(
        functools.partial(
            attend_kernel, heads=heads, count=count, blocks=blocks, parts=len(parts)
        ),
        grid_spec=pltpu.PrefetchScalarGridSpec(
            num_scalar_prefetch=2,
            grid=(heads,),
            in_specs=[
                per_head,
                whole(w_out.shape),
                whole(near_valid.shape),
                whole(far_valid.shape),
            ]
            + [pl.BlockSpec(memory_space=pl.ANY)] * len(parts),
            out_specs=[per_head] + [whole((quarter, D))] * 4,
            scratch_shapes=[
                pltpu.VMEM((2, slots * rows, WIDE), bf16),
                pltpu.VMEM((heads, rows, WIDE), bf16),
                pltpu.SemaphoreType.DMA((2, slots)),
            ],
        ),
        out_shape=[jax.ShapeDtypeStruct((heads, rows, WIDE), bf16)]
        + [jax.ShapeDtypeStruct((quarter, D), bf16)] * 4,
        compiler_params=params(44),
        cost_estimate=cost(
            2 * rows * heads * WIDE * (D + 512), 2 * heads * WIDE * rows * (slots + 4)
        ),
        name="attend",
    )(place, chosen, queries, w_out, near_valid, far_valid, *parts)


def attend_back_kernel(place, chosen, *refs, heads, count, blocks, parts):
    q_ref, w_ref, near_valid, far_valid = refs[:4]
    pieces = refs[4:8]
    kv_parts = refs[8 : 8 + parts]
    dq_ref, grad_ref = refs[8 + parts : 10 + parts]
    outs = refs[10 + parts : 10 + 2 * parts]
    keys, sums, sems = refs[10 + 2 * parts :]
    rows = blocks * QB
    size = rows // 4
    head, buffer = bring_blocks(kv_parts, keys, sems, heads, rows)
    listed = Listed(place, chosen, keys, near_valid, far_valid, rows, count)

    @pl.when(head == 0)
    def _():
        for k in range(4):
            grad_ref[piece_rows(place, STEPS[k], size), :] = pieces[k][...]

    sums[...] = jnp.zeros_like(sums)
    transposed = (((1,), (1,)), ((), ()))
    over_queries = (((0,), (0,)), ((), ()))
    for b in range(blocks):
        at = pl.ds(b * QB, QB)
        near_at = listed.near_starts(b)
        far_at = [(listed.far_start(head, b, s), KB) for s in range(SEL)]
        near_kv = listed.load(buffer, near_at)
        far_kv = listed.load(buffer, far_at)
        near_ok, far_ok = listed.masks(head, b)
        queries = q_ref[0, at, :]
        near, far = softmax(queries, near_kv, far_kv, near_ok, far_ok)
        mixed = lax.dot_general(
            grad_ref[at, :], w_ref[...], transposed, preferred_element_type=f32
        ).astype(bf16)
        near_grad = lax.dot_general(mixed, near_kv, transposed, preferred_element_type=f32)
        far_grad = lax.dot_general(mixed, far_kv, transposed, preferred_element_type=f32)
        inner = jnp.sum(near * near_grad, axis=-1, keepdims=True)
        inner = inner + jnp.sum(far * far_grad, axis=-1, keepdims=True)
        near_scores = (near * (near_grad - inner)).astype(bf16)
        far_scores = (far * (far_grad - inner)).astype(bf16)
        grad_q = jnp.dot(near_scores, near_kv, preferred_element_type=f32)
        grad_q = grad_q + jnp.dot(far_scores, far_kv, preferred_element_type=f32)
        dq_ref[0, at, :] = (grad_q.astype(bf16).astype(f32) * scale).astype(bf16)
        near_sum = lax.dot_general(
            near_scores, queries, over_queries, preferred_element_type=f32
        ) + lax.dot_general(near.astype(bf16), mixed, over_queries, preferred_element_type=f32)
        far_sum = lax.dot_general(
            far_scores, queries, over_queries, preferred_element_type=f32
        ) + lax.dot_general(far.astype(bf16), mixed, over_queries, preferred_element_type=f32)
        done = 0
        for start, length in near_at:
            sums[pl.ds(start, length), :] += near_sum[done : done + length]
            done += length
        for s, (start, length) in enumerate(far_at):
            sums[pl.ds(start, length), :] += far_sum[s * KB : (s + 1) * KB]
    if parts == 1:
        for slot in range(count):
            outs[0][slot, 0] = sums[pl.ds(slot * rows, rows), :].astype(bf16)
    else:
        for slot in range(parts):
            outs[slot][0] = sums[pl.ds(slot * rows, rows), :].astype(bf16)


def attend_back(place, chosen, queries, w_out, near_valid, far_valid, pieces, parts, count):
    heads, rows, _ = queries.shape
    blocks = rows // QB
    quarter = rows // 4
    per_head = pl.BlockSpec((1, rows, WIDE), lambda h, *_: (h, 0, 0))
    slots = count if len(parts) == 1 else len(parts)
    if len(parts) == 1:
        out_specs = [pl.BlockSpec((count, 1, rows, WIDE), lambda h, *_: (0, h, 0, 0))]
    else:
        out_specs = [per_head] * len(parts)
    return pl.pallas_call(
        functools.partial(
            attend_back_kernel, heads=heads, count=count, blocks=blocks, parts=len(parts)
        ),
        grid_spec=pltpu.PrefetchScalarGridSpec(
            num_scalar_prefetch=2,
            grid=(heads,),
            in_specs=[
                per_head,
                pl.BlockSpec((WIDE, D), lambda h, *_: (h, 0)),
                whole(near_valid.shape),
                whole(far_valid.shape),
            ]
            + [whole((quarter, D))] * 4
            + [pl.BlockSpec(memory_space=pl.ANY)] * len(parts),
            out_specs=[per_head, whole((rows, D))] + out_specs,
            scratch_shapes=[
                pltpu.VMEM((2, slots * rows, WIDE), bf16),
                pltpu.VMEM((slots * rows, WIDE), f32),
                pltpu.SemaphoreType.DMA((2, slots)),
            ],
        ),
        out_shape=[
            jax.ShapeDtypeStruct((heads, rows, WIDE), bf16),
            jax.ShapeDtypeStruct((rows, D), bf16),
        ]
        + [jax.ShapeDtypeStruct(part.shape, bf16) for part in parts],
        compiler_params=params(62 if len(parts) == 1 else 44),
        cost_estimate=cost(
            2 * rows * heads * WIDE * (D + 1536), 4 * heads * WIDE * rows * (slots + 4)
        ),
        name="attend_back",
    )(place, chosen, queries, w_out, near_valid, far_valid, *pieces, *parts)


def project_back_kernel(place, *refs, heads, terms):
    dq_ref, w_ref = refs[:2]
    kv_refs = refs[2 : 2 + terms]
    dkv_ref, bias_ref = refs[2 + terms : 4 + terms]
    outs = refs[4 + terms :]
    rows = dq_ref.shape[1]
    size = rows // 4
    for h in range(heads):
        total = kv_refs[0][h].astype(f32)
        for term in kv_refs[1:]:
            total = total + term[h].astype(f32)
        low = total.astype(bf16)
        dkv_ref[h] = low
        bias_ref[h : h + 1, :] = jnp.sum(dq_ref[h].astype(f32), axis=0, keepdims=True)
        bias_ref[heads + h : heads + h + 1, :] = jnp.sum(low.astype(f32), axis=0, keepdims=True)
    for k in range(4):
        at = piece_rows(place, STEPS[k], size)
        grads = jnp.concatenate(
            [dq_ref[h, at, :] for h in range(heads)] + [dkv_ref[h, at, :] for h in range(heads)],
            axis=1,
        )
        outs[k][...] = lax.dot_general(
            grads, w_ref[...], (((1,), (1,)), ((), ())), preferred_element_type=f32
        ).astype(bf16)


def project_back(place, dq, w_all, kv_terms):
    heads, rows, _ = dq.shape
    quarter = rows // 4
    return pl.pallas_call(
        functools.partial(project_back_kernel, heads=heads, terms=len(kv_terms)),
        grid_spec=pltpu.PrefetchScalarGridSpec(
            num_scalar_prefetch=1,
            grid=(1,),
            in_specs=[whole(dq.shape), whole(w_all.shape)] + [whole(dq.shape)] * len(kv_terms),
            out_specs=[whole(dq.shape), whole((2 * heads, WIDE))] + [whole((quarter, D))] * 4,
        ),
        out_shape=[
            jax.ShapeDtypeStruct(dq.shape, bf16),
            jax.ShapeDtypeStruct((2 * heads, WIDE), f32),
        ]
        + [jax.ShapeDtypeStruct((quarter, D), bf16)] * 4,
        compiler_params=params(32),
        cost_estimate=cost(4 * rows * D * heads * WIDE, 4 * D * heads * WIDE + 12 * rows * D),
        name="project_back",
    )(place, dq, w_all, *kv_terms)


def feed_kernel(place, *refs):
    pieces = refs[:4]
    up_ref, bias_ref, down_ref, normed_ref, hidden_ref, slope_ref = refs[4:10]
    outs = refs[10:]
    size = pieces[0].shape[0]
    root = 0.7978845608028654
    cubic = 0.044715
    for k in range(4):
        at = pl.ds(k * size, size)
        normed = pieces[k][...]
        normed_ref[at, :] = normed
        inner = jnp.dot(normed, up_ref[...], preferred_element_type=f32) + bias_ref[...]
        square = inner * inner
        bend = jnp.tanh(root * inner * (1.0 + cubic * square))
        half = 0.5 * (1.0 + bend)
        hidden = (inner * half).astype(bf16)
        hidden_ref[at, :] = hidden
        slope = half + 0.5 * inner * (1.0 - bend * bend) * (root * (1.0 + 3.0 * cubic * square))
        slope_ref[at, :] = slope.astype(bf16)
        outs[k][...] = jnp.dot(hidden, down_ref[...], preferred_element_type=f32).astype(bf16)


def feed(place, pieces, w_up, b_up, w_down):
    quarter = pieces[0].shape[0]
    rows = 4 * quarter
    units = w_up.shape[1]
    return pl.pallas_call(
        feed_kernel,
        grid_spec=pltpu.PrefetchScalarGridSpec(
            num_scalar_prefetch=1,
            grid=(1,),
            in_specs=[whole((quarter, D))] * 4
            + [whole(w_up.shape), whole(b_up.shape), whole(w_down.shape)],
            out_specs=[whole((rows, D)), whole((rows, units)), whole((rows, units))]
            + [whole((quarter, D))] * 4,
        ),
        out_shape=[
            jax.ShapeDtypeStruct((rows, D), bf16),
            jax.ShapeDtypeStruct((rows, units), bf16),
            jax.ShapeDtypeStruct((rows, units), bf16),
        ]
        + [jax.ShapeDtypeStruct((quarter, D), bf16)] * 4,
        compiler_params=params(32),
        cost_estimate=cost(4 * rows * D * units, 4 * D * units + 10 * rows * D, rows * units),
        name="feed",
    )(place, *pieces, w_up, b_up, w_down)


def feed_back_kernel(place, *refs):
    pieces = refs[:4]
    down_ref, up_ref, slope_ref, grad_ref, inner_ref, bias_ref = refs[4:10]
    outs = refs[10:]
    size = pieces[0].shape[0]
    transposed = (((1,), (1,)), ((), ()))
    total = None
    for k in range(4):
        at = pl.ds(k * size, size)
        grad = pieces[k][...]
        grad_ref[at, :] = grad
        hidden = lax.dot_general(grad, down_ref[...], transposed, preferred_element_type=f32)
        inner = (hidden * slope_ref[at, :].astype(f32)).astype(bf16)
        inner_ref[at, :] = inner
        part = jnp.sum(inner.astype(f32), axis=0, keepdims=True)
        total = part if total is None else total + part
        outs[k][...] = lax.dot_general(
            inner, up_ref[...], transposed, preferred_element_type=f32
        ).astype(bf16)
    bias_ref[...] = total


def feed_back(place, pieces, w_up, w_down, slope):
    rows, units = slope.shape
    quarter = rows // 4
    if len(pieces) == 1:
        arrays = tuple(pieces) * 4
        specs = [
            pl.BlockSpec((quarter, D), lambda i, place, step=step: (place[0] ^ step, 0))
            for step in STEPS
        ]
    else:
        arrays = tuple(pieces)
        specs = [whole((quarter, D))] * 4
    return pl.pallas_call(
        feed_back_kernel,
        grid_spec=pltpu.PrefetchScalarGridSpec(
            num_scalar_prefetch=1,
            grid=(1,),
            in_specs=specs + [whole(w_down.shape), whole(w_up.shape), whole(slope.shape)],
            out_specs=[whole((rows, D)), whole((rows, units)), whole((1, units))]
            + [whole((quarter, D))] * 4,
        ),
        out_shape=[
            jax.ShapeDtypeStruct((rows, D), bf16),
            jax.ShapeDtypeStruct((rows, units), bf16),
            jax.ShapeDtypeStruct((1, units), f32),
        ]
        + [jax.ShapeDtypeStruct((quarter, D), bf16)] * 4,
        compiler_params=params(32),
        cost_estimate=cost(4 * rows * D * units, 4 * D * units + 10 * rows * D),
        name="feed_back",
    )(place, *arrays, w_down, w_up, slope)


def add_norm_kernel(place, *refs, bias_row, norm_row):
    a, b, c, residual, param, valid = refs[:6]
    out_ref, low_ref, normed_ref, squares_ref = refs[6:]
    branch = a[...].astype(f32) + b[...].astype(f32) + c[...].astype(f32) + row(param, bias_row)
    total = residual[...].astype(f32) + branch
    out_ref[...] = total
    low = total.astype(bf16)
    low_ref[...] = low
    if norm_row is not None:
        unit, _ = normalise(low.astype(f32))
        gain, shift = row(param, GAIN + norm_row), row(param, SHIFT + norm_row)
        normed_ref[...] = (unit * gain + shift).astype(bf16)
    else:
        normed_ref[...] = low
    weight = valid[...]
    squares_ref[0:1, :] = jnp.sum(weight * branch * branch, axis=0, keepdims=True)
    squares_ref[1:2, :] = jnp.sum(weight * total * total, axis=0, keepdims=True)


def own_quarter(quarter):
    return pl.BlockSpec((quarter, D), lambda i, place: (place[0], 0))


def add_norm(place, terms, residual, gathered, valid, rows, bias_row, norm_row):
    quarter = rows // 4
    spec = whole((quarter, D))
    return pl.pallas_call(
        functools.partial(add_norm_kernel, bias_row=bias_row, norm_row=norm_row),
        grid_spec=pltpu.PrefetchScalarGridSpec(
            num_scalar_prefetch=1,
            grid=(1,),
            in_specs=[spec] * 3
            + [
                own_quarter(quarter) if residual is gathered else spec,
                param_spec(rows),
                whole(valid.shape),
            ],
            out_specs=[spec, spec, spec, whole((2, D))],
        ),
        out_shape=[
            jax.ShapeDtypeStruct((quarter, D), f32),
            jax.ShapeDtypeStruct((quarter, D), bf16),
            jax.ShapeDtypeStruct((quarter, D), bf16),
            jax.ShapeDtypeStruct((2, D), f32),
        ],
        compiler_params=params(16),
        cost_estimate=cost(20 * quarter * D, 18 * quarter * D),
        name="add_norm",
    )(place, *terms, residual, gathered, valid)


def norm_back_kernel(place, *refs, norm_row):
    a, b, c, source, gradient, param = refs[:6]
    out_ref, low_ref, sums_ref = refs[6:]
    grad_normed = a[...].astype(f32) + b[...].astype(f32) + c[...].astype(f32)
    unit, inverse = normalise(source[...].astype(f32))
    grad_unit = grad_normed * row(param, GAIN + norm_row)
    first = jnp.mean(grad_unit, axis=-1, keepdims=True)
    second = jnp.mean(grad_unit * unit, axis=-1, keepdims=True)
    total = gradient[...].astype(f32) + inverse * (grad_unit - first - unit * second)
    out_ref[...] = total
    low = total.astype(bf16)
    low_ref[...] = low
    sums_ref[0:1, :] = jnp.sum(grad_normed * unit, axis=0, keepdims=True)
    sums_ref[1:2, :] = jnp.sum(grad_normed, axis=0, keepdims=True)
    sums_ref[2:3, :] = jnp.sum(low.astype(f32), axis=0, keepdims=True)


def norm_back(place, terms, source, gradient, gathered, rows, norm_row):
    quarter = rows // 4
    spec = whole((quarter, D))
    pick = lambda array: spec if array.shape[0] == quarter else own_quarter(quarter)
    return pl.pallas_call(
        functools.partial(norm_back_kernel, norm_row=norm_row),
        grid_spec=pltpu.PrefetchScalarGridSpec(
            num_scalar_prefetch=1,
            grid=(1,),
            in_specs=[spec] * 3 + [pick(source), pick(gradient), param_spec(rows)],
            out_specs=[spec, spec, whole((3, D))],
        ),
        out_shape=[
            jax.ShapeDtypeStruct((quarter, D), f32),
            jax.ShapeDtypeStruct((quarter, D), bf16),
            jax.ShapeDtypeStruct((3, D), f32),
        ],
        compiler_params=params(16),
        cost_estimate=cost(20 * quarter * D, 18 * quarter * D),
        name="norm_back",
    )(place, *terms, source, gradient, gathered)


def columns_kernel(place, *refs):
    pieces, out = refs[:4], refs[4]
    size = pieces[0].shape[0]
    width = out.shape[1]
    for p in range(4):

        @pl.when(place[0] == p)
        def _():
            for k in range(4):
                at = piece_rows(place, STEPS[k], size)
                out[at, :] = pieces[k][:, p * width : (p + 1) * width]


def columns(place, pieces):
    quarter = pieces[0].shape[0]
    return pl.pallas_call(
        columns_kernel,
        grid_spec=pltpu.PrefetchScalarGridSpec(
            num_scalar_prefetch=1,
            grid=(1,),
            in_specs=[whole((quarter, D))] * 4,
            out_specs=whole((4 * quarter, D // 4)),
        ),
        out_shape=jax.ShapeDtypeStruct((4 * quarter, D // 4), bf16),
        compiler_params=params(16),
        cost_estimate=cost(quarter * D, 16 * quarter * D),
        name="columns",
    )(place, *pieces)


def on_device(
    residual_in,
    cotangent,
    w_qkv,
    b_qv,
    w_out,
    b_out,
    w_up,
    b_up,
    w_down,
    b_down,
    ln_gain,
    ln_bias,
    selection,
    lengths,
    valid,
):
    rows = residual_in.shape[0]
    heads = selection.shape[0]
    blocks = rows // QB
    quarter = rows // 4
    count = lax.axis_size("tok")
    position = lax.axis_index("tok")
    member = lax.axis_index("head")
    width = D // 4
    place = jnp.stack(
        [member.astype(jnp.int32), position.astype(jnp.int32), lengths[0], jnp.int32(0)]
    )
    first_row = position * rows

    small = jnp.concatenate(
        [ln_gain.reshape(-1, width), ln_bias.reshape(-1, width), b_out, b_down], axis=0
    )
    small = jnp.pad(small, ((0, PARAM_ROWS - small.shape[0]), (0, 0)))
    gathered = lax.all_gather(
        jnp.concatenate([residual_in, small], axis=0), "head", axis=1, tiled=True
    )
    cotangent_full = lax.all_gather(cotangent, "head", axis=1, tiled=True)

    split = w_qkv.reshape(LAYERS, D, 3, heads, HD)
    w_all = jnp.concatenate(
        [
            jnp.pad(split[:, :, 0], ((0, 0), (0, 0), (0, 0), (0, WIDE - HD))),
            jnp.concatenate([split[:, :, 1], split[:, :, 2]], axis=-1),
        ],
        axis=2,
    ).reshape(LAYERS, D, 2 * heads * WIDE)
    b_split = b_qv.reshape(LAYERS, 2, heads, HD)
    b_all = (
        jnp.concatenate(
            [
                jnp.pad(b_split[:, 0], ((0, 0), (0, 0), (0, HD))),
                jnp.pad(b_split[:, 1], ((0, 0), (0, 0), (HD, 0))),
            ],
            axis=1,
        )
        .reshape(LAYERS, 1, 2 * heads * WIDE)
        .astype(f32)
    )
    w_mix = jnp.pad(
        w_out.reshape(LAYERS, heads, HD, D), ((0, 0), (0, 0), (HD, 0), (0, 0))
    ).reshape(LAYERS, heads * WIDE, D)
    b_inner = b_up.astype(f32)

    chosen = lax.dynamic_slice_in_dim(selection, position * blocks, blocks, 1).reshape(heads, -1)
    far_valid = jnp.tile(valid.reshape(-1, KB), (1, SEL)).astype(f32)
    padded = jnp.concatenate([jnp.zeros((WINDOW,), jnp.int32), valid])
    near = lax.dynamic_slice_in_dim(padded, first_row, rows + WINDOW).reshape(-1, WINDOW)
    near_valid = jnp.concatenate([near[:-1], near[1:]], axis=1).astype(f32)
    own_valid = lax.dynamic_slice_in_dim(valid, first_row + member * quarter, quarter)
    own_valid = own_valid.astype(f32)[:, None]

    residual = gathered
    normed_pieces = None
    lows = []
    kept = []
    squares = []
    for l in range(LAYERS):
        normed, queries, own_kv = project(
            place, normed_pieces, gathered, w_all[l], b_all[l], rows, heads
        )
        parts = gather_blocks(own_kv)
        mixed, *pieces = attend(
            place, chosen, queries, w_mix[l], near_valid, far_valid, parts, count
        )
        residual, low_second, normed_own, branch_squares = add_norm(
            place, sum_quarters(pieces), residual, gathered, own_valid, rows, B_OUT + l, 2 * l + 1
        )
        normed_second, hidden, slope, *pieces = feed(
            place, share_quarters(normed_own), w_up[l], b_inner[l : l + 1], w_down[l]
        )
        residual, low_next, normed_own, second_squares = add_norm(
            place,
            sum_quarters(pieces),
            residual,
            gathered,
            own_valid,
            rows,
            B_DOWN + l,
            2 * l + 2 if l + 1 < LAYERS else None,
        )
        squares.append((second_squares[1], branch_squares[0], second_squares[0]))
        kept.append((normed, queries, parts, mixed, low_second, normed_second, hidden, slope))
        lows.append(low_next)
        if l + 1 < LAYERS:
            normed_pieces = share_quarters(normed_own)
    residual_out = columns(place, share_quarters(lows[-1]))

    gradient = cotangent_full
    own_low = lax.dynamic_slice_in_dim(cotangent_full, member * quarter, quarter, 0)
    grad_pieces = (cotangent_full,)
    grads = [None] * LAYERS
    sums_down = jnp.sum(own_low.astype(f32), axis=0)
    for l in reversed(range(LAYERS)):
        normed, queries, parts, mixed, low_second, normed_second, hidden, slope = kept[l]
        second_full, grad_inner, grad_b_up, *pieces = feed_back(
            place, grad_pieces, w_up[l], w_down[l], slope
        )
        grad_w_down = jnp.einsum(
            "tf,td->fd", hidden, second_full, preferred_element_type=f32
        ).astype(bf16)
        grad_w_up = jnp.einsum(
            "td,tf->df", normed_second, grad_inner, preferred_element_type=f32
        ).astype(bf16)
        gradient, low, second_sums = norm_back(
            place, sum_quarters(pieces), low_second, gradient, gathered, rows, 2 * l + 1
        )
        dq, branch_full, *kv_grads = attend_back(
            place,
            chosen,
            queries,
            w_mix[l],
            near_valid,
            far_valid,
            share_quarters(low),
            parts,
            count,
        )
        grad_w_out = jnp.einsum(
            "htc,td->hcd", mixed, branch_full, preferred_element_type=f32
        ).astype(bf16)[:, HD:].reshape(heads * HD, D)
        dkv, bias_sums, *pieces = project_back(place, dq, w_all[l], return_blocks(kv_grads))
        grad_q = jnp.einsum("td,htc->dhc", normed, dq, preferred_element_type=f32).astype(bf16)
        grad_kv = jnp.einsum("td,htc->dhc", normed, dkv, preferred_element_type=f32).astype(bf16)
        grad_w_qkv = jnp.stack(
            [
                grad_q[..., :HD].reshape(D, -1),
                grad_kv[..., :HD].reshape(D, -1),
                grad_kv[..., HD:].reshape(D, -1),
            ],
            axis=1,
        )
        gradient, low, first_sums = norm_back(
            place,
            sum_quarters(pieces),
            lows[l - 1] if l else gathered,
            gradient,
            gathered,
            rows,
            2 * l,
        )
        fed = block_sum(jnp.concatenate([grad_w_up, grad_w_down], axis=0))
        attended = block_sum(
            jnp.concatenate([grad_w_out, grad_w_qkv.reshape(-1, D)], axis=0)
        )
        out_rows = heads * HD
        weights = (
            attended[out_rows:].reshape(D, 3, out_rows),
            attended[:out_rows],
            fed[:D],
            fed[D:],
        )
        grads[l] = (
            weights,
            grad_b_up[0],
            jnp.concatenate(
                [
                    bias_sums[:heads, :HD].reshape(-1),
                    bias_sums[heads:, HD:].reshape(-1),
                    jnp.zeros((D - 2 * heads * HD,), f32),
                ]
            ),
            jnp.stack([first_sums[0], second_sums[0]]),
            jnp.stack([first_sums[1], second_sums[1]]),
            second_sums[2],
            sums_down,
        )
        sums_down = first_sums[2]
        if l:
            grad_pieces = share_quarters(low)
    grad_residual = columns(place, share_quarters(low))

    over_all = jnp.concatenate(
        [grads[l][3] for l in range(LAYERS)]
        + [grads[l][4] for l in range(LAYERS)]
        + [jnp.stack([grads[l][5] for l in range(LAYERS)])]
        + [jnp.stack([grads[l][6] for l in range(LAYERS)])]
        + [jnp.stack([vector for layer in squares for vector in layer])],
        axis=0,
    )
    over_tok = jnp.stack(
        [grads[l][1] for l in range(LAYERS)] + [grads[l][2] for l in range(LAYERS)]
    )
    packed = small_sum(
        jnp.concatenate([small_sum(over_all, ("head",)), over_tok], axis=0), ("tok",)
    )
    stat_row = 4 * LAYERS + 2 * LAYERS
    tok_row = stat_row + 3 * LAYERS
    mine = lax.dynamic_slice_in_dim(packed[:stat_row], member * width, width, 1)
    grad_ln_gain = mine[: 2 * LAYERS].reshape(LAYERS, 2, width)
    grad_ln_bias = mine[2 * LAYERS : 4 * LAYERS].reshape(LAYERS, 2, width)
    grad_b_out = mine[4 * LAYERS : 5 * LAYERS]
    grad_b_down = mine[5 * LAYERS : 6 * LAYERS]
    square_sums = jnp.sum(packed[stat_row:tok_row], axis=-1).reshape(LAYERS, 3)
    valid_count = jnp.maximum(jnp.sum(valid.astype(f32)), 1.0)
    statistics = jnp.sqrt(square_sums / (valid_count * D))
    grad_b_up = packed[tok_row : tok_row + LAYERS]
    grad_b_qv = packed[tok_row + LAYERS :, : 2 * heads * HD].reshape(LAYERS, 2, heads * HD)
    stacked = [
        jnp.stack([grads[l][0][m] for l in range(LAYERS)]) for m in range(4)
    ]
    return (
        residual_out,
        grad_residual,
        stacked[0],
        grad_b_qv,
        stacked[1],
        grad_b_out,
        stacked[2],
        grad_b_up,
        stacked[3],
        grad_b_down,
        grad_ln_gain,
        grad_ln_bias,
        statistics,
    )


def solution(mesh):
    in_specs = (
        P("tok", "head"),
        P("tok", "head"),
        P(None, None, None, "head"),
        P(None, None, "head"),
        P(None, "head", None),
        P(None, "head"),
        P(None, None, "head"),
        P(None, "head"),
        P(None, "head", None),
        P(None, "head"),
        P(None, None, "head"),
        P(None, None, "head"),
        P("head", None, None),
        P(),
        P(),
    )
    out_specs = (
        P("tok", "head"),
        P("tok", "head"),
        P(None, None, None, "head"),
        P(None, None, "head"),
        P(None, "head", None),
        P(None, "head"),
        P(None, None, "head"),
        P(None, "head"),
        P(None, "head", None),
        P(None, "head"),
        P(None, None, "head"),
        P(None, None, "head"),
        P(),
    )
    return jax.shard_map(
        on_device, mesh=mesh, in_specs=in_specs, out_specs=out_specs, check_vma=False
    )
```

time: 1330 us -> 692 us (0.52)
  waiting for transfers between devices: 772 us -> 213 us
  blocking collectives: 171 us -> 21.6 us
  starting transfers between devices: 11.8 us -> 127 us
  Pallas kernels: 0 us -> 110 us
  matrix products: 95.3 us -> 12.2 us
  other arithmetic: 96.9 us -> 67.2 us
  local copies, waits for them, and re-layouts: 155 us -> 126 us
  between operations: 18.2 us -> 4.05 us
    psum x1 -> x0, waiting for transfers between devices: 370 us -> none  [on_device(): lax.psum((stacked[0], stacked[1], stacked[2], stacked[3], stacked[4], sta...]
    reduce_scatter x10 -> x0, waiting for transfers between devices: 304 us -> none  [the longest x2 196 us: on_device(): lax.psum_scatter(term.reshape(row_count * lax.axis_size('tok'), head_coun...]
    ppermute x4 -> x105, waiting for transfers between devices: 8.96 us -> 213 us  [the longest x93 175 us: swap(): lax.ppermute(value, axis, [(i, i ^ step) for i in range(lax.axis_size(axi...]
    ppermute x4 -> x105, starting transfers between devices: 10.3 us -> 127 us  [the longest x93 92.1 us: swap(): lax.ppermute(value, axis, [(i, i ^ step) for i in range(lax.axis_size(axi...]
    pallas_call x0 -> x22, Pallas kernels: none -> 110 us  [the longest x2 38.5 us: attend_back(): pl.pallas_call(functools.partial(attend_back_kernel, heads=heads, count=c...]
    all_gather x2 -> x0, waiting for transfers between devices: 88.6 us -> none  [on_device(): shard_piece = lax.all_gather(own_blocks, 'tok', axis=0, tiled=True)]
    dot_general x50 -> x4, matrix products: 92.1 us -> 4.68 us  [the longest x2 3.07 us: on_device(): jnp.einsum('htc,td->hcd', mixed, branch_full, preferred_element_type=f32)]
    psum x2 -> x0, blocking collectives: 79.7 us -> none  [the longest x1 39.9 us: on_device(): square_sums = lax.psum(jnp.stack(local_squares), ('head', 'tok'))]
  transfers between devices with their start and end apart: 17 -> 105, of which waited for: 13 -> 51; matrix products, arithmetic and copies ran while one was open for 8% -> 20% of each run, Pallas kernels for 0% -> 9%
where the time goes in v1:
time: 692 us; the launch traced here: 681 us
  waiting for transfers between devices  213 us (31%)
  starting transfers between devices  127 us (18%)
  local copies, waits for them, and re-layouts  126 us (18%)
  Pallas kernels  110 us (16%)
  other arithmetic  67.2 us (10%)
  blocking collectives  21.6 us (3%)
  matrix products  12.2 us (2%)
    ppermute x93, waiting for transfers between devices, swap(): lax.ppermute(value, axis, [(i, i ^ step) for i in range(lax.axis_size(axi...  175 us
    ppermute x93, starting transfers between devices, swap(): lax.ppermute(value, axis, [(i, i ^ step) for i in range(lax.axis_size(axi...  92.1 us
    unnamed x350, local copies, waits for them, and re-layouts  48.6 us
    pallas_call x2, Pallas kernels, attend_back(): pl.pallas_call(functools.partial(attend_back_kernel, heads=heads, count=c...  38.5 us
    ppermute x12, waiting for transfers between devices, shift_by(): lax.ppermute(value, axis, [(i, i + step) for i in range(count) if 0 <= i...  37.9 us
    ppermute x12, starting transfers between devices, shift_by(): lax.ppermute(value, axis, [(i, i + step) for i in range(count) if 0 <= i...  34.8 us
    pallas_call x2, Pallas kernels, attend(): pl.pallas_call(functools.partial(attend_kernel, heads=heads, count=count,...  27.7 us
    another operation x6, other arithmetic, on_device(): jnp.stack([grads[l][0][m] for l in range(LAYERS)])  14.1 us
  transfers between devices with their start and end apart: 105, of which 51 were waited for; matrix products, arithmetic and copies ran while one was open for 20% of the time, Pallas kernels for 9%

profile of v1, /device:TPU:0, one launch (start us, length us, event | category | flops | bytes accessed | tf_op | source)
XLA Modules:
  0.0 681.1 jit_solution(9044588419212904848)
XLA Ops:
  3.9 11.1 %all_gather.6 = bf16[528,768]{0,1:T(8,128)(2,1)S(1)} all-gather(bf16[528,192]{0,1:T(8,128)(2,1)S(1)} %fusion.19), channel_id=1, replica_groups=mesh['head'=4,'tok'=8] {'head'}, dimensions={1}, use_global_device_ids=true | all-gather | bytes 1013760 | tf_op jit(solution)/shard_map/all_gather | solution.py:802
  29.4 6.4 collective-permute-done.refs_5_.refs_9_
  51.9 5.1 collective-permute-start.5
  64.9 5.8 collective-permute-done.6.refs_11_.refs_15_
  73.7 13.7 %attend.2 = (bf16[3,512,128]{2,1,0:T(8,128)(2,1)S(1)}, bf16[128,768]{1,0:T(8,128)(2,1)S(1)}, bf16[128,768]{1,0:T(8,128)(2,1)S(1)}, bf16[128,768]{1,0:T(8,128)(2,1)}, bf16[128,768]{1,0:T(8,128)(2,1)S(1)}) custom-call(s32[4]{0:T(128)S(1)} %pad_add_fusion.place, s32[3,32]{1,0:T(4,128)S(1)} %reshape.194.chosen, bf16[3,512,128]{2,1,0:T(8,128)(2,1)S(1)} %copy-done.16, ...), custom_call_target="tpu_custom_call" | custom-call | flops 503316480 | bytes 4718592 | tf_op jit(solution)/shard_map/attend/pallas_call | solution.py:359
  92.5 6.0 collective-permute-done.9.refs_2_
  115.3 5.8 collective-permute-done.15.refs_2_
  125.3 5.3 collective-permute-done.16.refs_1_
  142.8 6.5 collective-permute-done.19.refs_5_.refs_9_
  177.9 6.5 collective-permute-done.25.refs_11_.refs_15_
  184.4 14.1 %attend.3 = (bf16[3,512,128]{2,1,0:T(8,128)(2,1)S(1)}, bf16[128,768]{1,0:T(8,128)(2,1)S(1)}, bf16[128,768]{1,0:T(8,128)(2,1)S(1)}, bf16[128,768]{1,0:T(8,128)(2,1)S(1)}, bf16[128,768]{1,0:T(8,128)(2,1)S(1)}) custom-call(s32[4]{0:T(128)S(1)} %pad_add_fusion.place, s32[3,32]{1,0:T(4,128)S(1)} %reshape.194.chosen, ...), custom_call_target="tpu_custom_call" | custom-call | flops 503316480 | bytes 4718592 | tf_op jit(solution)/shard_map/attend/pallas_call | solution.py:359
  201.4 5.8 collective-permute-done.28.refs_2_
  211.3 5.3 collective-permute-done.29.refs_1_
  216.7 10.5 %all_gather.7 = bf16[512,768]{0,1:T(8,128)(2,1)} all-gather(bf16[512,192]{0,1:T(8,128)(2,1)} %param.16), channel_id=1, replica_groups=mesh['head'=4,'tok'=8] {'head'}, dimensions={1}, use_global_device_ids=true | all-gather | bytes 983040 | tf_op jit(solution)/shard_map/all_gather | solution.py:805
  272.3 19.8 %attend_back.2 = (bf16[3,512,128]{2,1,0:T(8,128)(2,1)S(1)}, bf16[512,768]{1,0:T(8,128)(2,1)S(1)}, bf16[3,512,128]{2,1,0:T(8,128)(2,1)S(1)}, bf16[3,512,128]{2,1,...) custom-call(s32[4]{0:T(128)S(1)} %pad_add_fusion.place, ...), custom_call_target="tpu_custom_call" | custom-call | flops 905969664 | bytes 9437184 | tf_op jit(solution)/shard_map/attend_back/pallas_call | solution.py:461
  318.4 5.7 collective-permute-done.48
  328.2 6.0 collective-permute-done.101
  335.1 6.0 collective-permute-done.49
  357.6 9.1 %collective-permute-start.103 = (bf16[384,768]{1,0:T(8,128)(2,1)}, bf16[384,768]{1,0:T(8,128)(2,1)}, u32[]{:S(2)}, u32[]{:S(2)}) collective-permute-start(bf16[384,768]{1,0:T(8,128)(2,1)} %pad_maximum_fusion.15), channel_id=1, source_target_pairs={{0,2},{1,3},{2,0},{3,1},{4,6},{5,7},{6,4},{7,5},{8,10},{9,11},{10,... | collective-permute-start | bytes 1769480 | tf_op jit(solution)/shard_map/ppermute | solution.py:38
  424.7 7.7 %collective-permute-done.84 = bf16[96,768]{1,0:T(8,128)(2,1)S(1)} collective-permute-done((bf16[96,768]{1,0:T(8,128)(2,1)S(1)}, bf16[96,768]{1,0:T(8,128)(2,1)S(1)}, u32[]{:S(2)}, u32[]{:S(2)}) %collective-permute-start.84) | collective-permute-done | bytes 147488 | tf_op jit(solution)/shard_map/ppermute | solution.py:38
  433.8 8.3 %collective-permute-done.85 = bf16[96,768]{1,0:T(8,128)(2,1)S(1)} collective-permute-done((bf16[96,768]{1,0:T(8,128)(2,1)S(1)}, bf16[96,768]{1,0:T(8,128)(2,1)S(1)}, u32[]{:S(2)}, u32[]{:S(2)}) %collective-permute-start.85) | collective-permute-done | bytes 147488 | tf_op jit(solution)/shard_map/ppermute | solution.py:38
  453.9 18.7 %attend_back.3 = (bf16[3,512,128]{2,1,0:T(8,128)(2,1)S(1)}, bf16[512,768]{1,0:T(8,128)(2,1)S(1)}, bf16[3,512,128]{2,1,0:T(8,128)(2,1)S(1)}, bf16[3,512,128]{2,1,...) custom-call(s32[4]{0:T(128)S(1)} %pad_add_fusion.place, ...), custom_call_target="tpu_custom_call" | custom-call | flops 905969664 | bytes 9437184 | tf_op jit(solution)/shard_map/attend_back/pallas_call | solution.py:461
  496.4 5.6 collective-permute-done.66
  510.5 7.2 %collective-permute-done.67 = bf16[3,512,128]{2,1,0:T(8,128)(2,1)S(1)} collective-permute-done((bf16[3,512,128]{2,1,0:T(8,128)(2,1)S(1)}, bf16[3,512,128]{2,1,0:T(8,128)(2,1)S(1)}, u32[]{:S(2)}, u32[]{:S(2)}) %collective-permute-start.67) | collective-permute-done | bytes 393248 | tf_op jit(solution)/shard_map/ppermute | solution.py:43
  523.9 6.4 collective-permute-done.68
  538.9 7.0 %collective-permute-done.95 = bf16[192,768]{1,0:T(8,128)(2,1)} collective-permute-done((bf16[192,768]{1,0:T(8,128)(2,1)}, bf16[192,768]{1,0:T(8,128)(2,1)}, u32[]{:S(2)}, u32[]{:S(2)}) %collective-permute-start.95) | collective-permute-done | bytes 294944 | tf_op jit(solution)/shard_map/ppermute | solution.py:38
  576.3 10.2 %collective-permute-start.97 = (bf16[384,768]{1,0:T(8,128)(2,1)}, bf16[384,768]{1,0:T(8,128)(2,1)}, u32[]{:S(2)}, u32[]{:S(2)}) collective-permute-start(bf16[384,768]{1,0:T(8,128)(2,1)} %pad_maximum_fusion.14), channel_id=1, source_target_pairs={{0,2},{1,3},{2,0},{3,1},{4,6},{5,7},{6,4},{7,5},{8,10},{9,11},{10,... | collective-permute-start | bytes 1769480 | tf_op jit(solution)/shard_map/ppermute | solution.py:38
  590.9 8.6 %collective-permute-start.77 = (bf16[192,768]{1,0:T(8,128)(2,1)}, bf16[192,768]{1,0:T(8,128)(2,1)S(1)}, u32[]{:S(2)}, u32[]{:S(2)}) collective-permute-start(bf16[192,768]{1,0:T(8,128)(2,1)} %dynamic-slice_bitcast_fusion.9), channel_id=1, source_target_pairs={{0,2},{1,3},{2,0},{3,1},{4,6},{5,7},{6,4},{7,5},{8,10},{9,11},{10,... | collective-permute-start | bytes 884744 | tf_op jit(solution)/shard_map/ppermute | solution.py:38
  613.2 6.5 collective-permute-done.78
  637.1 13.1 %collective-permute-done.98 = bf16[768,768]{1,0:T(8,128)(2,1)} collective-permute-done((bf16[768,768]{1,0:T(8,128)(2,1)}, bf16[768,768]{1,0:T(8,128)(2,1)}, u32[]{:S(2)}, u32[]{:S(2)}) %collective-permute-start.98) | collective-permute-done | bytes 1179680 | tf_op jit(solution)/shard_map/ppermute | solution.py:38
  665.8 7.1 %pad_maximum_fusion = f32[2,768,3,192]{3,2,1,0:T(4,128)} fusion(f32[1,768,3,192]{3,2,1,0:T(4,128)} %stack_reshape.31, f32[1,768,3,192]{3,2,1,0:T(4,128)} %stack_reshape.27), kind=kLoop, calls=%fused_computation | loop fusion | flops 884736 | bytes 7077888 | tf_op jit(solution)/shard_map/stack | solution.py:987
  672.9 6.6 copy.183
  (735 shorter events, 409.5 us)
Async XLA Ops:
  211.3 17.2 %collective-permute-start.30 = (bf16[128,768]{1,0:T(8,128)(2,1)}, bf16[128,768]{1,0:T(8,128)(2,1)}, u32[]{:S(2)}, u32[]{:S(2)}) collective-permute-start(bf16[128,768]{1,0:T(8,128)(2,1)} %get-tuple-element.170.refs_0_), channel_id=1, source_target_pairs={{0,8},{8,0},{16,24},{24,16},{1,9},{9,1},{17,25},{25,17},{2,10},{10... | collective-permute-start | bytes 589832 | tf_op jit(solution)/shard_map/ppermute | solution.py:38
  243.3 49.4 %collective-permute-start.99 = (bf16[768,768]{1,0:T(8,128)(2,1)}, bf16[768,768]{1,0:T(8,128)(2,1)}, u32[]{:S(2)}, u32[]{:S(2)}) collective-permute-start(bf16[768,768]{1,0:T(8,128)(2,1)} %dynamic-slice_bitcast_fusion), channel_id=1, source_target_pairs={{0,1},{1,0},{2,3},{3,2},{4,5},{5,4},{6,7},{7,6},{8,9},{9,8},{10,11... | collective-permute-start | bytes 3538952 | tf_op jit(solution)/shard_map/ppermute | solution.py:38
  271.3 36.1 %collective-permute-start.35 = (bf16[128,768]{1,0:T(8,128)(2,1)}, bf16[128,768]{1,0:T(8,128)(2,1)}, u32[]{:S(2)}, u32[]{:S(2)}) collective-permute-start(bf16[128,768]{1,0:T(8,128)(2,1)} %get-tuple-element.176.refs_0_), channel_id=1, source_target_pairs={{0,16},{8,24},{16,0},{24,8},{1,17},{9,25},{17,1},{25,9},{2,18},{10... | collective-permute-start | bytes 589832 | tf_op jit(solution)/shard_map/ppermute | solution.py:38
  272.2 72.4 %collective-permute-start.36 = (bf16[128,768]{1,0:T(8,128)(2,1)}, bf16[128,768]{1,0:T(8,128)(2,1)}, u32[]{:S(2)}, u32[]{:S(2)}) collective-permute-start(bf16[128,768]{1,0:T(8,128)(2,1)} %get-tuple-element.176.refs_0_), channel_id=1, source_target_pairs={{0,8},{8,0},{16,24},{24,16},{1,9},{9,1},{17,25},{25,17},{2,10},{10... | collective-permute-start | bytes 589832 | tf_op jit(solution)/shard_map/ppermute | solution.py:38
  305.0 19.0 %collective-permute-start.48 = (bf16[3,512,128]{2,1,0:T(8,128)(2,1)}, bf16[3,512,128]{2,1,0:T(8,128)(2,1)}, u32[]{:S(2)}, u32[]{:S(2)}) collective-permute-start(bf16[3,512,128]{2,1,0:T(8,128)(2,1)} %add_convert_fusion.5), channel_id=1, source_target_pairs={{2,0},{3,1},{4,2},{5,3},{6,4},{7,5},{10,8},{11,9},{12,10},{13,11},... | collective-permute-start | bytes 1179656 | tf_op jit(solution)/shard_map/ppermute | solution.py:43
  307.4 37.2 %collective-permute-start.37 = (bf16[128,768]{1,0:T(8,128)(2,1)}, bf16[128,768]{1,0:T(8,128)(2,1)}, u32[]{:S(2)}, u32[]{:S(2)}) collective-permute-start(bf16[128,768]{1,0:T(8,128)(2,1)} %collective-permute-done.35.refs_1_), channel_id=1, source_target_pairs={{0,8},{8,0},{16,24},{24,16},{1,9},{9,1},{17,25},{25,17},{2,10},{10... | collective-permute-start | bytes 589832 | tf_op jit(solution)/shard_map/ppermute | solution.py:38
  312.7 22.4 %collective-permute-start.45 = (bf16[3,512,128]{2,1,0:T(8,128)(2,1)}, bf16[3,512,128]{2,1,0:T(8,128)(2,1)S(1)}, u32[]{:S(2)}, u32[]{:S(2)}) collective-permute-start(bf16[3,512,128]{2,1,0:T(8,128)(2,1)} %copy-done.116), channel_id=1, source_target_pairs={{0,1},{1,0},{2,3},{3,2},{4,5},{5,4},{6,7},{7,6},{8,9},{9,8},{10,11... | collective-permute-start | bytes 1179656 | tf_op jit(solution)/shard_map/ppermute | solution.py:38
  315.2 19.0 %collective-permute-start.101 = (bf16[192,768]{1,0:T(8,128)(2,1)S(1)}, bf16[192,768]{1,0:T(8,128)(2,1)S(1)}, u32[]{:S(2)}, u32[]{:S(2)}) collective-permute-start(bf16[192,768]{1,0:T(8,128)(2,1)S(1)} %dynamic-slice_bitcast_fusion.6), channel_id=1, source_target_pairs={{0,4},{1,5},{2,6},{3,7},{4,0},{5,1},{6,2},{7,3},{8,12},{9,13},{10,... | collective-permute-start | bytes 884744 | tf_op jit(solution)/shard_map/ppermute | solution.py:38
  334.2 32.5 %collective-permute-start.44 = (bf16[3,512,128]{2,1,0:T(8,128)(2,1)}, bf16[3,512,128]{2,1,0:T(8,128)(2,1)}, u32[]{:S(2)}, u32[]{:S(2)}) collective-permute-start(bf16[3,512,128]{2,1,0:T(8,128)(2,1)} %get-tuple-element.186), channel_id=1, source_target_pairs={{0,1},{1,0},{2,3},{3,2},{4,5},{5,4},{6,7},{7,6},{8,9},{9,8},{10,11... | collective-permute-start | bytes 1179656 | tf_op jit(solution)/shard_map/ppermute | solution.py:38
  335.1 20.4 %collective-permute-start.102 = (bf16[192,768]{1,0:T(8,128)(2,1)}, bf16[192,768]{1,0:T(8,128)(2,1)}, u32[]{:S(2)}, u32[]{:S(2)}) collective-permute-start(bf16[192,768]{1,0:T(8,128)(2,1)} %fusion.12), channel_id=1, source_target_pairs={{0,4},{1,5},{2,6},{3,7},{4,0},{5,1},{6,2},{7,3},{8,12},{9,13},{10,... | collective-permute-start | bytes 884744 | tf_op jit(solution)/shard_map/ppermute | solution.py:38
  342.0 24.7 %collective-permute-start.50 = (bf16[3,512,128]{2,1,0:T(8,128)(2,1)}, bf16[3,512,128]{2,1,0:T(8,128)(2,1)}, u32[]{:S(2)}, u32[]{:S(2)}) collective-permute-start(bf16[3,512,128]{2,1,0:T(8,128)(2,1)} %add_convert_fusion.3), channel_id=1, source_target_pairs={{2,0},{3,1},{4,2},{5,3},{6,4},{7,5},{10,8},{11,9},{12,10},{13,11},... | collective-permute-start | bytes 1179656 | tf_op jit(solution)/shard_map/ppermute | solution.py:43
  357.6 49.5 %collective-permute-start.103 = (bf16[384,768]{1,0:T(8,128)(2,1)}, bf16[384,768]{1,0:T(8,128)(2,1)}, u32[]{:S(2)}, u32[]{:S(2)}) collective-permute-start(bf16[384,768]{1,0:T(8,128)(2,1)} %pad_maximum_fusion.15), channel_id=1, source_target_pairs={{0,2},{1,3},{2,0},{3,1},{4,6},{5,7},{6,4},{7,5},{8,10},{9,11},{10,... | collective-permute-start | bytes 1769480 | tf_op jit(solution)/shard_map/ppermute | solution.py:38
  373.1 26.2 %collective-permute-start.51 = (bf16[128,768]{1,0:T(8,128)(2,1)}, bf16[128,768]{1,0:T(8,128)(2,1)}, u32[]{:S(2)}, u32[]{:S(2)}) collective-permute-start(bf16[128,768]{1,0:T(8,128)(2,1)} %get-tuple-element.194), channel_id=1, source_target_pairs={{0,8},{8,0},{16,24},{24,16},{1,9},{9,1},{17,25},{25,17},{2,10},{10... | collective-permute-start | bytes 589832 | tf_op jit(solution)/shard_map/ppermute | solution.py:38
  373.1 22.1 %collective-permute-start.52 = (bf16[128,768]{1,0:T(8,128)(2,1)}, bf16[128,768]{1,0:T(8,128)(2,1)}, u32[]{:S(2)}, u32[]{:S(2)}) collective-permute-start(bf16[128,768]{1,0:T(8,128)(2,1)} %get-tuple-element.196), channel_id=1, source_target_pairs={{0,8},{8,0},{16,24},{24,16},{1,9},{9,1},{17,25},{25,17},{2,10},{10... | collective-permute-start | bytes 589832 | tf_op jit(solution)/shard_map/ppermute | solution.py:38
  409.5 78.4 %collective-permute-start.104 = (bf16[768,768]{1,0:T(8,128)(2,1)}, bf16[768,768]{1,0:T(8,128)(2,1)}, u32[]{:S(2)}, u32[]{:S(2)}) collective-permute-start(bf16[768,768]{1,0:T(8,128)(2,1)} %pad_maximum_fusion.11), channel_id=1, source_target_pairs={{0,1},{1,0},{2,3},{3,2},{4,5},{5,4},{6,7},{7,6},{8,9},{9,8},{10,11... | collective-permute-start | bytes 3538952 | tf_op jit(solution)/shard_map/ppermute | solution.py:38
  416.7 28.1 %collective-permute-start.57 = (bf16[128,768]{1,0:T(8,128)(2,1)S(1)}, bf16[128,768]{1,0:T(8,128)(2,1)S(1)}, u32[]{:S(2)}, u32[]{:S(2)}) collective-permute-start(bf16[128,768]{1,0:T(8,128)(2,1)S(1)} %get-tuple-element.202), channel_id=1, source_target_pairs={{0,8},{8,0},{16,24},{24,16},{1,9},{9,1},{17,25},{25,17},{2,10},{10... | collective-permute-start | bytes 589832 | tf_op jit(solution)/shard_map/ppermute | solution.py:38
  443.3 48.3 %collective-permute-start.93 = (bf16[768,768]{1,0:T(8,128)(2,1)}, bf16[768,768]{1,0:T(8,128)(2,1)}, u32[]{:S(2)}, u32[]{:S(2)}) collective-permute-start(bf16[768,768]{1,0:T(8,128)(2,1)} %dynamic-slice_bitcast_fusion.1), channel_id=1, source_target_pairs={{0,1},{1,0},{2,3},{3,2},{4,5},{5,4},{6,7},{7,6},{8,9},{9,8},{10,11... | collective-permute-start | bytes 3538952 | tf_op jit(solution)/shard_map/ppermute | solution.py:38
  453.3 65.9 %collective-permute-start.87 = (bf16[384,768]{1,0:T(8,128)(2,1)}, bf16[384,768]{1,0:T(8,128)(2,1)}, u32[]{:S(2)}, u32[]{:S(2)}) collective-permute-start(bf16[384,768]{1,0:T(8,128)(2,1)} %pad_maximum_fusion.13), channel_id=1, source_target_pairs={{0,1},{1,0},{2,3},{3,2},{4,5},{5,4},{6,7},{7,6},{8,9},{9,8},{10,11... | collective-permute-start | bytes 1769480 | tf_op jit(solution)/shard_map/ppermute | solution.py:38
  478.8 70.7 %collective-permute-start.63 = (bf16[3,512,128]{2,1,0:T(8,128)(2,1)}, bf16[3,512,128]{2,1,0:T(8,128)(2,1)}, u32[]{:S(2)}, u32[]{:S(2)}) collective-permute-start(bf16[3,512,128]{2,1,0:T(8,128)(2,1)} %get-tuple-element.210), channel_id=1, source_target_pairs={{0,1},{1,0},{2,3},{3,2},{4,5},{5,4},{6,7},{7,6},{8,9},{9,8},{10,11... | collective-permute-start | bytes 1179656 | tf_op jit(solution)/shard_map/ppermute | solution.py:38
  480.3 21.7 %collective-permute-start.66 = (bf16[3,512,128]{2,1,0:T(8,128)(2,1)}, bf16[3,512,128]{2,1,0:T(8,128)(2,1)}, u32[]{:S(2)}, u32[]{:S(2)}) collective-permute-start(bf16[3,512,128]{2,1,0:T(8,128)(2,1)} %get-tuple-element.216), channel_id=1, source_target_pairs={{0,1},{1,0},{2,3},{3,2},{4,5},{5,4},{6,7},{7,6},{8,9},{9,8},{10,11... | collective-permute-start | bytes 1179656 | tf_op jit(solution)/shard_map/ppermute | solution.py:38
  487.9 21.1 %collective-permute-start.65 = (bf16[3,512,128]{2,1,0:T(8,128)(2,1)S(1)}, bf16[3,512,128]{2,1,0:T(8,128)(2,1)S(1)}, u32[]{:S(2)}, u32[]{:S(2)}) collective-permute-start(bf16[3,512,128]{2,1,0:T(8,128)(2,1)S(1)} %copy-done.118), channel_id=1, source_target_pairs={{0,1},{1,0},{2,3},{3,2},{4,5},{5,4},{6,7},{7,6},{8,9},{9,8},{10,11... | collective-permute-start | bytes 1179656 | tf_op jit(solution)/shard_map/ppermute | solution.py:38
  494.6 25.9 %collective-permute-start.94 = (bf16[384,768]{1,0:T(8,128)(2,1)S(1)}, bf16[384,768]{1,0:T(8,128)(2,1)S(1)}, u32[]{:S(2)}, u32[]{:S(2)}) collective-permute-start(bf16[384,768]{1,0:T(8,128)(2,1)S(1)} %dynamic-slice_bitcast_fusion.3), channel_id=1, source_target_pairs={{0,2},{1,3},{2,0},{3,1},{4,6},{5,7},{6,4},{7,5},{8,10},{9,11},{10,... | collective-permute-start | bytes 1769480 | tf_op jit(solution)/shard_map/ppermute | solution.py:38
  521.5 24.4 %collective-permute-start.95 = (bf16[192,768]{1,0:T(8,128)(2,1)}, bf16[192,768]{1,0:T(8,128)(2,1)}, u32[]{:S(2)}, u32[]{:S(2)}) collective-permute-start(bf16[192,768]{1,0:T(8,128)(2,1)} %dynamic-slice_bitcast_fusion.7), channel_id=1, source_target_pairs={{0,4},{1,5},{2,6},{3,7},{4,0},{5,1},{6,2},{7,3},{8,12},{9,13},{10,... | collective-permute-start | bytes 884744 | tf_op jit(solution)/shard_map/ppermute | solution.py:38
  531.2 18.3 %collective-permute-start.69 = (bf16[3,512,128]{2,1,0:T(8,128)(2,1)}, bf16[3,512,128]{2,1,0:T(8,128)(2,1)}, u32[]{:S(2)}, u32[]{:S(2)}) collective-permute-start(bf16[3,512,128]{2,1,0:T(8,128)(2,1)} %add_convert_fusion), channel_id=1, source_target_pairs={{2,0},{3,1},{4,2},{5,3},{6,4},{7,5},{10,8},{11,9},{12,10},{13,11},... | collective-permute-start | bytes 1179656 | tf_op jit(solution)/shard_map/ppermute | solution.py:43
  547.7 26.6 %collective-permute-start.96 = (bf16[192,768]{1,0:T(8,128)(2,1)}, bf16[192,768]{1,0:T(8,128)(2,1)}, u32[]{:S(2)}, u32[]{:S(2)}) collective-permute-start(bf16[192,768]{1,0:T(8,128)(2,1)} %fusion.13), channel_id=1, source_target_pairs={{0,4},{1,5},{2,6},{3,7},{4,0},{5,1},{6,2},{7,3},{8,12},{9,13},{10,... | collective-permute-start | bytes 884744 | tf_op jit(solution)/shard_map/ppermute | solution.py:38
  556.2 30.4 %collective-permute-start.70 = (bf16[128,768]{1,0:T(8,128)(2,1)}, bf16[128,768]{1,0:T(8,128)(2,1)S(1)}, u32[]{:S(2)}, u32[]{:S(2)}) collective-permute-start(bf16[128,768]{1,0:T(8,128)(2,1)} %get-tuple-element.218), channel_id=1, source_target_pairs={{0,8},{8,0},{16,24},{24,16},{1,9},{9,1},{17,25},{25,17},{2,10},{10... | collective-permute-start | bytes 589832 | tf_op jit(solution)/shard_map/ppermute | solution.py:38
  571.6 17.0 %collective-permute-start.76 = (bf16[384,768]{1,0:T(8,128)(2,1)}, bf16[384,768]{1,0:T(8,128)(2,1)}, u32[]{:S(2)}, u32[]{:S(2)}) collective-permute-start(bf16[384,768]{1,0:T(8,128)(2,1)} %dynamic-slice_bitcast_fusion.5), channel_id=1, source_target_pairs={{0,1},{1,0},{2,3},{3,2},{4,5},{5,4},{6,7},{7,6},{8,9},{9,8},{10,11... | collective-permute-start | bytes 1769480 | tf_op jit(solution)/shard_map/ppermute | solution.py:38
  576.3 33.6 %collective-permute-start.97 = (bf16[384,768]{1,0:T(8,128)(2,1)}, bf16[384,768]{1,0:T(8,128)(2,1)}, u32[]{:S(2)}, u32[]{:S(2)}) collective-permute-start(bf16[384,768]{1,0:T(8,128)(2,1)} %pad_maximum_fusion.14), channel_id=1, source_target_pairs={{0,2},{1,3},{2,0},{3,1},{4,6},{5,7},{6,4},{7,5},{8,10},{9,11},{10,... | collective-permute-start | bytes 1769480 | tf_op jit(solution)/shard_map/ppermute | solution.py:38
  590.9 17.8 %collective-permute-start.77 = (bf16[192,768]{1,0:T(8,128)(2,1)}, bf16[192,768]{1,0:T(8,128)(2,1)S(1)}, u32[]{:S(2)}, u32[]{:S(2)}) collective-permute-start(bf16[192,768]{1,0:T(8,128)(2,1)} %dynamic-slice_bitcast_fusion.9), channel_id=1, source_target_pairs={{0,2},{1,3},{2,0},{3,1},{4,6},{5,7},{6,4},{7,5},{8,10},{9,11},{10,... | collective-permute-start | bytes 884744 | tf_op jit(solution)/shard_map/ppermute | solution.py:38
  606.8 24.2 %collective-permute-start.74 = (bf16[128,768]{1,0:T(8,128)(2,1)S(1)}, bf16[128,768]{1,0:T(8,128)(2,1)S(1)}, u32[]{:S(2)}, u32[]{:S(2)}) collective-permute-start(bf16[128,768]{1,0:T(8,128)(2,1)S(1)} %get-tuple-element.222.refs_0_), channel_id=1, source_target_pairs={{0,8},{8,0},{16,24},{24,16},{1,9},{9,1},{17,25},{25,17},{2,10},{10... | collective-permute-start | bytes 589832 | tf_op jit(solution)/shard_map/ppermute | solution.py:38
  621.0 29.2 %collective-permute-start.98 = (bf16[768,768]{1,0:T(8,128)(2,1)}, bf16[768,768]{1,0:T(8,128)(2,1)}, u32[]{:S(2)}, u32[]{:S(2)}) collective-permute-start(bf16[768,768]{1,0:T(8,128)(2,1)} %pad_maximum_fusion.10), channel_id=1, source_target_pairs={{0,1},{1,0},{2,3},{3,2},{4,5},{5,4},{6,7},{7,6},{8,9},{9,8},{10,11... | collective-permute-start | bytes 3538952 | tf_op jit(solution)/shard_map/ppermute | solution.py:38
  635.3 23.8 %collective-permute-start.81 = (bf16[384,768]{1,0:T(8,128)(2,1)S(1)}, bf16[384,768]{1,0:T(8,128)(2,1)S(1)}, u32[]{:S(2)}, u32[]{:S(2)}) collective-permute-start(bf16[384,768]{1,0:T(8,128)(2,1)S(1)} %pad_maximum_fusion.12), channel_id=1, source_target_pairs={{0,1},{1,0},{2,3},{3,2},{4,5},{5,4},{6,7},{7,6},{8,9},{9,8},{10,11... | collective-permute-start | bytes 1769480 | tf_op jit(solution)/shard_map/ppermute | solution.py:38
  (245 other events, 2482.1 us)

commit v2 on v1

v2 whole, which is shorter than its diff:
```python
import functools

import jax
import jax.numpy as jnp
from jax import lax
from jax.experimental import pallas as pl
from jax.experimental.pallas import tpu as pltpu
from jax.sharding import PartitionSpec as P

D = 768
HD = 64
LAYERS = 2
WINDOW = 64
KB = 16
SEL = 4
QB = 64
WIDE = 2 * HD

epsilon = 1e-05
negative = -1e30
scale = HD ** (-0.5)
bf16 = jnp.bfloat16
f32 = jnp.float32

STEPS = (0, 2, 1, 3)
GAIN, SHIFT, B_OUT, B_DOWN, PARAM_ROWS = 0, 4, 8, 10, 16


def params(megabytes):
    return pltpu.CompilerParams(vmem_limit_bytes=megabytes * 2**20)


def cost(flops, moved, special=0):
    return pl.CostEstimate(flops=int(flops), bytes_accessed=int(moved), transcendentals=int(special))


def swap(value, axis, step):
    return lax.ppermute(value, axis, [(i, i ^ step) for i in range(lax.axis_size(axis))])


def rotate(value, axis, step):
    count = lax.axis_size(axis)
    return lax.ppermute(value, axis, [(i, (i + step) % count) for i in range(count)])


def share_quarters(own):
    across = swap(own, "head", 2)
    beside = swap(own, "head", 1)
    both = swap(across, "head", 1)
    return own, across, beside, both


def sum_quarters(pieces):
    own, across, beside, both = pieces
    first = swap(both, "head", 1)
    onward = (across.astype(f32) + first.astype(f32)).astype(bf16)
    second = swap(beside, "head", 1)
    third = swap(onward, "head", 2)
    return own, second, third


def small_sum(value, axes):
    for axis in axes:
        step = 1
        while step < lax.axis_size(axis):
            value = value + swap(value, axis, step)
            step *= 2
    return value


def ring_form(count):
    return count == 8


ORDERS = ((0, 1, 2), (1, 2, 0))


class Bundle:
    def __init__(self, halves):
        self.ring = ring_form(lax.axis_size("tok"))
        self.step = 0
        if not self.ring:
            self.result = lax.psum(halves, "tok")
            return
        self.kept = [keep for keep, give in halves]
        self.start([give for keep, give in halves], 0)

    def start(self, values, stage):
        self.coming = [
            swap(value, "tok", 1 << order[stage]) for value, order in zip(values, ORDERS)
        ]

    def advance(self, other):
        if not self.ring or self.step == 6:
            return other
        coming, other = lax.optimization_barrier((self.coming, other))
        self.step += 1
        if self.step < 3:
            self.kept, gives = fold(self.kept, coming)
            self.start(gives, self.step)
        elif self.step == 3:
            self.kept, _ = fold(self.kept, coming)
            self.start(self.kept, 2)
        elif self.step < 6:
            self.kept = join(self.kept, coming)
            self.start(self.kept, 5 - self.step)
        else:
            self.result = list(zip(self.kept, coming))
        return other


def gather_blocks(own):
    count = lax.axis_size("tok")
    if not ring_form(count):
        return [lax.all_gather(own, "tok")]
    current = own
    parts = []
    for hop in range(count // 2):
        other = swap(current, "tok", 1)
        after = None
        if hop < count // 2 - 1:
            after = rotate(current, "tok", 2)
            current, other, after = lax.optimization_barrier((current, other, after))
        parts += [current, other]
        current = after
    return parts


def return_blocks(parts, between):
    count = lax.axis_size("tok")
    if not ring_form(count):
        return [lax.psum_scatter(parts[0], "tok", scatter_dimension=0, tiled=False)]
    running = None
    for d in range(count // 2 - 1, 0, -1):
        got = swap(parts[2 * d + 1], "tok", 1)
        total = parts[2 * d].astype(f32) + got.astype(f32)
        if running is not None:
            total = total + running.astype(f32)
        running = rotate(total.astype(bf16), "tok", -2)
        if d == 2:
            running = between(running)
    return [parts[0], swap(parts[1], "tok", 1), running]


def slot_of(block, tok, count):
    if not ring_form(count):
        return block
    away = (tok >> 1) - (block >> 1)
    return 2 * jnp.maximum(away, 0) + ((tok ^ block) & 1)


ON_LANES = (((1,), (1,)), ((), ()))
ON_ROWS = (((0,), (0,)), ((), ()))


def normalise(rows):
    average = jnp.mean(rows, axis=-1, keepdims=True)
    centred = rows - average
    spread = jnp.mean(centred * centred, axis=-1, keepdims=True)
    inverse = lax.rsqrt(spread + epsilon)
    return centred * inverse, inverse


def row(ref, index):
    return ref[index : index + 1, :].astype(f32)


def piece_rows(place, step, size):
    return pl.ds(pl.multiple_of((place[0] ^ step) * size, size), size)


def project_kernel(place, *refs, heads, first):
    pieces = refs[:4]
    if first:
        param_pieces = refs[4:8]
        w_ref, bias_ref, normed_ref, q_ref, kv_ref, low_ref, param_ref, staged, turned = refs[8:]
        width = staged.shape[0] // 4
        for k in range(4):
            staged[piece_rows(place, STEPS[k], width), :] = pieces[k][...]
            turned[piece_rows(place, STEPS[k], width), :] = param_pieces[k][...].astype(f32)
        param_ref[...] = jnp.transpose(turned[...])[:PARAM_ROWS]
    else:
        w_ref, bias_ref, normed_ref, q_ref, kv_ref = refs[4:]
    size = normed_ref.shape[0] // 4
    for k in range(4):
        if first:
            rows = pl.ds(k * size, size)
            part = jnp.transpose(staged[:, k * size : (k + 1) * size].astype(f32))

            @pl.when(place[0] == k)
            def _():
                low_ref[...] = part.astype(bf16)

            unit, _ = normalise(part)
            normed = (unit * row(param_ref, GAIN) + row(param_ref, SHIFT)).astype(bf16)
        else:
            rows = piece_rows(place, STEPS[k], size)
            normed = pieces[k][...]
        normed_ref[rows, :] = normed
        projected = lax.dot_general(normed, w_ref[...], ON_LANES, preferred_element_type=f32)
        projected = projected + bias_ref[...]
        for h in range(heads):
            q_ref[h, rows, :] = (projected[:, h * WIDE : (h + 1) * WIDE] * scale).astype(bf16)
            at = (heads + h) * WIDE
            kv_ref[h, rows, :] = projected[:, at : at + WIDE].astype(bf16)


def whole(shape):
    return pl.BlockSpec(shape, lambda *_: (0,) * len(shape))


def project(place, pieces, param_pieces, w_all, bias_all, rows, heads):
    first = param_pieces is not None
    arrays = tuple(pieces) + (tuple(param_pieces) if first else ())
    columns = w_all.shape[0]
    out_shapes = [
        jax.ShapeDtypeStruct((rows, D), bf16),
        jax.ShapeDtypeStruct((heads, rows, WIDE), bf16),
        jax.ShapeDtypeStruct((heads, rows, WIDE), bf16),
    ]
    scratch = []
    if first:
        out_shapes += [
            jax.ShapeDtypeStruct((rows // 4, D), bf16),
            jax.ShapeDtypeStruct((PARAM_ROWS, D), f32),
        ]
        scratch = [pltpu.VMEM((D, rows), bf16), pltpu.VMEM((D, 128), f32)]
    return pl.pallas_call(
        functools.partial(project_kernel, heads=heads, first=first),
        grid_spec=pltpu.PrefetchScalarGridSpec(
            num_scalar_prefetch=1,
            grid=(1,),
            in_specs=[whole(array.shape) for array in arrays + (w_all, bias_all)],
            out_specs=[whole(shape.shape) for shape in out_shapes],
            scratch_shapes=scratch,
        ),
        out_shape=out_shapes,
        compiler_params=params(12),
        cost_estimate=cost(2 * rows * D * columns, 2 * D * columns + 8 * rows * D),
        name="project",
    )(place, *arrays, w_all, bias_all)


def turn_kernel(place, *refs):
    pieces = refs[:4]
    out_ref, sums_ref, staged = refs[4:]
    width = staged.shape[0] // 4
    size = out_ref.shape[0] // 4
    for k in range(4):
        staged[piece_rows(place, STEPS[k], width), :] = pieces[k][...]
    for k in range(4):
        part = jnp.transpose(staged[:, k * size : (k + 1) * size].astype(f32))
        out_ref[k * size : (k + 1) * size, :] = part.astype(bf16)

        @pl.when(place[0] == k)
        def _():
            sums_ref[...] = jnp.sum(part, axis=0, keepdims=True)


def turn(place, pieces):
    width, rows = pieces[0].shape
    return pl.pallas_call(
        turn_kernel,
        grid_spec=pltpu.PrefetchScalarGridSpec(
            num_scalar_prefetch=1,
            grid=(1,),
            in_specs=[whole((width, rows))] * 4,
            out_specs=[whole((rows, D)), whole((1, D))],
            scratch_shapes=[pltpu.VMEM((D, rows), bf16)],
        ),
        out_shape=[jax.ShapeDtypeStruct((rows, D), bf16), jax.ShapeDtypeStruct((1, D), f32)],
        compiler_params=params(6),
        cost_estimate=cost(rows * D, 4 * rows * D),
        name="turn",
    )(place, *pieces)


def fold_kernel(*refs, count):
    for half in range(2):
        kept, came = refs[2 * half : 2 * half + 2]
        keep_ref = refs[4 + half]
        total = lambda at: (kept[at].astype(f32) + came[at].astype(f32)).astype(bf16)
        if count == 1:
            keep_ref[...] = total(slice(0, 1))
        else:
            keep_ref[...] = total(slice(0, count // 2))
            refs[6 + half][...] = total(slice(count // 2, count))


def fold(kept, came):
    count = kept[0].shape[0]
    after = max(count // 2, 1)
    outs = 2 if count == 1 else 4
    shapes = [(after,) + kept[i % 2].shape[1:] for i in range(outs)]
    results = pl.pallas_call(
        functools.partial(fold_kernel, count=count),
        grid=(1,),
        in_specs=[whole(kept[i // 2].shape) for i in range(4)],
        out_specs=[whole(shape) for shape in shapes],
        out_shape=[jax.ShapeDtypeStruct(shape, bf16) for shape in shapes],
        compiler_params=params(8),
        cost_estimate=cost(2 * kept[0].size, 12 * kept[0].size),
        name="fold",
    )(kept[0], came[0], kept[1], came[1])
    return list(results[:2]), list(results[2:])


def join_kernel(*refs):
    for half in range(2):
        count = refs[half].shape[0]
        refs[4 + half][:count] = refs[half][...]
        refs[4 + half][count:] = refs[2 + half][...]


def join(kept, came):
    shapes = [(2 * array.shape[0],) + array.shape[1:] for array in kept]
    return pl.pallas_call(
        join_kernel,
        grid=(1,),
        in_specs=[whole(array.shape) for array in (*kept, *came)],
        out_specs=[whole(shape) for shape in shapes],
        out_shape=[jax.ShapeDtypeStruct(shape, bf16) for shape in shapes],
        compiler_params=params(6),
        cost_estimate=cost(kept[0].size, 16 * kept[0].size),
        name="join",
    )(*kept, *came)


def copies(parts, scratch, sems, head, buffer, rows):
    if len(parts) == 1:
        count = parts[0].shape[0]
        return [
            pltpu.make_async_copy(
                parts[0].at[slot, head],
                scratch.at[buffer, pl.ds(slot * rows, rows), :],
                sems.at[buffer, slot],
            )
            for slot in range(count)
        ]
    return [
        pltpu.make_async_copy(
            part.at[head], scratch.at[buffer, pl.ds(slot * rows, rows), :], sems.at[buffer, slot]
        )
        for slot, part in enumerate(parts)
    ]


def bring_blocks(parts, scratch, sems, heads, rows):
    head = pl.program_id(0)
    buffer = lax.rem(head, 2)

    @pl.when(head == 0)
    def _():
        for copy in copies(parts, scratch, sems, 0, 0, rows):
            copy.start()

    @pl.when(head + 1 < heads)
    def _():
        for copy in copies(parts, scratch, sems, head + 1, 1 - buffer, rows):
            copy.start()

    for copy in copies(parts, scratch, sems, head, buffer, rows):
        copy.wait()
    return head, buffer


def listed_rows(place, starts, head, b, rows):
    own, before = place[3], place[4]
    if b == 0:
        near = [
            (pl.multiple_of(before + rows - WINDOW, WINDOW), WINDOW),
            (pl.multiple_of(own, WINDOW), WINDOW),
        ]
    else:
        near = [(pl.multiple_of(own + (b - 1) * QB, WINDOW), 2 * WINDOW)]
    far = [(pl.multiple_of(starts[head, b * SEL + s], KB), KB) for s in range(SEL)]
    return near + far


def load_rows(keys, buffer, where):
    return jnp.concatenate([keys[buffer, pl.ds(start, size), :] for start, size in where], axis=0)


def mask_kernel(place, chosen, near_ref, far_ref, out_ref, *, heads, blocks):
    rows = blocks * QB
    tok, boundary = place[1], place[2]
    wide = 2 * WINDOW
    line = lax.broadcasted_iota(jnp.int32, (QB, wide), 1)
    column = lax.broadcasted_iota(jnp.int32, (QB, wide), 0)
    band = (line > column) & (line <= column + WINDOW)
    diagonal = line == column + WINDOW
    in_second = lambda position: jnp.where(position >= boundary, 1, 0)
    lane = lax.broadcasted_iota(jnp.int32, (1, SEL * KB), 1)
    for b in range(blocks):
        first = tok * rows + b * QB
        query_seq = in_second(first + lax.broadcasted_iota(jnp.int32, (QB, 1), 0))
        key = first - WINDOW + lax.broadcasted_iota(jnp.int32, (1, wide), 1)
        near = band & (diagonal | (near_ref[b : b + 1, :] > 0.0))
        near = jnp.where(near & (in_second(key) == query_seq), 0.0, negative)
        for head in range(heads):
            usable = jnp.zeros((1, SEL * KB), f32)
            token = lane & (KB - 1)
            for s in range(SEL):
                block = chosen[head, b * SEL + s]
                here = (lane >= s * KB) & (lane < (s + 1) * KB)
                early = block * KB + KB <= first - WINDOW
                usable = jnp.where(here & early, far_ref[pl.ds(block, 1), :], usable)
                token = token + jnp.where(here, block * KB, 0)
            far = (usable > 0.0) & (in_second(token) == query_seq)
            at = pl.ds(b * QB, QB)
            out_ref[head, at, :wide] = near
            out_ref[head, at, wide:] = jnp.where(far, 0.0, negative)


def masks(place, chosen, near_valid, far_valid, heads, rows):
    listed = 2 * WINDOW + SEL * KB
    return pl.pallas_call(
        functools.partial(mask_kernel, heads=heads, blocks=rows // QB),
        grid_spec=pltpu.PrefetchScalarGridSpec(
            num_scalar_prefetch=2,
            grid=(1,),
            in_specs=[whole(near_valid.shape), whole(far_valid.shape)],
            out_specs=whole((heads, rows, listed)),
        ),
        out_shape=jax.ShapeDtypeStruct((heads, rows, listed), f32),
        compiler_params=params(6),
        cost_estimate=cost(20 * heads * rows * listed, 4 * heads * rows * listed),
        name="masks",
    )(place, chosen, near_valid, far_valid)


def attend_kernel(place, starts, *refs, heads, blocks, parts):
    q_ref, w_ref, mask_ref = refs[:3]
    kv_parts = refs[3 : 3 + parts]
    mixed_ref, probs_ref = refs[3 + parts : 5 + parts]
    outs = refs[5 + parts : 9 + parts]
    keys, gathered, work, sems = refs[9 + parts :]
    rows = blocks * QB
    head, buffer = bring_blocks(kv_parts, keys, sems, heads, rows)
    blocks_at = [pl.ds(b * QB, QB) for b in range(blocks)]
    where = [listed_rows(place, starts, head, b, rows) for b in range(blocks)]
    for b, at in enumerate(blocks_at):
        kv = load_rows(keys, buffer, where[b])
        scores = lax.dot_general(q_ref[0, at, :], kv, ON_LANES, preferred_element_type=f32)
        work[at, :] = scores + mask_ref[0, at, :]
    scores = work[...]
    weights = jnp.exp(scores - jnp.max(scores, axis=-1, keepdims=True))
    weights = weights * (1.0 / jnp.sum(weights, axis=-1, keepdims=True))
    probs_ref[0] = weights.astype(bf16)
    for b, at in enumerate(blocks_at):
        kv = load_rows(keys, buffer, where[b])
        out = jnp.dot(probs_ref[0, at, :], kv, preferred_element_type=f32).astype(bf16)
        mixed_ref[0, at, :] = out
        gathered[head, at, :] = out

    @pl.when(head == heads - 1)
    def _():
        size = rows // 4
        for k in range(4):
            at = piece_rows(place, STEPS[k], size)
            mixed = jnp.concatenate([gathered[h, at, :] for h in range(heads)], axis=1)
            outs[k][...] = jnp.dot(mixed, w_ref[...], preferred_element_type=f32).astype(bf16)


def attend(place, starts, queries, w_out, mask, parts, count):
    heads, rows, _ = queries.shape
    quarter = rows // 4
    listed = mask.shape[2]
    per_head = lambda columns: pl.BlockSpec((1, rows, columns), lambda h, *_: (h, 0, 0))
    slots = count if len(parts) == 1 else len(parts)
    return pl.pallas_call(
        functools.partial(attend_kernel, heads=heads, blocks=rows // QB, parts=len(parts)),
        grid_spec=pltpu.PrefetchScalarGridSpec(
            num_scalar_prefetch=2,
            grid=(heads,),
            in_specs=[per_head(WIDE), whole(w_out.shape), per_head(listed)]
            + [pl.BlockSpec(memory_space=pl.ANY)] * len(parts),
            out_specs=[per_head(WIDE), per_head(listed)] + [whole((quarter, D))] * 4,
            scratch_shapes=[
                pltpu.VMEM((2, slots * rows, WIDE), bf16),
                pltpu.VMEM((heads, rows, WIDE), bf16),
                pltpu.VMEM((rows, listed), f32),
                pltpu.SemaphoreType.DMA((2, slots)),
            ],
        ),
        out_shape=[
            jax.ShapeDtypeStruct((heads, rows, WIDE), bf16),
            jax.ShapeDtypeStruct((heads, rows, listed), bf16),
        ]
        + [jax.ShapeDtypeStruct((quarter, D), bf16)] * 4,
        compiler_params=params(30 if len(parts) == 1 else 12),
        cost_estimate=cost(
            2 * rows * heads * WIDE * (D + 512), 2 * heads * WIDE * rows * (slots + 4)
        ),
        name="attend",
    )(place, starts, queries, w_out, mask, *parts)


def attend_back_kernel(place, starts, *refs, heads, count, blocks, parts):
    q_ref, probs_ref, w_ref = refs[:3]
    pieces = refs[3:7]
    kv_parts = refs[7 : 7 + parts]
    dq_ref, grad_ref = refs[7 + parts : 9 + parts]
    outs = refs[9 + parts : 9 + 2 * parts]
    keys, sums, mixed_ref, work, scores_ref, grads_ref, sems = refs[9 + 2 * parts :]
    rows = blocks * QB
    size = rows // 4
    head, buffer = bring_blocks(kv_parts, keys, sems, heads, rows)

    @pl.when(head == 0)
    def _():
        for k in range(4):
            grad_ref[piece_rows(place, STEPS[k], size), :] = pieces[k][...]

    sums[...] = jnp.zeros_like(sums)
    mixed_ref[...] = lax.dot_general(
        grad_ref[...], w_ref[...], ON_LANES, preferred_element_type=f32
    ).astype(bf16)
    blocks_at = [pl.ds(b * QB, QB) for b in range(blocks)]
    where = [listed_rows(place, starts, head, b, rows) for b in range(blocks)]
    for b, at in enumerate(blocks_at):
        kv = load_rows(keys, buffer, where[b])
        work[at, :] = lax.dot_general(
            mixed_ref[at, :], kv, ON_LANES, preferred_element_type=f32
        )
    weights = probs_ref[0].astype(f32)
    grad_probs = work[...]
    inner = jnp.sum(weights * grad_probs, axis=-1, keepdims=True)
    scores_ref[...] = (weights * (grad_probs - inner)).astype(bf16)
    for b, at in enumerate(blocks_at):
        kv = load_rows(keys, buffer, where[b])
        grad_q = jnp.dot(scores_ref[at, :], kv, preferred_element_type=f32)
        dq_ref[0, at, :] = (grad_q.astype(bf16).astype(f32) * scale).astype(bf16)
    for b, at in enumerate(blocks_at):
        grads_ref[b] = lax.dot_general(
            jnp.concatenate([scores_ref[at, :], probs_ref[0, at, :]], axis=0),
            jnp.concatenate([q_ref[0, at, :], mixed_ref[at, :]], axis=0),
            ON_ROWS,
            preferred_element_type=f32,
        )
    for b in range(blocks):
        done = 0
        for start, length in where[b]:
            sums[pl.ds(start, length), :] += grads_ref[b, done : done + length, :]
            done += length
    if parts == 1:
        for slot in range(count):
            outs[0][slot, 0] = sums[pl.ds(slot * rows, rows), :].astype(bf16)
    else:
        for slot in range(parts):
            outs[slot][0] = sums[pl.ds(slot * rows, rows), :].astype(bf16)


def attend_back(place, starts, queries, probs, w_out, pieces, parts, count):
    heads, rows, _ = queries.shape
    quarter = rows // 4
    listed = probs.shape[2]
    per_head = lambda columns: pl.BlockSpec((1, rows, columns), lambda h, *_: (h, 0, 0))
    slots = count if len(parts) == 1 else len(parts)
    if len(parts) == 1:
        out_specs = [pl.BlockSpec((count, 1, rows, WIDE), lambda h, *_: (0, h, 0, 0))]
    else:
        out_specs = [per_head(WIDE)] * len(parts)
    return pl.pallas_call(
        functools.partial(
            attend_back_kernel, heads=heads, count=count, blocks=rows // QB, parts=len(parts)
        ),
        grid_spec=pltpu.PrefetchScalarGridSpec(
            num_scalar_prefetch=2,
            grid=(heads,),
            in_specs=[
                per_head(WIDE),
                per_head(listed),
                pl.BlockSpec((WIDE, D), lambda h, *_: (h, 0)),
            ]
            + [whole((quarter, D))] * 4
            + [pl.BlockSpec(memory_space=pl.ANY)] * len(parts),
            out_specs=[per_head(WIDE), whole((rows, D))] + out_specs,
            scratch_shapes=[
                pltpu.VMEM((2, slots * rows, WIDE), bf16),
                pltpu.VMEM((slots * rows, WIDE), f32),
                pltpu.VMEM((rows, WIDE), bf16),
                pltpu.VMEM((rows, listed), f32),
                pltpu.VMEM((rows, listed), bf16),
                pltpu.VMEM((rows // QB, listed, WIDE), f32),
                pltpu.SemaphoreType.DMA((2, slots)),
            ],
        ),
        out_shape=[
            jax.ShapeDtypeStruct((heads, rows, WIDE), bf16),
            jax.ShapeDtypeStruct((rows, D), bf16),
        ]
        + [jax.ShapeDtypeStruct(part.shape, bf16) for part in parts],
        compiler_params=params(62 if len(parts) == 1 else 16),
        cost_estimate=cost(
            2 * rows * heads * WIDE * (D + 1536), 4 * heads * WIDE * rows * (slots + 4)
        ),
        name="attend_back",
    )(place, starts, queries, probs, w_out, *pieces, *parts)


def project_back_kernel(place, *refs, heads, terms):
    dq_ref, w_ref = refs[:2]
    kv_refs = refs[2 : 2 + terms]
    dkv_ref, bias_ref = refs[2 + terms : 4 + terms]
    outs = refs[4 + terms :]
    rows = dq_ref.shape[1]
    size = rows // 4
    for h in range(heads):
        total = kv_refs[0][h].astype(f32)
        for term in kv_refs[1:]:
            total = total + term[h].astype(f32)
        low = total.astype(bf16)
        dkv_ref[h] = low
        bias_ref[h : h + 1, :] = jnp.sum(dq_ref[h].astype(f32), axis=0, keepdims=True)
        bias_ref[heads + h : heads + h + 1, :] = jnp.sum(low.astype(f32), axis=0, keepdims=True)
    for k in range(4):
        at = piece_rows(place, STEPS[k], size)
        grads = jnp.concatenate(
            [dq_ref[h, at, :] for h in range(heads)] + [dkv_ref[h, at, :] for h in range(heads)],
            axis=1,
        )
        outs[k][...] = jnp.dot(grads, w_ref[...], preferred_element_type=f32).astype(bf16)


def project_back(place, dq, w_all, kv_terms):
    heads, rows, _ = dq.shape
    quarter = rows // 4
    return pl.pallas_call(
        functools.partial(project_back_kernel, heads=heads, terms=len(kv_terms)),
        grid_spec=pltpu.PrefetchScalarGridSpec(
            num_scalar_prefetch=1,
            grid=(1,),
            in_specs=[whole(dq.shape), whole(w_all.shape)] + [whole(dq.shape)] * len(kv_terms),
            out_specs=[whole(dq.shape), whole((2 * heads, WIDE))] + [whole((quarter, D))] * 4,
        ),
        out_shape=[
            jax.ShapeDtypeStruct(dq.shape, bf16),
            jax.ShapeDtypeStruct((2 * heads, WIDE), f32),
        ]
        + [jax.ShapeDtypeStruct((quarter, D), bf16)] * 4,
        compiler_params=params(12),
        cost_estimate=cost(4 * rows * D * heads * WIDE, 4 * D * heads * WIDE + 12 * rows * D),
        name="project_back",
    )(place, dq, w_all, *kv_terms)


def feed_kernel(place, *refs):
    pieces = refs[:4]
    up_ref, bias_ref, down_ref, kept_ref, slope_ref = refs[4:9]
    outs = refs[9:]
    size = pieces[0].shape[0]
    root = 0.7978845608028654
    cubic = 0.044715
    for k in range(4):
        at = pl.ds(k * size, size)
        normed = pieces[k][...]
        kept_ref[0, at, :] = normed
        inner = jnp.dot(normed, up_ref[...], preferred_element_type=f32) + bias_ref[...]
        square = inner * inner
        bend = jnp.tanh(root * inner * (1.0 + cubic * square))
        half = 0.5 * (1.0 + bend)
        hidden = (inner * half).astype(bf16)
        kept_ref[1, at, :] = hidden
        slope = half + 0.5 * inner * (1.0 - bend * bend) * (root * (1.0 + 3.0 * cubic * square))
        slope_ref[at, :] = slope.astype(bf16)
        outs[k][...] = jnp.dot(hidden, down_ref[...], preferred_element_type=f32).astype(bf16)


def feed(place, pieces, w_up, b_up, w_down):
    quarter = pieces[0].shape[0]
    rows = 4 * quarter
    units = w_up.shape[1]
    return pl.pallas_call(
        feed_kernel,
        grid_spec=pltpu.PrefetchScalarGridSpec(
            num_scalar_prefetch=1,
            grid=(1,),
            in_specs=[whole((quarter, D))] * 4
            + [whole(w_up.shape), whole(b_up.shape), whole(w_down.shape)],
            out_specs=[whole((2, rows, D)), whole((rows, units))] + [whole((quarter, D))] * 4,
        ),
        out_shape=[
            jax.ShapeDtypeStruct((2, rows, D), bf16),
            jax.ShapeDtypeStruct((rows, units), bf16),
        ]
        + [jax.ShapeDtypeStruct((quarter, D), bf16)] * 4,
        compiler_params=params(14),
        cost_estimate=cost(4 * rows * D * units, 4 * D * units + 10 * rows * D, rows * units),
        name="feed",
    )(place, *pieces, w_up, b_up, w_down)


def feed_back_kernel(place, *refs):
    pieces = refs[:4]
    down_ref, up_ref, slope_ref, kept_ref, bias_ref = refs[4:9]
    outs = refs[9:]
    size = pieces[0].shape[0]
    transposed = (((1,), (1,)), ((), ()))
    total = None
    for k in range(4):
        at = pl.ds(k * size, size)
        grad = pieces[k][...]
        kept_ref[1, at, :] = grad
        hidden = lax.dot_general(grad, down_ref[...], transposed, preferred_element_type=f32)
        inner = (hidden * slope_ref[at, :].astype(f32)).astype(bf16)
        kept_ref[0, at, :] = inner
        part = jnp.sum(inner.astype(f32), axis=0, keepdims=True)
        total = part if total is None else total + part
        outs[k][...] = lax.dot_general(
            inner, up_ref[...], transposed, preferred_element_type=f32
        ).astype(bf16)
    bias_ref[...] = total


def feed_back(place, pieces, w_up, w_down, slope):
    rows, units = slope.shape
    quarter = rows // 4
    if len(pieces) == 1:
        arrays = tuple(pieces) * 4
        specs = [
            pl.BlockSpec((quarter, D), lambda i, place, step=step: (place[0] ^ step, 0))
            for step in STEPS
        ]
    else:
        arrays = tuple(pieces)
        specs = [whole((quarter, D))] * 4
    return pl.pallas_call(
        feed_back_kernel,
        grid_spec=pltpu.PrefetchScalarGridSpec(
            num_scalar_prefetch=1,
            grid=(1,),
            in_specs=specs + [whole(w_down.shape), whole(w_up.shape), whole(slope.shape)],
            out_specs=[whole((2, rows, D)), whole((1, units))] + [whole((quarter, D))] * 4,
        ),
        out_shape=[
            jax.ShapeDtypeStruct((2, rows, D), bf16),
            jax.ShapeDtypeStruct((1, units), f32),
        ]
        + [jax.ShapeDtypeStruct((quarter, D), bf16)] * 4,
        compiler_params=params(14),
        cost_estimate=cost(4 * rows * D * units, 4 * D * units + 10 * rows * D),
        name="feed_back",
    )(place, *arrays, w_down, w_up, slope)


def add_norm_kernel(place, *refs, bias_row, norm_row):
    a, b, c, residual, param, valid = refs[:6]
    out_ref, low_ref, normed_ref, squares_ref = refs[6:]
    branch = a[...].astype(f32) + b[...].astype(f32) + c[...].astype(f32) + row(param, bias_row)
    total = residual[...].astype(f32) + branch
    out_ref[...] = total
    low = total.astype(bf16)
    low_ref[...] = low
    if norm_row is not None:
        unit, _ = normalise(low.astype(f32))
        gain, shift = row(param, GAIN + norm_row), row(param, SHIFT + norm_row)
        normed_ref[...] = (unit * gain + shift).astype(bf16)
    else:
        normed_ref[...] = low
    weight = valid[...]
    squares_ref[0:1, :] = jnp.sum(weight * branch * branch, axis=0, keepdims=True)
    squares_ref[1:2, :] = jnp.sum(weight * total * total, axis=0, keepdims=True)


def own_quarter(quarter):
    return pl.BlockSpec((quarter, D), lambda i, place: (place[0], 0))


def add_norm(place, terms, residual, param, valid, rows, bias_row, norm_row):
    quarter = rows // 4
    spec = whole((quarter, D))
    return pl.pallas_call(
        functools.partial(add_norm_kernel, bias_row=bias_row, norm_row=norm_row),
        grid_spec=pltpu.PrefetchScalarGridSpec(
            num_scalar_prefetch=1,
            grid=(1,),
            in_specs=[spec] * 3
            + [
                spec,
                whole((PARAM_ROWS, D)),
                whole(valid.shape),
            ],
            out_specs=[spec, spec, spec, whole((2, D))],
        ),
        out_shape=[
            jax.ShapeDtypeStruct((quarter, D), f32),
            jax.ShapeDtypeStruct((quarter, D), bf16),
            jax.ShapeDtypeStruct((quarter, D), bf16),
            jax.ShapeDtypeStruct((2, D), f32),
        ],
        compiler_params=params(4),
        cost_estimate=cost(20 * quarter * D, 18 * quarter * D),
        name="add_norm",
    )(place, *terms, residual, param, valid)


def norm_back_kernel(place, *refs, norm_row):
    a, b, c, source, gradient, param = refs[:6]
    out_ref, low_ref, sums_ref = refs[6:]
    grad_normed = a[...].astype(f32) + b[...].astype(f32) + c[...].astype(f32)
    unit, inverse = normalise(source[...].astype(f32))
    grad_unit = grad_normed * row(param, GAIN + norm_row)
    first = jnp.mean(grad_unit, axis=-1, keepdims=True)
    second = jnp.mean(grad_unit * unit, axis=-1, keepdims=True)
    total = gradient[...].astype(f32) + inverse * (grad_unit - first - unit * second)
    out_ref[...] = total
    low = total.astype(bf16)
    low_ref[...] = low
    sums_ref[0:1, :] = jnp.sum(grad_normed * unit, axis=0, keepdims=True)
    sums_ref[1:2, :] = jnp.sum(grad_normed, axis=0, keepdims=True)
    sums_ref[2:3, :] = jnp.sum(low.astype(f32), axis=0, keepdims=True)


def norm_back(place, terms, source, gradient, param, rows, norm_row):
    quarter = rows // 4
    spec = whole((quarter, D))
    pick = lambda array: spec if array.shape[0] == quarter else own_quarter(quarter)
    return pl.pallas_call(
        functools.partial(norm_back_kernel, norm_row=norm_row),
        grid_spec=pltpu.PrefetchScalarGridSpec(
            num_scalar_prefetch=1,
            grid=(1,),
            in_specs=[spec] * 3 + [pick(source), pick(gradient), whole((PARAM_ROWS, D))],
            out_specs=[spec, spec, whole((3, D))],
        ),
        out_shape=[
            jax.ShapeDtypeStruct((quarter, D), f32),
            jax.ShapeDtypeStruct((quarter, D), bf16),
            jax.ShapeDtypeStruct((3, D), f32),
        ],
        compiler_params=params(4),
        cost_estimate=cost(20 * quarter * D, 18 * quarter * D),
        name="norm_back",
    )(place, *terms, source, gradient, param)


def piece_slot(place, piece, order):
    away = piece ^ place[5]
    bit = lambda i: (away >> order[i]) & 1
    return bit(0), 2 * bit(1) + bit(2)


def put_piece(place, keep_ref, give_ref, piece, order, value):
    sent, k = piece_slot(place, piece, order)

    @pl.when(sent == 0)
    def _():
        keep_ref[k] = value

    @pl.when(sent == 1)
    def _():
        give_ref[k] = value


def take_pieces(place, keep_ref, give_ref, staged, order):
    for piece in range(8):
        sent, k = piece_slot(place, piece, order)

        @pl.when(sent == 0)
        def _():
            staged[piece] = keep_ref[k]

        @pl.when(sent == 1)
        def _():
            staged[piece] = give_ref[k]


def feed_grads_kernel(place, left_ref, right_ref, *outs):
    half = D // 2
    low = half // 2
    for w in range(2):
        for i in range(2):
            for j in range(2):
                value = lax.dot_general(
                    left_ref[w, :, i * half : (i + 1) * half],
                    right_ref[w, :, j * half : (j + 1) * half],
                    ON_ROWS,
                    preferred_element_type=f32,
                ).astype(bf16)
                for part in range(2):
                    put_piece(
                        place,
                        outs[2 * w],
                        outs[2 * w + 1],
                        4 * i + 2 * j + part,
                        ORDERS[w],
                        value[part * low : (part + 1) * low],
                    )


def pieces_call(kernel, name, place, arrays, shape, flops):
    results = pl.pallas_call(
        kernel,
        grid_spec=pltpu.PrefetchScalarGridSpec(
            num_scalar_prefetch=1,
            grid=(1,),
            in_specs=[whole(array.shape) for array in arrays],
            out_specs=[whole((4,) + shape)] * 4,
        ),
        out_shape=[jax.ShapeDtypeStruct((4,) + shape, bf16)] * 4,
        compiler_params=params(14),
        cost_estimate=cost(flops, 2 * sum(array.size for array in arrays)),
        name=name,
    )(place, *arrays)
    return [results[:2], results[2:]]


def feed_grads(place, left, right):
    rows = left.shape[1]
    return pieces_call(
        feed_grads_kernel, "feed_grads", place, (left, right), (D // 4, D // 2), 4 * rows * D * D
    )


def mix_grads_kernel(place, normed_ref, dq_ref, dkv_ref, mixed_ref, grad_ref, *outs):
    heads = dq_ref.shape[0]
    half = D // 2
    low = heads * HD // 2
    for j in range(2):
        at = slice(j * half, (j + 1) * half)
        product = lambda left, right: [
            lax.dot_general(
                left[h], right[:, at], ON_ROWS, preferred_element_type=f32
            ).astype(bf16)
            for h in range(heads)
        ]
        join_heads = lambda parts, first: jnp.concatenate(
            [part[first : first + HD] for part in parts], axis=0
        )
        queries = product(dq_ref, normed_ref)
        pairs = product(dkv_ref, normed_ref)
        mixes = product(mixed_ref, grad_ref)
        values = (
            join_heads(queries, 0),
            join_heads(pairs, 0),
            join_heads(pairs, HD),
            join_heads(mixes, HD),
        )
        for g, value in enumerate(values):
            for part in range(2):
                put_piece(
                    place,
                    outs[2 * j],
                    outs[2 * j + 1],
                    2 * g + part,
                    ORDERS[j],
                    value[part * low : (part + 1) * low],
                )


def mix_grads(place, normed, dq, dkv, mixed, grad):
    heads, rows, _ = dq.shape
    return pieces_call(
        mix_grads_kernel,
        "mix_grads",
        place,
        (normed, dq, dkv, mixed, grad),
        (heads * HD // 2, D // 2),
        6 * rows * D * heads * WIDE,
    )


def feed_place_kernel(place, *refs):
    up_ref, down_ref, staged = refs[-3:]
    half = D // 2
    low = half // 2
    for w, out in enumerate((up_ref, down_ref)):
        take_pieces(place, refs[2 * w], refs[2 * w + 1], staged, ORDERS[w])
        for piece in range(8):
            i, j, part = piece // 4, (piece // 2) % 2, piece % 2
            top = i * half + part * low
            out[0, top : top + low, j * half : (j + 1) * half] = staged[piece].astype(f32)


def mix_place_kernel(place, *refs):
    qkv_ref, out_ref, staged = refs[-3:]
    half = D // 2
    low = staged.shape[1]
    for j in range(2):
        take_pieces(place, refs[2 * j], refs[2 * j + 1], staged, ORDERS[j])
        at = slice(j * half, (j + 1) * half)
        for piece in range(8):
            g, part = piece // 2, piece % 2
            rows = slice(part * low, (part + 1) * low)
            value = staged[piece].astype(f32)
            if g < 3:
                qkv_ref[0, g, rows, at] = value
            else:
                out_ref[0, rows, at] = value


def place_call(kernel, name, place, halves, earlier, shapes, layer):
    arrays = [array for half in halves for array in half]
    specs = [
        pl.BlockSpec((1,) + shape, lambda *_, rank=len(shape): (layer,) + (0,) * rank)
        for shape in shapes
    ]
    kept = [pl.BlockSpec(memory_space=pl.ANY)] * len(earlier)
    return pl.pallas_call(
        kernel,
        grid_spec=pltpu.PrefetchScalarGridSpec(
            num_scalar_prefetch=1,
            grid=(1,),
            in_specs=[whole(array.shape) for array in arrays] + kept,
            out_specs=specs,
            scratch_shapes=[pltpu.VMEM((8,) + arrays[0].shape[1:], bf16)],
        ),
        out_shape=[jax.ShapeDtypeStruct((LAYERS,) + shape, f32) for shape in shapes],
        input_output_aliases={5 + i: i for i in range(len(earlier))},
        compiler_params=params(18),
        cost_estimate=cost(4 * arrays[0].size, 24 * arrays[0].size),
        name=name,
    )(place, *arrays, *earlier)


def columns_kernel(place, *refs):
    pieces, out = refs[:4], refs[4]
    size = pieces[0].shape[0]
    width = out.shape[0]
    for p in range(4):

        @pl.when(place[0] == p)
        def _():
            for k in range(4):
                part = pieces[k][:, p * width : (p + 1) * width].astype(f32)
                q = p ^ STEPS[k]
                out[:, q * size : (q + 1) * size] = jnp.transpose(part).astype(bf16)


def columns(place, pieces):
    quarter = pieces[0].shape[0]
    return pl.pallas_call(
        columns_kernel,
        grid_spec=pltpu.PrefetchScalarGridSpec(
            num_scalar_prefetch=1,
            grid=(1,),
            in_specs=[whole((quarter, D))] * 4,
            out_specs=whole((D // 4, 4 * quarter)),
        ),
        out_shape=jax.ShapeDtypeStruct((D // 4, 4 * quarter), bf16),
        compiler_params=params(4),
        cost_estimate=cost(quarter * D, 16 * quarter * D),
        name="columns",
    )(place, *pieces)


def on_device(
    residual_in,
    cotangent,
    w_qkv,
    b_qv,
    w_out,
    b_out,
    w_up,
    b_up,
    w_down,
    b_down,
    ln_gain,
    ln_bias,
    selection,
    lengths,
    valid,
):
    rows = residual_in.shape[0]
    heads = selection.shape[0]
    blocks = rows // QB
    quarter = rows // 4
    count = lax.axis_size("tok")
    position = lax.axis_index("tok")
    member = lax.axis_index("head")
    width = D // 4
    first_row = position * rows
    chosen = lax.dynamic_slice_in_dim(selection, position * blocks, blocks, 1).reshape(heads, -1)
    per_device = rows // KB
    starts = slot_of(chosen // per_device, position, count) * rows + (chosen % per_device) * KB
    place = jnp.stack(
        [
            member,
            position,
            lengths[0],
            slot_of(position, position, count) * rows,
            slot_of(jnp.maximum(position - 1, 0), position, count) * rows,
            position if ring_form(count) else 0,
        ]
    ).astype(jnp.int32)

    first_pieces = share_quarters(residual_in.T)
    small = jnp.concatenate(
        [ln_gain.reshape(-1, width), ln_bias.reshape(-1, width), b_out, b_down], axis=0
    )
    small = jnp.pad(small, ((0, 128 - small.shape[0]), (0, 0)))
    param_pieces = share_quarters(small.T)

    split = jnp.transpose(w_qkv, (0, 2, 3, 1)).reshape(LAYERS, 3, heads, HD, D)
    w_all = jnp.concatenate(
        [
            jnp.pad(split[:, 0], ((0, 0), (0, 0), (0, WIDE - HD), (0, 0))),
            jnp.concatenate([split[:, 1], split[:, 2]], axis=2),
        ],
        axis=1,
    ).reshape(LAYERS, 2 * heads * WIDE, D)
    b_split = b_qv.reshape(LAYERS, 2, heads, HD)
    b_all = (
        jnp.concatenate(
            [
                jnp.pad(b_split[:, 0], ((0, 0), (0, 0), (0, HD))),
                jnp.pad(b_split[:, 1], ((0, 0), (0, 0), (HD, 0))),
            ],
            axis=1,
        )
        .reshape(LAYERS, 1, 2 * heads * WIDE)
        .astype(f32)
    )
    w_mix = jnp.pad(
        w_out.reshape(LAYERS, heads, HD, D), ((0, 0), (0, 0), (HD, 0), (0, 0))
    ).reshape(LAYERS, heads * WIDE, D)
    b_inner = b_up.astype(f32)

    far_valid = jnp.tile(valid.reshape(-1, KB), (1, SEL)).astype(f32)
    padded = jnp.concatenate([jnp.zeros((WINDOW,), jnp.int32), valid])
    near = lax.dynamic_slice_in_dim(padded, first_row, rows + WINDOW).reshape(-1, WINDOW)
    near_valid = jnp.concatenate([near[:-1], near[1:]], axis=1).astype(f32)
    own_valid = lax.dynamic_slice_in_dim(valid, first_row + member * quarter, quarter)
    own_valid = own_valid.astype(f32)[:, None]
    mask = masks(place, chosen, near_valid, far_valid, heads, rows)

    pieces = first_pieces
    lows = []
    kept = []
    squares = []
    for l in range(LAYERS):
        normed, queries, own_kv, *first = project(
            place, pieces, None if l else param_pieces, w_all[l], b_all[l], rows, heads
        )
        if l == 0:
            low_first, param = first
            residual = low_first
        parts = gather_blocks(own_kv)
        mixed, probs, *pieces = attend(place, starts, queries, w_mix[l], mask, parts, count)
        residual, low_second, normed_own, branch_squares = add_norm(
            place, sum_quarters(pieces), residual, param, own_valid, rows, B_OUT + l, 2 * l + 1
        )
        fed, slope, *pieces = feed(
            place, share_quarters(normed_own), w_up[l], b_inner[l : l + 1], w_down[l]
        )
        residual, low_next, normed_own, second_squares = add_norm(
            place,
            sum_quarters(pieces),
            residual,
            param,
            own_valid,
            rows,
            B_DOWN + l,
            2 * l + 2 if l + 1 < LAYERS else None,
        )
        squares.append((second_squares[1], branch_squares[0], second_squares[0]))
        kept.append((normed, queries, parts, mixed, probs, low_second, fed, slope))
        lows.append(low_next)
        if l + 1 < LAYERS:
            pieces = share_quarters(normed_own)
    residual_out = columns(place, share_quarters(lows[-1])).T

    gradient, sums_down = turn(place, share_quarters(cotangent.T))
    sums_down = sums_down[0]
    grad_pieces = (gradient,)
    grads = [None] * LAYERS
    placed_feed = placed_mix = ()
    shapes_feed = ((D, D), (D, D))
    shapes_mix = ((3, heads * HD, D), (heads * HD, D))
    mix_bundle = None
    feed_bundle = None
    nothing = lambda other: other
    for l in reversed(range(LAYERS)):
        normed, queries, parts, mixed, probs, low_second, fed, slope = kept[l]
        last_feed = feed_bundle.advance if feed_bundle else nothing
        last_mix = mix_bundle.advance if mix_bundle else nothing
        fed_back, grad_b_up, *pieces = feed_back(place, grad_pieces, w_up[l], w_down[l], slope)
        halves = feed_grads(place, fed, fed_back)
        terms, halves = lax.optimization_barrier((sum_quarters(pieces), halves))
        terms = last_feed(last_mix(terms))
        feed_bundle = Bundle(halves)
        gradient, low, second_sums = norm_back(
            place, terms, low_second, gradient, param, rows, 2 * l + 1
        )
        pieces = last_feed(last_mix(share_quarters(low)))
        if l + 1 < LAYERS:
            placed_feed = place_call(
                feed_place_kernel,
                "feed_place",
                place,
                old_feed.result,
                placed_feed,
                shapes_feed,
                l + 1,
            )
        dq, branch_full, *kv_grads = attend_back(
            place, starts, queries, probs, w_mix[l], pieces, parts, count
        )
        kv_grads = feed_bundle.advance(last_mix(kv_grads))
        kv_terms = return_blocks(
            kv_grads, lambda other: feed_bundle.advance(other)
        )
        kv_terms = feed_bundle.advance(last_mix(kv_terms))
        dkv, bias_sums, *pieces = project_back(place, dq, w_all[l], kv_terms)
        halves = mix_grads(place, normed, dq, dkv, mixed, branch_full)
        terms, halves = lax.optimization_barrier((sum_quarters(pieces), halves))
        terms = feed_bundle.advance(last_mix(terms))
        if l + 1 < LAYERS:
            placed_mix = place_call(
                mix_place_kernel, "mix_place", place, mix_bundle.result, placed_mix, shapes_mix, l + 1
            )
        mix_bundle = Bundle(halves)
        gradient, low, first_sums = norm_back(
            place, terms, lows[l - 1] if l else low_first, gradient, param, rows, 2 * l
        )
        pieces = share_quarters(low)
        if l:
            grad_pieces = mix_bundle.advance(pieces)
            old_feed = feed_bundle
        grads[l] = (
            None,
            grad_b_up[0],
            jnp.concatenate(
                [
                    bias_sums[:heads, :HD].reshape(-1),
                    bias_sums[heads:, HD:].reshape(-1),
                    jnp.zeros((D - 2 * heads * HD,), f32),
                ]
            ),
            jnp.stack([first_sums[0], second_sums[0]]),
            jnp.stack([first_sums[1], second_sums[1]]),
            second_sums[2],
            sums_down,
        )
        sums_down = first_sums[2]
    grad_residual = columns(place, pieces).T
    for bundle in (feed_bundle, mix_bundle):
        while bundle.ring and bundle.step < 6:
            bundle.advance(())
    placed_feed = place_call(
        feed_place_kernel, "feed_place", place, feed_bundle.result, placed_feed, shapes_feed, 0
    )
    placed_mix = place_call(
        mix_place_kernel, "mix_place", place, mix_bundle.result, placed_mix, shapes_mix, 0
    )

    over_all = jnp.concatenate(
        [grads[l][3] for l in range(LAYERS)]
        + [grads[l][4] for l in range(LAYERS)]
        + [jnp.stack([grads[l][5] for l in range(LAYERS)])]
        + [jnp.stack([grads[l][6] for l in range(LAYERS)])]
        + [jnp.stack([vector for layer in squares for vector in layer])],
        axis=0,
    )
    over_tok = jnp.stack(
        [grads[l][1] for l in range(LAYERS)] + [grads[l][2] for l in range(LAYERS)]
    )
    packed = small_sum(
        jnp.concatenate([small_sum(over_all, ("head",)), over_tok], axis=0), ("tok",)
    )
    stat_row = 4 * LAYERS + 2 * LAYERS
    tok_row = stat_row + 3 * LAYERS
    mine = lax.dynamic_slice_in_dim(packed[:stat_row], member * width, width, 1)
    grad_ln_gain = mine[: 2 * LAYERS].reshape(LAYERS, 2, width)
    grad_ln_bias = mine[2 * LAYERS : 4 * LAYERS].reshape(LAYERS, 2, width)
    grad_b_out = mine[4 * LAYERS : 5 * LAYERS]
    grad_b_down = mine[5 * LAYERS : 6 * LAYERS]
    square_sums = jnp.sum(packed[stat_row:tok_row], axis=-1).reshape(LAYERS, 3)
    valid_count = jnp.maximum(jnp.sum(valid.astype(f32)), 1.0)
    statistics = jnp.sqrt(square_sums / (valid_count * D))
    grad_b_up = packed[tok_row : tok_row + LAYERS]
    grad_b_qv = packed[tok_row + LAYERS :, : 2 * heads * HD].reshape(LAYERS, 2, heads * HD)
    return (
        residual_out,
        grad_residual,
        jnp.transpose(placed_mix[0], (0, 3, 1, 2)),
        grad_b_qv,
        placed_mix[1],
        grad_b_out,
        placed_feed[0],
        grad_b_up,
        placed_feed[1],
        grad_b_down,
        grad_ln_gain,
        grad_ln_bias,
        statistics,
    )


def solution(mesh):
    in_specs = (
        P("tok", "head"),
        P("tok", "head"),
        P(None, None, None, "head"),
        P(None, None, "head"),
        P(None, "head", None),
        P(None, "head"),
        P(None, None, "head"),
        P(None, "head"),
        P(None, "head", None),
        P(None, "head"),
        P(None, None, "head"),
        P(None, None, "head"),
        P("head", None, None),
        P(),
        P(),
    )
    out_specs = (
        P("tok", "head"),
        P("tok", "head"),
        P(None, None, None, "head"),
        P(None, None, "head"),
        P(None, "head", None),
        P(None, "head"),
        P(None, None, "head"),
        P(None, "head"),
        P(None, "head", None),
        P(None, "head"),
        P(None, None, "head"),
        P(None, None, "head"),
        P(),
    )
    return jax.shard_map(
        on_device, mesh=mesh, in_specs=in_specs, out_specs=out_specs, check_vma=False
    )
```

time: 692 us -> 560 us (0.81)
  local copies, waits for them, and re-layouts: 126 us -> 46.6 us
  other arithmetic: 67.2 us -> 7.2 us
  waiting for transfers between devices: 213 us -> 273 us
  blocking collectives: 21.6 us -> 0 us
  matrix products: 12.2 us -> 0 us
  starting transfers between devices: 127 us -> 117 us
    ppermute x93 -> x126, waiting for transfers between devices: 175 us -> 243 us  [swap(): lax.ppermute(value, axis, [(i, i ^ step) for i in range(lax.axis_size(axi...]
    another operation x12 -> x2, local copies, waits for them, and re-layouts: 26 us -> 0.12 us  [the longest x1 0.12 us: on_device(): jnp.stack([member, position, lengths[0], slot_of(position, position, coun...]
    ppermute x12, starting transfers between devices: 34.8 us -> 9.71 us  [rotate(): lax.ppermute(value, axis, [(i, (i + step) % count) for i in range(count)])]
    another operation x9 -> x0, other arithmetic: 24 us -> none  [the longest x6 14.1 us: on_device(): jnp.stack([grads[l][0][m] for l in range(LAYERS)])]
    all_gather x2 -> x0, blocking collectives: 21.6 us -> none  [the longest x1 11.1 us: on_device(): lax.all_gather(jnp.concatenate([residual_in, small], axis=0), 'head', axi...]
    unnamed x350 -> x173, local copies, waits for them, and re-layouts: 48.6 us -> 27.8 us
    pallas_call x2 -> x32, Pallas kernels: 27.7 us -> 48.3 us  [the longest x2 15.2 us: attend(): pl.pallas_call(functools.partial(attend_kernel, heads=heads, blocks=rows...]
    pallas_call x2, Pallas kernels: 38.5 us -> 18.6 us  [attend_back(): pl.pallas_call(functools.partial(attend_back_kernel, heads=heads, count=c...]
  transfers between devices with their start and end apart: 105 -> 138, of which waited for: 51 -> 66; matrix products, arithmetic and copies ran while one was open for 20% -> 5% of each run, Pallas kernels for 9% -> 11%
where the time goes in v2:
time: 560 us; the launch traced here: 551 us
  waiting for transfers between devices  273 us (49%)
  starting transfers between devices  117 us (21%)
  Pallas kernels  105 us (19%)
  local copies, waits for them, and re-layouts  46.6 us (8%)
  other arithmetic  7.2 us (1%)
    ppermute x126, waiting for transfers between devices, swap(): lax.ppermute(value, axis, [(i, i ^ step) for i in range(lax.axis_size(axi...  243 us
    ppermute x126, starting transfers between devices, swap(): lax.ppermute(value, axis, [(i, i ^ step) for i in range(lax.axis_size(axi...  107 us
    ppermute x12, waiting for transfers between devices, rotate(): lax.ppermute(value, axis, [(i, (i + step) % count) for i in range(count)])  29.9 us
    unnamed x173, local copies, waits for them, and re-layouts  27.8 us
    pallas_call x2, Pallas kernels, attend_back(): pl.pallas_call(functools.partial(attend_back_kernel, heads=heads, count=c...  18.6 us
    pallas_call x2, Pallas kernels, attend(): pl.pallas_call(functools.partial(attend_kernel, heads=heads, blocks=rows...  15.2 us
    pallas_call x4, Pallas kernels, pieces_call(): pl.pallas_call(kernel, grid_spec=pltpu.PrefetchScalarGridSpec(num_scalar_...  14.6 us
    pallas_call x4, Pallas kernels, place_call(): pl.pallas_call(kernel, grid_spec=pltpu.PrefetchScalarGridSpec(num_scalar_...  11.3 us
  transfers between devices with their start and end apart: 138, of which 66 were waited for; matrix products, arithmetic and copies ran while one was open for 5% of the time, Pallas kernels for 11%

profile of v2, /device:TPU:0, one launch (start us, length us, event | category | flops | bytes accessed | tf_op | source)
XLA Modules:
  0.0 550.7 jit_solution(1435250778530653064)
XLA Ops:
  20.3 7.5 %collective-permute-done.6.refs_4_.refs_8_ = bf16[3,512,128]{2,1,0:T(8,128)(2,1)S(1)} collective-permute-done((bf16[3,512,128]{2,1,0:T(8,128)(2,1)S(1)}, bf16[3,512,128]{2,1,0:T(8,128)(2,1)S(1)}, u32[]{:S(2)}, u32[]{:S(2)}) %collective-permute-start.6) | collective-permute-done | bytes 393248 | tf_op jit(solution)/shard_map/ppermute | solution.py:38
  31.5 9.8 %collective-permute-done.8.refs_6_.refs_10_ = bf16[3,512,128]{2,1,0:T(8,128)(2,1)S(1)} collective-permute-done((bf16[3,512,128]{2,1,0:T(8,128)(2,1)S(1)}, bf16[3,512,128]{2,1,0:T(8,128)(2,1)S(1)}, u32[]{:S(2)}, u32[]{:S(2)}) %collective-permute-start.8) | collective-permute-done | bytes 393248 | tf_op jit(solution)/shard_map/ppermute | solution.py:38
  45.4 7.5 %collective-permute-done.10.refs_8_.refs_12_ = bf16[3,512,128]{2,1,0:T(8,128)(2,1)} collective-permute-done((bf16[3,512,128]{2,1,0:T(8,128)(2,1)}, bf16[3,512,128]{2,1,0:T(8,128)(2,1)}, u32[]{:S(2)}, u32[]{:S(2)}) %collective-permute-start.10) | collective-permute-done | bytes 393248 | tf_op jit(solution)/shard_map/ppermute | solution.py:38
  59.1 5.1 collective-permute-done.12.refs_10_.refs_14_
  66.2 7.2 %attend.2 = (bf16[3,512,128]{2,1,0:T(8,128)(2,1)S(1)}, bf16[3,512,192]{2,1,0:T(8,128)(2,1)S(1)}, bf16[128,768]{1,0:T(8,128)(2,1)S(1)}, bf16[128,768]{1,0:T(8,128...) custom-call(s32[6]{0:T(128)S(1)} %stack.23.place, s32[3,32]{1,0:T(4,128)S(1)} %fusion.7.starts, ...), custom_call_target="tpu_custom_call" | custom-call | flops 503316480 | bytes 4718592 | tf_op jit(solution)/shard_map/attend/pallas_call | solution.py:471
  79.6 5.0 collective-permute-done.15.refs_2_
  101.0 5.5 %collective-permute-done.21.refs_2_ = bf16[128,768]{1,0:T(8,128)(2,1)S(1)} collective-permute-done((bf16[128,768]{1,0:T(8,128)(2,1)S(1)}, bf16[128,768]{1,0:T(8,128)(2,1)S(1)}, u32[]{:S(2)}, u32[]{:S(2)}) %collective-permute-start.21) | collective-permute-done | bytes 196640 | tf_op jit(solution)/shard_map/ppermute | solution.py:38
  109.0 4.7 collective-permute-done.22.refs_1_
  117.9 10.7 %collective-permute-done.25.refs_4_.refs_8_ = bf16[3,512,128]{2,1,0:T(8,128)(2,1)S(1)} collective-permute-done((bf16[3,512,128]{2,1,0:T(8,128)(2,1)S(1)}, bf16[3,512,128]{2,1,0:T(8,128)(2,1)S(1)}, u32[]{:S(2)}, u32[]{:S(2)}) %collective-permute-start.25) | collective-permute-done | bytes 393248 | tf_op jit(solution)/shard_map/ppermute | solution.py:38
  132.1 8.5 %collective-permute-done.27.refs_6_.refs_10_ = bf16[3,512,128]{2,1,0:T(8,128)(2,1)S(1)} collective-permute-done((bf16[3,512,128]{2,1,0:T(8,128)(2,1)S(1)}, bf16[3,512,128]{2,1,0:T(8,128)(2,1)S(1)}, u32[]{:S(2)}, u32[]{:S(2)}) %collective-permute-start.27) | collective-permute-done | bytes 393248 | tf_op jit(solution)/shard_map/ppermute | solution.py:38
  144.6 7.9 %collective-permute-done.29.refs_8_.refs_12_ = bf16[3,512,128]{2,1,0:T(8,128)(2,1)S(1)} collective-permute-done((bf16[3,512,128]{2,1,0:T(8,128)(2,1)S(1)}, bf16[3,512,128]{2,1,0:T(8,128)(2,1)S(1)}, u32[]{:S(2)}, u32[]{:S(2)}) %collective-permute-start.29) | collective-permute-done | bytes 393248 | tf_op jit(solution)/shard_map/ppermute | solution.py:38
  156.4 6.2 %collective-permute-done.31.refs_10_.refs_14_ = bf16[3,512,128]{2,1,0:T(8,128)(2,1)S(1)} collective-permute-done((bf16[3,512,128]{2,1,0:T(8,128)(2,1)S(1)}, bf16[3,512,128]{2,1,0:T(8,128)(2,1)S(1)}, u32[]{:S(2)}, u32[]{:S(2)}) %collective-permute-start.31) | collective-permute-done | bytes 393248 | tf_op jit(solution)/shard_map/ppermute | solution.py:38
  162.7 8.0 %attend.3 = (bf16[3,512,128]{2,1,0:T(8,128)(2,1)S(1)}, bf16[3,512,192]{2,1,0:T(8,128)(2,1)S(1)}, bf16[128,768]{1,0:T(8,128)(2,1)S(1)}, bf16[128,768]{1,0:T(8,128...) custom-call(s32[6]{0:T(128)S(1)} %stack.23.place, s32[3,32]{1,0:T(4,128)S(1)} %fusion.7.starts, ...), custom_call_target="tpu_custom_call" | custom-call | flops 503316480 | bytes 4718592 | tf_op jit(solution)/shard_map/attend/pallas_call | solution.py:471
  174.4 5.7 %collective-permute-done.34.refs_2_ = bf16[128,768]{1,0:T(8,128)(2,1)S(1)} collective-permute-done((bf16[128,768]{1,0:T(8,128)(2,1)S(1)}, bf16[128,768]{1,0:T(8,128)(2,1)S(1)}, u32[]{:S(2)}, u32[]{:S(2)}) %collective-permute-start.34) | collective-permute-done | bytes 196640 | tf_op jit(solution)/shard_map/ppermute | solution.py:38
  198.5 4.2 feed_grads.2
  208.2 4.6 collective-permute-done.50.refs_4_
  214.3 10.2 %attend_back.2 = (bf16[3,512,128]{2,1,0:T(8,128)(2,1)S(1)}, bf16[512,768]{1,0:T(8,128)(2,1)S(1)}, bf16[3,512,128]{2,1,0:T(8,128)(2,1)S(1)}, bf16[3,512,128]{2,1,...) custom-call(s32[6]{0:T(128)S(1)} %stack.23.place, ...), custom_call_target="tpu_custom_call" | custom-call | flops 905969664 | bytes 9437184 | tf_op jit(solution)/shard_map/attend_back/pallas_call | solution.py:564
  226.6 9.9 %collective-permute-done.58 = bf16[3,512,128]{2,1,0:T(8,128)(2,1)S(1)} collective-permute-done((bf16[3,512,128]{2,1,0:T(8,128)(2,1)S(1)}, bf16[3,512,128]{2,1,0:T(8,128)(2,1)S(1)}, u32[]{:S(2)}, u32[]{:S(2)}) %collective-permute-start.58) | collective-permute-done | bytes 393248 | tf_op jit(solution)/shard_map/ppermute | solution.py:38
  236.7 7.4 %collective-permute-done.57 = bf16[3,512,128]{2,1,0:T(8,128)(2,1)S(1)} collective-permute-done((bf16[3,512,128]{2,1,0:T(8,128)(2,1)S(1)}, bf16[3,512,128]{2,1,0:T(8,128)(2,1)S(1)}, u32[]{:S(2)}, u32[]{:S(2)}) %collective-permute-start.57) | collective-permute-done | bytes 393248 | tf_op jit(solution)/shard_map/ppermute | solution.py:38
  252.0 15.1 %collective-permute-done.55.refs_1_ = bf16[2,192,384]{2,1,0:T(8,128)(2,1)S(1)} collective-permute-done((bf16[2,192,384]{2,1,0:T(8,128)(2,1)S(1)}, bf16[2,192,384]{2,1,0:T(8,128)(2,1)S(1)}, u32[]{:S(2)}, u32[]{:S(2)}) %collective-permute-start.55) | collective-permute-done | bytes 294944 | tf_op jit(solution)/shard_map/ppermute | solution.py:38
  272.8 11.0 %collective-permute-done.61.refs_1_ = bf16[1,192,384]{2,1,0:T(8,128)(2,1)S(1)} collective-permute-done((bf16[1,192,384]{2,1,0:T(8,128)(2,1)S(1)}, bf16[1,192,384]{2,1,0:T(8,128)(2,1)S(1)}, u32[]{:S(2)}, u32[]{:S(2)}) %collective-permute-start.61) | collective-permute-done | bytes 147488 | tf_op jit(solution)/shard_map/ppermute | solution.py:38
  320.2 4.3 feed_grads.3
  325.0 9.4 %collective-permute-done.81.refs_1_ = bf16[2,96,384]{2,1,0:T(8,128)(2,1)S(1)} collective-permute-done((bf16[2,96,384]{2,1,0:T(8,128)(2,1)S(1)}, bf16[2,96,384]{2,1,0:T(8,128)(2,1)S(1)}, u32[]{:S(2)}, u32[]{:S(2)}) %collective-permute-start.81) | collective-permute-done | bytes 147488 | tf_op jit(solution)/shard_map/ppermute | solution.py:38
  345.9 7.7 %collective-permute-done.83.refs_1_ = bf16[1,96,384]{2,1,0:T(8,128)(2,1)S(1)} collective-permute-done((bf16[1,96,384]{2,1,0:T(8,128)(2,1)S(1)}, bf16[1,96,384]{2,1,0:T(8,128)(2,1)S(1)}, u32[]{:S(2)}, u32[]{:S(2)}) %collective-permute-start.83) | collective-permute-done | bytes 73760 | tf_op jit(solution)/shard_map/ppermute | solution.py:38
  364.7 8.4 %attend_back.3 = (bf16[3,512,128]{2,1,0:T(8,128)(2,1)S(1)}, bf16[512,768]{1,0:T(8,128)(2,1)S(1)}, bf16[3,512,128]{2,1,0:T(8,128)(2,1)S(1)}, bf16[3,512,128]{2,1,...) custom-call(s32[6]{0:T(128)S(1)} %stack.23.place, ...), custom_call_target="tpu_custom_call" | custom-call | flops 905969664 | bytes 9437184 | tf_op jit(solution)/shard_map/attend_back/pallas_call | solution.py:564
  375.3 9.9 %collective-permute-done.97 = bf16[3,512,128]{2,1,0:T(8,128)(2,1)S(1)} collective-permute-done((bf16[3,512,128]{2,1,0:T(8,128)(2,1)S(1)}, bf16[3,512,128]{2,1,0:T(8,128)(2,1)S(1)}, u32[]{:S(2)}, u32[]{:S(2)}) %collective-permute-start.97) | collective-permute-done | bytes 393248 | tf_op jit(solution)/shard_map/ppermute | solution.py:38
  394.1 7.9 %collective-permute-done.98 = bf16[3,512,128]{2,1,0:T(8,128)(2,1)S(1)} collective-permute-done((bf16[3,512,128]{2,1,0:T(8,128)(2,1)S(1)}, bf16[3,512,128]{2,1,0:T(8,128)(2,1)S(1)}, u32[]{:S(2)}, u32[]{:S(2)}) %collective-permute-start.98) | collective-permute-done | bytes 393248 | tf_op jit(solution)/shard_map/ppermute | solution.py:43
  405.4 3.9 collective-permute-done.40.refs_2_
  413.8 4.1 collective-permute-done.99
  424.7 11.8 %collective-permute-done.103.refs_3_ = bf16[2,96,384]{2,1,0:T(8,128)(2,1)S(1)} collective-permute-done((bf16[2,96,384]{2,1,0:T(8,128)(2,1)S(1)}, bf16[2,96,384]{2,1,0:T(8,128)(2,1)S(1)}, u32[]{:S(2)}, u32[]{:S(2)}) %collective-permute-start.103) | collective-permute-done | bytes 147488 | tf_op jit(solution)/shard_map/ppermute | solution.py:38
  479.6 5.6 %collective-permute-done.119.refs_1_ = bf16[2,96,384]{2,1,0:T(8,128)(2,1)S(1)} collective-permute-done((bf16[2,96,384]{2,1,0:T(8,128)(2,1)}, bf16[2,96,384]{2,1,0:T(8,128)(2,1)S(1)}, u32[]{:S(2)}, u32[]{:S(2)}) %collective-permute-start.119) | collective-permute-done | bytes 147488 | tf_op jit(solution)/shard_map/ppermute | solution.py:38
  496.9 4.6 collective-permute-done.132
  (551 shorter events, 307.9 us)
Async XLA Ops:
  204.2 20.3 %collective-permute-start.53 = (bf16[4,192,384]{2,1,0:T(8,128)(2,1)S(1)}, bf16[4,192,384]{2,1,0:T(8,128)(2,1)S(1)}, u32[]{:S(2)}, u32[]{:S(2)}) collective-permute-start(bf16[4,192,384]{2,1,0:T(8,128)(2,1)S(1)} %get-tuple-element.419), channel_id=1, source_target_pairs={{0,1},{1,0},{2,3},{3,2},{4,5},{5,4},{6,7},{7,6},{8,9},{9,8},{10,11... | collective-permute-start | bytes 1769480 | tf_op jit(solution)/shard_map/ppermute | solution.py:38
  205.7 18.7 %collective-permute-start.54 = (bf16[4,192,384]{2,1,0:T(8,128)(2,1)S(1)}, bf16[4,192,384]{2,1,0:T(8,128)(2,1)S(1)}, u32[]{:S(2)}, u32[]{:S(2)}) collective-permute-start(bf16[4,192,384]{2,1,0:T(8,128)(2,1)S(1)} %get-tuple-element.420), channel_id=1, source_target_pairs={{0,2},{1,3},{2,0},{3,1},{4,6},{5,7},{6,4},{7,5},{8,10},{9,11},{10,... | collective-permute-start | bytes 1769480 | tf_op jit(solution)/shard_map/ppermute | solution.py:38
  225.0 19.1 %collective-permute-start.57 = (bf16[3,512,128]{2,1,0:T(8,128)(2,1)S(1)}, bf16[3,512,128]{2,1,0:T(8,128)(2,1)S(1)}, u32[]{:S(2)}, u32[]{:S(2)}) collective-permute-start(bf16[3,512,128]{2,1,0:T(8,128)(2,1)S(1)} %get-tuple-element.436), channel_id=1, source_target_pairs={{0,1},{1,0},{2,3},{3,2},{4,5},{5,4},{6,7},{7,6},{8,9},{9,8},{10,11... | collective-permute-start | bytes 1179656 | tf_op jit(solution)/shard_map/ppermute | solution.py:38
  246.3 22.5 %collective-permute-start.60 = (bf16[3,512,128]{2,1,0:T(8,128)(2,1)S(1)}, bf16[3,512,128]{2,1,0:T(8,128)(2,1)S(1)}, u32[]{:S(2)}, u32[]{:S(2)}) collective-permute-start(bf16[3,512,128]{2,1,0:T(8,128)(2,1)S(1)} %add_convert_fusion.4), channel_id=1, source_target_pairs={{0,6},{1,7},{2,0},{3,1},{4,2},{5,3},{6,4},{7,5},{8,14},{9,15},{10,... | collective-permute-start | bytes 1179656 | tf_op jit(solution)/shard_map/ppermute | solution.py:43
  248.5 20.4 %collective-permute-start.64 = (bf16[3,512,128]{2,1,0:T(8,128)(2,1)S(1)}, bf16[3,512,128]{2,1,0:T(8,128)(2,1)S(1)}, u32[]{:S(2)}, u32[]{:S(2)}) collective-permute-start(bf16[3,512,128]{2,1,0:T(8,128)(2,1)S(1)} %get-tuple-element.447), channel_id=1, source_target_pairs={{0,1},{1,0},{2,3},{3,2},{4,5},{5,4},{6,7},{7,6},{8,9},{9,8},{10,11... | collective-permute-start | bytes 1179656 | tf_op jit(solution)/shard_map/ppermute | solution.py:38
  249.3 17.9 %collective-permute-start.55 = (bf16[2,192,384]{2,1,0:T(8,128)(2,1)S(1)}, bf16[2,192,384]{2,1,0:T(8,128)(2,1)S(1)}, u32[]{:S(2)}, u32[]{:S(2)}) collective-permute-start(bf16[2,192,384]{2,1,0:T(8,128)(2,1)S(1)} %get-tuple-element.433), channel_id=1, source_target_pairs={{0,2},{1,3},{2,0},{3,1},{4,6},{5,7},{6,4},{7,5},{8,10},{9,11},{10,... | collective-permute-start | bytes 884744 | tf_op jit(solution)/shard_map/ppermute | solution.py:38
  249.4 19.5 %collective-permute-start.56 = (bf16[2,192,384]{2,1,0:T(8,128)(2,1)S(1)}, bf16[2,192,384]{2,1,0:T(8,128)(2,1)S(1)}, u32[]{:S(2)}, u32[]{:S(2)}) collective-permute-start(bf16[2,192,384]{2,1,0:T(8,128)(2,1)S(1)} %get-tuple-element.434), channel_id=1, source_target_pairs={{0,4},{1,5},{2,6},{3,7},{4,0},{5,1},{6,2},{7,3},{8,12},{9,13},{10,... | collective-permute-start | bytes 884744 | tf_op jit(solution)/shard_map/ppermute | solution.py:38
  250.5 22.3 %collective-permute-start.63 = (bf16[3,512,128]{2,1,0:T(8,128)(2,1)S(1)}, bf16[3,512,128]{2,1,0:T(8,128)(2,1)S(1)}, u32[]{:S(2)}, u32[]{:S(2)}) collective-permute-start(bf16[3,512,128]{2,1,0:T(8,128)(2,1)S(1)} %get-tuple-element.445), channel_id=1, source_target_pairs={{0,1},{1,0},{2,3},{3,2},{4,5},{5,4},{6,7},{7,6},{8,9},{9,8},{10,11... | collective-permute-start | bytes 1179656 | tf_op jit(solution)/shard_map/ppermute | solution.py:38
  313.1 24.1 %collective-permute-start.85 = (bf16[2,192,384]{2,1,0:T(8,128)(2,1)S(1)}, bf16[2,192,384]{2,1,0:T(8,128)(2,1)S(1)}, u32[]{:S(2)}, u32[]{:S(2)}) collective-permute-start(bf16[2,192,384]{2,1,0:T(8,128)(2,1)S(1)} %get-tuple-element.517.refs_0_), channel_id=1, source_target_pairs={{0,2},{1,3},{2,0},{3,1},{4,6},{5,7},{6,4},{7,5},{8,10},{9,11},{10,... | collective-permute-start | bytes 884744 | tf_op jit(solution)/shard_map/ppermute | solution.py:38
  314.5 22.8 %collective-permute-start.86 = (bf16[2,192,384]{2,1,0:T(8,128)(2,1)S(1)}, bf16[2,192,384]{2,1,0:T(8,128)(2,1)S(1)}, u32[]{:S(2)}, u32[]{:S(2)}) collective-permute-start(bf16[2,192,384]{2,1,0:T(8,128)(2,1)S(1)} %get-tuple-element.518.refs_1_), channel_id=1, source_target_pairs={{0,4},{1,5},{2,6},{3,7},{4,0},{5,1},{6,2},{7,3},{8,12},{9,13},{10,... | collective-permute-start | bytes 884744 | tf_op jit(solution)/shard_map/ppermute | solution.py:38
  319.5 17.7 %collective-permute-start.82 = (bf16[2,96,384]{2,1,0:T(8,128)(2,1)S(1)}, bf16[2,96,384]{2,1,0:T(8,128)(2,1)S(1)}, u32[]{:S(2)}, u32[]{:S(2)}) collective-permute-start(bf16[2,96,384]{2,1,0:T(8,128)(2,1)S(1)} %get-tuple-element.505), channel_id=1, source_target_pairs={{0,4},{1,5},{2,6},{3,7},{4,0},{5,1},{6,2},{7,3},{8,12},{9,13},{10,... | collective-permute-start | bytes 442376 | tf_op jit(solution)/shard_map/ppermute | solution.py:38
  338.3 20.3 %collective-permute-start.87 = (bf16[128,768]{1,0:T(8,128)(2,1)S(1)}, bf16[128,768]{1,0:T(8,128)(2,1)S(1)}, u32[]{:S(2)}, u32[]{:S(2)}) collective-permute-start(bf16[128,768]{1,0:T(8,128)(2,1)S(1)} %get-tuple-element.542.refs_3_), channel_id=1, source_target_pairs={{0,16},{8,24},{16,0},{24,8},{1,17},{9,25},{17,1},{25,9},{2,18},{10... | collective-permute-start | bytes 589832 | tf_op jit(solution)/shard_map/ppermute | solution.py:38
  339.8 23.2 %collective-permute-start.92 = (bf16[4,192,384]{2,1,0:T(8,128)(2,1)S(1)}, bf16[4,192,384]{2,1,0:T(8,128)(2,1)S(1)}, u32[]{:S(2)}, u32[]{:S(2)}) collective-permute-start(bf16[4,192,384]{2,1,0:T(8,128)(2,1)S(1)} %get-tuple-element.536.refs_0_), channel_id=1, source_target_pairs={{0,1},{1,0},{2,3},{3,2},{4,5},{5,4},{6,7},{7,6},{8,9},{9,8},{10,11... | collective-permute-start | bytes 1769480 | tf_op jit(solution)/shard_map/ppermute | solution.py:38
  340.2 23.7 %collective-permute-start.93 = (bf16[4,192,384]{2,1,0:T(8,128)(2,1)S(1)}, bf16[4,192,384]{2,1,0:T(8,128)(2,1)S(1)}, u32[]{:S(2)}, u32[]{:S(2)}) collective-permute-start(bf16[4,192,384]{2,1,0:T(8,128)(2,1)S(1)} %get-tuple-element.537.refs_2_), channel_id=1, source_target_pairs={{0,2},{1,3},{2,0},{3,1},{4,6},{5,7},{6,4},{7,5},{8,10},{9,11},{10,... | collective-permute-start | bytes 1769480 | tf_op jit(solution)/shard_map/ppermute | solution.py:38
  353.6 19.6 %collective-permute-start.79 = (bf16[4,192,384]{2,1,0:T(8,128)(2,1)S(1)}, bf16[4,192,384]{2,1,0:T(8,128)(2,1)S(1)}, u32[]{:S(2)}, u32[]{:S(2)}) collective-permute-start(bf16[4,192,384]{2,1,0:T(8,128)(2,1)S(1)} %get-tuple-element.497), channel_id=1, source_target_pairs={{0,1},{1,0},{2,3},{3,2},{4,5},{5,4},{6,7},{7,6},{8,9},{9,8},{10,11... | collective-permute-start | bytes 1769480 | tf_op jit(solution)/shard_map/ppermute | solution.py:38
  355.3 17.9 %collective-permute-start.80 = (bf16[4,192,384]{2,1,0:T(8,128)(2,1)S(1)}, bf16[4,192,384]{2,1,0:T(8,128)(2,1)S(1)}, u32[]{:S(2)}, u32[]{:S(2)}) collective-permute-start(bf16[4,192,384]{2,1,0:T(8,128)(2,1)S(1)} %get-tuple-element.498), channel_id=1, source_target_pairs={{0,2},{1,3},{2,0},{3,1},{4,6},{5,7},{6,4},{7,5},{8,10},{9,11},{10,... | collective-permute-start | bytes 1769480 | tf_op jit(solution)/shard_map/ppermute | solution.py:38
  375.3 17.3 %collective-permute-start.96 = (bf16[3,512,128]{2,1,0:T(8,128)(2,1)S(1)}, bf16[3,512,128]{2,1,0:T(8,128)(2,1)S(1)}, u32[]{:S(2)}, u32[]{:S(2)}) collective-permute-start(bf16[3,512,128]{2,1,0:T(8,128)(2,1)S(1)} %get-tuple-element.569), channel_id=1, source_target_pairs={{0,1},{1,0},{2,3},{3,2},{4,5},{5,4},{6,7},{7,6},{8,9},{9,8},{10,11... | collective-permute-start | bytes 1179656 | tf_op jit(solution)/shard_map/ppermute | solution.py:38
  385.4 16.7 %collective-permute-start.98 = (bf16[3,512,128]{2,1,0:T(8,128)(2,1)S(1)}, bf16[3,512,128]{2,1,0:T(8,128)(2,1)S(1)}, u32[]{:S(2)}, u32[]{:S(2)}) collective-permute-start(bf16[3,512,128]{2,1,0:T(8,128)(2,1)S(1)} %add_convert_fusion.2), channel_id=1, source_target_pairs={{0,6},{1,7},{2,0},{3,1},{4,2},{5,3},{6,4},{7,5},{8,14},{9,15},{10,... | collective-permute-start | bytes 1179656 | tf_op jit(solution)/shard_map/ppermute | solution.py:43
  388.1 24.8 %collective-permute-start.94 = (bf16[2,192,384]{2,1,0:T(8,128)(2,1)S(1)}, bf16[2,192,384]{2,1,0:T(8,128)(2,1)S(1)}, u32[]{:S(2)}, u32[]{:S(2)}) collective-permute-start(bf16[2,192,384]{2,1,0:T(8,128)(2,1)S(1)} %get-tuple-element.566), channel_id=1, source_target_pairs={{0,2},{1,3},{2,0},{3,1},{4,6},{5,7},{6,4},{7,5},{8,10},{9,11},{10,... | collective-permute-start | bytes 884744 | tf_op jit(solution)/shard_map/ppermute | solution.py:38
  392.6 21.2 %collective-permute-start.95 = (bf16[2,192,384]{2,1,0:T(8,128)(2,1)S(1)}, bf16[2,192,384]{2,1,0:T(8,128)(2,1)S(1)}, u32[]{:S(2)}, u32[]{:S(2)}) collective-permute-start(bf16[2,192,384]{2,1,0:T(8,128)(2,1)S(1)} %get-tuple-element.567), channel_id=1, source_target_pairs={{0,4},{1,5},{2,6},{3,7},{4,0},{5,1},{6,2},{7,3},{8,12},{9,13},{10,... | collective-permute-start | bytes 884744 | tf_op jit(solution)/shard_map/ppermute | solution.py:38
  413.0 23.6 %collective-permute-start.104 = (bf16[3,512,128]{2,1,0:T(8,128)(2,1)S(1)}, bf16[3,512,128]{2,1,0:T(8,128)(2,1)S(1)}, u32[]{:S(2)}, u32[]{:S(2)}) collective-permute-start(bf16[3,512,128]{2,1,0:T(8,128)(2,1)S(1)} %get-tuple-element.583), channel_id=1, source_target_pairs={{0,1},{1,0},{2,3},{3,2},{4,5},{5,4},{6,7},{7,6},{8,9},{9,8},{10,11... | collective-permute-start | bytes 1179656 | tf_op jit(solution)/shard_map/ppermute | solution.py:38
  418.1 18.5 %collective-permute-start.106 = (bf16[3,512,128]{2,1,0:T(8,128)(2,1)S(1)}, bf16[3,512,128]{2,1,0:T(8,128)(2,1)S(1)}, u32[]{:S(2)}, u32[]{:S(2)}) collective-permute-start(bf16[3,512,128]{2,1,0:T(8,128)(2,1)S(1)} %add_convert_fusion), channel_id=1, source_target_pairs={{0,6},{1,7},{2,0},{3,1},{4,2},{5,3},{6,4},{7,5},{8,14},{9,15},{10,... | collective-permute-start | bytes 1179656 | tf_op jit(solution)/shard_map/ppermute | solution.py:43
  420.3 17.9 %collective-permute-start.100 = (bf16[1,192,384]{2,1,0:T(8,128)(2,1)S(1)}, bf16[1,192,384]{2,1,0:T(8,128)(2,1)S(1)}, u32[]{:S(2)}, u32[]{:S(2)}) collective-permute-start(bf16[1,192,384]{2,1,0:T(8,128)(2,1)S(1)} %get-tuple-element.576), channel_id=1, source_target_pairs={{0,4},{1,5},{2,6},{3,7},{4,0},{5,1},{6,2},{7,3},{8,12},{9,13},{10,... | collective-permute-start | bytes 442376 | tf_op jit(solution)/shard_map/ppermute | solution.py:38
  460.1 30.3 %collective-permute-start.41 = (bf16[128,768]{1,0:T(8,128)(2,1)}, bf16[128,768]{1,0:T(8,128)(2,1)}, u32[]{:S(2)}, u32[]{:S(2)}) collective-permute-start(bf16[128,768]{1,0:T(8,128)(2,1)} %get-tuple-element.398.refs_0_), channel_id=1, source_target_pairs={{0,16},{8,24},{16,0},{24,8},{1,17},{9,25},{17,1},{25,9},{2,18},{10... | collective-permute-start | bytes 589832 | tf_op jit(solution)/shard_map/ppermute | solution.py:38
  474.3 28.1 %collective-permute-start.134 = (bf16[2,192,384]{2,1,0:T(8,128)(2,1)S(1)}, bf16[2,192,384]{2,1,0:T(8,128)(2,1)S(1)}, u32[]{:S(2)}, u32[]{:S(2)}) collective-permute-start(bf16[2,192,384]{2,1,0:T(8,128)(2,1)S(1)} %get-tuple-element.677.refs_0_), channel_id=1, source_target_pairs={{0,2},{1,3},{2,0},{3,1},{4,6},{5,7},{6,4},{7,5},{8,10},{9,11},{10,... | collective-permute-start | bytes 884744 | tf_op jit(solution)/shard_map/ppermute | solution.py:38
  476.1 27.8 %collective-permute-start.135 = (bf16[2,192,384]{2,1,0:T(8,128)(2,1)S(1)}, bf16[2,192,384]{2,1,0:T(8,128)(2,1)S(1)}, u32[]{:S(2)}, u32[]{:S(2)}) collective-permute-start(bf16[2,192,384]{2,1,0:T(8,128)(2,1)S(1)} %get-tuple-element.678.refs_1_), channel_id=1, source_target_pairs={{0,4},{1,5},{2,6},{3,7},{4,0},{5,1},{6,2},{7,3},{8,12},{9,13},{10,... | collective-permute-start | bytes 884744 | tf_op jit(solution)/shard_map/ppermute | solution.py:38
  494.4 17.4 %collective-permute-start.42 = (bf16[128,768]{1,0:T(8,128)(2,1)}, bf16[128,768]{1,0:T(8,128)(2,1)S(1)}, u32[]{:S(2)}, u32[]{:S(2)}) collective-permute-start(bf16[128,768]{1,0:T(8,128)(2,1)} %get-tuple-element.398.refs_0_), channel_id=1, source_target_pairs={{0,8},{8,0},{16,24},{24,16},{1,9},{9,1},{17,25},{25,17},{2,10},{10... | collective-permute-start | bytes 589832 | tf_op jit(solution)/shard_map/ppermute | solution.py:38
  509.6 26.1 %collective-permute-start.114 = (bf16[128,768]{1,0:T(8,128)(2,1)}, bf16[128,768]{1,0:T(8,128)(2,1)}, u32[]{:S(2)}, u32[]{:S(2)}) collective-permute-start(bf16[128,768]{1,0:T(8,128)(2,1)} %get-tuple-element.625.refs_0_), channel_id=1, source_target_pairs={{0,16},{8,24},{16,0},{24,8},{1,17},{9,25},{17,1},{25,9},{2,18},{10... | collective-permute-start | bytes 589832 | tf_op jit(solution)/shard_map/ppermute | solution.py:38
  511.0 33.6 %collective-permute-start.136 = (bf16[4,192,384]{2,1,0:T(8,128)(2,1)S(1)}, bf16[4,192,384]{2,1,0:T(8,128)(2,1)S(1)}, u32[]{:S(2)}, u32[]{:S(2)}) collective-permute-start(bf16[4,192,384]{2,1,0:T(8,128)(2,1)S(1)} %get-tuple-element.681.refs_0_), channel_id=1, source_target_pairs={{0,1},{1,0},{2,3},{3,2},{4,5},{5,4},{6,7},{7,6},{8,9},{9,8},{10,11... | collective-permute-start | bytes 1769480 | tf_op jit(solution)/shard_map/ppermute | solution.py:38
  512.5 32.1 %collective-permute-start.137 = (bf16[4,192,384]{2,1,0:T(8,128)(2,1)S(1)}, bf16[4,192,384]{2,1,0:T(8,128)(2,1)S(1)}, u32[]{:S(2)}, u32[]{:S(2)}) collective-permute-start(bf16[4,192,384]{2,1,0:T(8,128)(2,1)S(1)} %get-tuple-element.682.refs_2_), channel_id=1, source_target_pairs={{0,2},{1,3},{2,0},{3,1},{4,6},{5,7},{6,4},{7,5},{8,10},{9,11},{10,... | collective-permute-start | bytes 1769480 | tf_op jit(solution)/shard_map/ppermute | solution.py:38
  513.1 19.5 %collective-permute-start.125 = (bf16[2,96,384]{2,1,0:T(8,128)(2,1)}, bf16[2,96,384]{2,1,0:T(8,128)(2,1)}, u32[]{:S(2)}, u32[]{:S(2)}) collective-permute-start(bf16[2,96,384]{2,1,0:T(8,128)(2,1)} %get-tuple-element.648.refs_0_), channel_id=1, source_target_pairs={{0,2},{1,3},{2,0},{3,1},{4,6},{5,7},{6,4},{7,5},{8,10},{9,11},{10,... | collective-permute-start | bytes 442376 | tf_op jit(solution)/shard_map/ppermute | solution.py:38
  515.8 16.9 %collective-permute-start.126 = (bf16[2,96,384]{2,1,0:T(8,128)(2,1)}, bf16[2,96,384]{2,1,0:T(8,128)(2,1)}, u32[]{:S(2)}, u32[]{:S(2)}) collective-permute-start(bf16[2,96,384]{2,1,0:T(8,128)(2,1)} %get-tuple-element.649.refs_1_), channel_id=1, source_target_pairs={{0,4},{1,5},{2,6},{3,7},{4,0},{5,1},{6,2},{7,3},{8,12},{9,13},{10,... | collective-permute-start | bytes 442376 | tf_op jit(solution)/shard_map/ppermute | solution.py:38
  (191 other events, 2018.7 us)

commit v3 on v2

v3 whole, which is shorter than its diff:
```python
import functools

import jax
import jax.numpy as jnp
from jax import lax
from jax.experimental import pallas as pl
from jax.experimental.pallas import tpu as pltpu
from jax.sharding import PartitionSpec as P

D = 768
HD = 64
LAYERS = 2
WINDOW = 64
KB = 16
SEL = 4
QB = 64
WIDE = 2 * HD

epsilon = 1e-05
negative = -1e30
scale = HD ** (-0.5)
bf16 = jnp.bfloat16
f32 = jnp.float32

STEPS = (0, 2, 1, 3)
GAIN, SHIFT, B_OUT, B_DOWN, PARAM_ROWS = 0, 4, 8, 10, 16


def params(megabytes):
    return pltpu.CompilerParams(vmem_limit_bytes=megabytes * 2**20)


def cost(flops, moved, special=0):
    return pl.CostEstimate(flops=int(flops), bytes_accessed=int(moved), transcendentals=int(special))


def swap(value, axis, step):
    return lax.ppermute(value, axis, [(i, i ^ step) for i in range(lax.axis_size(axis))])


def rotate(value, axis, step):
    count = lax.axis_size(axis)
    return lax.ppermute(value, axis, [(i, (i + step) % count) for i in range(count)])


def share_features(own):
    across = swap(own, "head", 2)
    beside = swap(own, "head", 1)
    both = swap(across, "head", 1)
    return own, across, beside, both


def share_rows(own):
    return own, swap(own, "head", 1)


def sum_rows(pieces):
    own, other = pieces
    chip = (own.astype(f32) + swap(other, "head", 1).astype(f32)).astype(bf16)
    return chip, swap(chip, "head", 2)


def small_sum(value, axis):
    step = 1
    while step < lax.axis_size(axis):
        value = value + swap(value, axis, step)
        step *= 2
    return value


def finish_in_turn(other, *bundles):
    if not bundles[0].ring:
        return
    turns = {True: [], False: []}
    for index in TURNS:
        bundle = bundles[index]
        if bundle.step == 6:
            continue
        stage = bundle.step if bundle.step < 3 else 5 - bundle.step
        queue = turns[bundle.order[stage] == 0]
        depth = COLUMN_DEPTH if bundle.order[stage] == 0 else Z_DEPTH
        bundle.send(queue[-depth] if len(queue) >= depth else other)
        queue.append(bundle.coming)


def ring_form(count):
    return count == 8


COLUMN_FIRST = (0, 1, 2)

TURNS = (0, 1, 2, 5, 3, 0, 2, 4, 1, 3, 2, 5, 3, 2, 4, 3, 5, 3, 4, 4, 4, 5, 5, 5)
COLUMN_DEPTH, Z_DEPTH = 2, 3


def after(value, other):
    return lax.optimization_barrier((value, other))[0]


class Bundle:
    def __init__(self, pieces, order):
        self.ring = ring_form(lax.axis_size("tok"))
        self.step, self.order = 0, order
        self.kept, self.out = pieces
        if not self.ring:
            self.result = lax.psum(tuple(pieces), "tok")

    def send(self, other=None):
        if not self.ring or self.step == 6:
            return
        if self.step:
            kept, came = self.kept, self.coming
            if other is not None:
                kept, came = after((kept, came), other)
            if self.step < 3:
                self.kept, self.out = merge("split", kept, came)
            else:
                (self.kept,) = merge("add" if self.step == 3 else "join", kept, came)
                self.out = self.kept
        stage = self.step if self.step < 3 else 5 - self.step
        self.coming = swap(self.out, "tok", 1 << self.order[stage])
        self.step += 1

    def take(self, other):
        if not self.ring:
            return other
        self.coming, other = lax.optimization_barrier((self.coming, other))
        return other

    def finish(self):
        while self.ring and self.step < 6:
            self.send()
        if self.ring:
            self.result = (self.kept, self.coming)
        return self.result


def gather_blocks(chunks):
    count = lax.axis_size("tok")
    if not ring_form(count):
        return [lax.all_gather(chunk, "tok") for chunk in chunks]
    parts = [None] * (2 * count)
    for k, current in enumerate(chunks):
        for hop in range(count // 2):
            other = swap(current, "tok", 1)
            after = None
            if hop < count // 2 - 1:
                after = rotate(current, "tok", 2)
                current, other, after = lax.optimization_barrier((current, other, after))
            parts[4 * hop + k] = current
            parts[4 * hop + 2 + k] = other
            current = after
    return parts


def return_blocks(parts, meanwhile):
    count = lax.axis_size("tok")
    if not ring_form(count):
        return [
            [lax.psum_scatter(part, "tok", scatter_dimension=0, tiled=False)] for part in parts
        ]
    running = [None, None]
    own = [None, None]
    got = [None, None]
    for d in range(count // 2 - 1, -1, -1):
        for k in range(2):
            mine, other = parts[4 * d + k], parts[4 * d + 2 + k]
            if got[k] is not None:
                other, got[k] = lax.optimization_barrier((other, got[k]))
                total = own[k].astype(f32) + got[k].astype(f32)
                if running[k] is not None:
                    total = total + running[k].astype(f32)
                running[k] = rotate(total.astype(bf16), "tok", -2)
            own[k], got[k] = mine, swap(other, "tok", 1)
        if d == 1:
            running = meanwhile(running)
    return [[own[k], got[k], running[k]] for k in range(2)]


def slot_of(block, tok, count):
    if not ring_form(count):
        return block
    away = (tok >> 1) - (block >> 1)
    return 2 * jnp.maximum(away, 0) + ((tok ^ block) & 1)


ON_LANES = (((1,), (1,)), ((), ()))
ON_ROWS = (((0,), (0,)), ((), ()))


def normalise(rows):
    average = jnp.mean(rows, axis=-1, keepdims=True)
    centred = rows - average
    spread = jnp.mean(centred * centred, axis=-1, keepdims=True)
    inverse = lax.rsqrt(spread + epsilon)
    return centred * inverse, inverse


def row(ref, index):
    return ref[index : index + 1, :].astype(f32)


def piece_rows(place, step, size):
    return pl.ds(pl.multiple_of((place[0] ^ step) * size, size), size)


def half_rows(place, k, size):
    return pl.ds(pl.multiple_of(((place[0] & 1) ^ k) * size, size), size)


def project_kernel(place, *refs, heads, first):
    if first:
        pieces, param_pieces = refs[:4], refs[4:8]
        w_ref, bias_ref, normed_ref, q_ref = refs[8:12]
        kv_refs = refs[12:14]
        low_ref, param_ref, staged, turned = refs[14:]
        width = staged.shape[0] // 4
        for k in range(4):
            staged[piece_rows(place, STEPS[k], width), :] = pieces[k][...]
            turned[piece_rows(place, STEPS[k], width), :] = param_pieces[k][...].astype(f32)
        param_ref[...] = jnp.transpose(turned[...])[:PARAM_ROWS]
    else:
        pieces = refs[:2]
        w_ref, bias_ref, normed_ref, q_ref = refs[2:6]
        kv_refs = refs[6:]
    size = normed_ref.shape[0] // 2
    for k in range(2):
        rows = half_rows(place, k, size)
        if first:
            part = jnp.transpose(staged[:, rows].astype(f32))
            if k == 0:
                low_ref[...] = part.astype(bf16)
            unit, _ = normalise(part)
            normed = (unit * row(param_ref, GAIN) + row(param_ref, SHIFT)).astype(bf16)
        else:
            normed = pieces[k][...]
        normed_ref[rows, :] = normed
        projected = lax.dot_general(normed, w_ref[...], ON_LANES, preferred_element_type=f32)
        projected = projected + bias_ref[...]
        for h in range(heads):
            q_ref[h, rows, :] = (projected[:, h * WIDE : (h + 1) * WIDE] * scale).astype(bf16)
            at = (heads + h) * WIDE
            kv_refs[k][h] = projected[:, at : at + WIDE].astype(bf16)


def whole(shape):
    return pl.BlockSpec(shape, lambda *_: (0,) * len(shape))


def project(place, pieces, param_pieces, w_all, bias_all, rows, heads):
    first = param_pieces is not None
    arrays = tuple(pieces) + (tuple(param_pieces) if first else ())
    columns = w_all.shape[0]
    out_shapes = [
        jax.ShapeDtypeStruct((rows, D), bf16),
        jax.ShapeDtypeStruct((heads, rows, WIDE), bf16),
        jax.ShapeDtypeStruct((heads, rows // 2, WIDE), bf16),
        jax.ShapeDtypeStruct((heads, rows // 2, WIDE), bf16),
    ]
    scratch = []
    if first:
        out_shapes += [
            jax.ShapeDtypeStruct((rows // 2, D), bf16),
            jax.ShapeDtypeStruct((PARAM_ROWS, D), f32),
        ]
        scratch = [pltpu.VMEM((D, rows), bf16), pltpu.VMEM((D, 128), f32)]
    return pl.pallas_call(
        functools.partial(project_kernel, heads=heads, first=first),
        grid_spec=pltpu.PrefetchScalarGridSpec(
            num_scalar_prefetch=1,
            grid=(1,),
            in_specs=[whole(array.shape) for array in arrays + (w_all, bias_all)],
            out_specs=[whole(shape.shape) for shape in out_shapes],
            scratch_shapes=scratch,
        ),
        out_shape=out_shapes,
        compiler_params=params(12),
        cost_estimate=cost(2 * rows * D * columns, 2 * D * columns + 8 * rows * D),
        name="project",
    )(place, *arrays, w_all, bias_all)


def turn_kernel(place, *refs):
    pieces = refs[:4]
    out_ref, sums_ref, staged = refs[4:]
    width = staged.shape[0] // 4
    size = out_ref.shape[0] // 2
    for k in range(4):
        staged[piece_rows(place, STEPS[k], width), :] = pieces[k][...]
    for k in range(2):
        part = jnp.transpose(staged[:, k * size : (k + 1) * size].astype(f32))
        out_ref[k * size : (k + 1) * size, :] = part.astype(bf16)

        @pl.when((place[0] & 1) == k)
        def _():
            sums_ref[...] = jnp.sum(part, axis=0, keepdims=True)


def turn(place, pieces):
    width, rows = pieces[0].shape
    return pl.pallas_call(
        turn_kernel,
        grid_spec=pltpu.PrefetchScalarGridSpec(
            num_scalar_prefetch=1,
            grid=(1,),
            in_specs=[whole((width, rows))] * 4,
            out_specs=[whole((rows, D)), whole((1, D))],
            scratch_shapes=[pltpu.VMEM((D, rows), bf16)],
        ),
        out_shape=[jax.ShapeDtypeStruct((rows, D), bf16), jax.ShapeDtypeStruct((1, D), f32)],
        compiler_params=params(6),
        cost_estimate=cost(rows * D, 4 * rows * D),
        name="turn",
    )(place, *pieces)


def merge_kernel(kept, came, *outs, act):
    count = kept.shape[0]
    if act == "join":
        outs[0][:count] = kept[...]
        outs[0][count:] = came[...]
        return
    each = count // len(outs)
    for i, out in enumerate(outs):
        at = slice(i * each, (i + 1) * each)
        out[...] = (kept[at].astype(f32) + came[at].astype(f32)).astype(bf16)


def merge(act, kept, came):
    count = kept.shape[0]
    counts = {"add": [count], "split": [count // 2] * 2, "join": [2 * count]}[act]
    shapes = [(n,) + kept.shape[1:] for n in counts]
    return pl.pallas_call(
        functools.partial(merge_kernel, act=act),
        grid=(1,),
        in_specs=[whole(kept.shape)] * 2,
        out_specs=[whole(shape) for shape in shapes],
        out_shape=[jax.ShapeDtypeStruct(shape, bf16) for shape in shapes],
        compiler_params=params(8),
        cost_estimate=cost(kept.size, 8 * kept.size),
        name="merge",
    )(kept, came)


def chunk_rows(place, slot, k, rows):
    return pl.ds(pl.multiple_of(slot * rows + ((place[0] & 1) ^ k) * (rows // 2), rows // 2), rows // 2)


def copies(place, parts, scratch, sems, head, buffer, rows):
    if len(parts) == 2:
        sources = [parts[k].at[slot, head] for slot in range(parts[0].shape[0]) for k in range(2)]
    else:
        sources = [part.at[head] for part in parts]
    return [
        pltpu.make_async_copy(
            source,
            scratch.at[buffer, chunk_rows(place, i // 2, i % 2, rows), :],
            sems.at[buffer, i],
        )
        for i, source in enumerate(sources)
    ]


def bring_blocks(place, parts, scratch, sems, heads, rows):
    head = pl.program_id(0)
    buffer = lax.rem(head, 2)

    @pl.when(head == 0)
    def _():
        for copy in copies(place, parts, scratch, sems, 0, 0, rows):
            copy.start()

    @pl.when(head + 1 < heads)
    def _():
        for copy in copies(place, parts, scratch, sems, head + 1, 1 - buffer, rows):
            copy.start()

    for copy in copies(place, parts, scratch, sems, head, buffer, rows):
        copy.wait()
    return head, buffer


def listed_rows(place, starts, head, b, rows):
    own, before = place[3], place[4]
    if b == 0:
        near = [
            (pl.multiple_of(before + rows - WINDOW, WINDOW), WINDOW),
            (pl.multiple_of(own, WINDOW), WINDOW),
        ]
    else:
        near = [(pl.multiple_of(own + (b - 1) * QB, WINDOW), 2 * WINDOW)]
    far = [(pl.multiple_of(starts[head, b * SEL + s], KB), KB) for s in range(SEL)]
    return near + far


def load_rows(keys, buffer, where):
    return jnp.concatenate([keys[buffer, pl.ds(start, size), :] for start, size in where], axis=0)


def mask_kernel(place, chosen, near_ref, far_ref, out_ref, *, heads, blocks):
    rows = blocks * QB
    tok, boundary = place[1], place[2]
    wide = 2 * WINDOW
    line = lax.broadcasted_iota(jnp.int32, (QB, wide), 1)
    column = lax.broadcasted_iota(jnp.int32, (QB, wide), 0)
    band = (line > column) & (line <= column + WINDOW)
    diagonal = line == column + WINDOW
    in_second = lambda position: jnp.where(position >= boundary, 1, 0)
    lane = lax.broadcasted_iota(jnp.int32, (1, SEL * KB), 1)
    for b in range(blocks):
        first = tok * rows + b * QB
        query_seq = in_second(first + lax.broadcasted_iota(jnp.int32, (QB, 1), 0))
        key = first - WINDOW + lax.broadcasted_iota(jnp.int32, (1, wide), 1)
        near = band & (diagonal | (near_ref[b : b + 1, :] > 0.0))
        near = jnp.where(near & (in_second(key) == query_seq), 0.0, negative)
        for head in range(heads):
            usable = jnp.zeros((1, SEL * KB), f32)
            token = lane & (KB - 1)
            for s in range(SEL):
                block = chosen[head, b * SEL + s]
                here = (lane >= s * KB) & (lane < (s + 1) * KB)
                early = block * KB + KB <= first - WINDOW
                usable = jnp.where(here & early, far_ref[pl.ds(block, 1), :], usable)
                token = token + jnp.where(here, block * KB, 0)
            far = (usable > 0.0) & (in_second(token) == query_seq)
            at = pl.ds(b * QB, QB)
            out_ref[head, at, :wide] = near
            out_ref[head, at, wide:] = jnp.where(far, 0.0, negative)


def masks(place, chosen, near_valid, far_valid, heads, rows):
    listed = 2 * WINDOW + SEL * KB
    return pl.pallas_call(
        functools.partial(mask_kernel, heads=heads, blocks=rows // QB),
        grid_spec=pltpu.PrefetchScalarGridSpec(
            num_scalar_prefetch=2,
            grid=(1,),
            in_specs=[whole(near_valid.shape), whole(far_valid.shape)],
            out_specs=whole((heads, rows, listed)),
        ),
        out_shape=jax.ShapeDtypeStruct((heads, rows, listed), f32),
        compiler_params=params(6),
        cost_estimate=cost(20 * heads * rows * listed, 4 * heads * rows * listed),
        name="masks",
    )(place, chosen, near_valid, far_valid)


def attend_kernel(place, starts, *refs, heads, blocks, parts):
    q_ref, w_ref, mask_ref = refs[:3]
    kv_parts = refs[3 : 3 + parts]
    mixed_ref, probs_ref = refs[3 + parts : 5 + parts]
    outs = refs[5 + parts : 7 + parts]
    keys, gathered, work, sems = refs[7 + parts :]
    rows = blocks * QB
    head, buffer = bring_blocks(place, kv_parts, keys, sems, heads, rows)
    blocks_at = [pl.ds(b * QB, QB) for b in range(blocks)]
    where = [listed_rows(place, starts, head, b, rows) for b in range(blocks)]
    for b, at in enumerate(blocks_at):
        kv = load_rows(keys, buffer, where[b])
        scores = lax.dot_general(q_ref[0, at, :], kv, ON_LANES, preferred_element_type=f32)
        work[at, :] = scores + mask_ref[0, at, :]
    scores = work[...]
    weights = jnp.exp(scores - jnp.max(scores, axis=-1, keepdims=True))
    weights = weights * (1.0 / jnp.sum(weights, axis=-1, keepdims=True))
    probs_ref[0] = weights.astype(bf16)
    for b, at in enumerate(blocks_at):
        kv = load_rows(keys, buffer, where[b])
        out = jnp.dot(probs_ref[0, at, :], kv, preferred_element_type=f32).astype(bf16)
        mixed_ref[0, at, :] = out
        gathered[head, at, :] = out

    @pl.when(head == heads - 1)
    def _():
        size = rows // 2
        for k in range(2):
            at = half_rows(place, k, size)
            mixed = jnp.concatenate([gathered[h, at, :] for h in range(heads)], axis=1)
            outs[k][...] = jnp.dot(mixed, w_ref[...], preferred_element_type=f32).astype(bf16)


def attend(place, starts, queries, w_out, mask, parts, count):
    heads, rows, _ = queries.shape
    listed = mask.shape[2]
    per_head = lambda columns: pl.BlockSpec((1, rows, columns), lambda h, *_: (h, 0, 0))
    slots = count if len(parts) == 2 else len(parts) // 2
    return pl.pallas_call(
        functools.partial(attend_kernel, heads=heads, blocks=rows // QB, parts=len(parts)),
        grid_spec=pltpu.PrefetchScalarGridSpec(
            num_scalar_prefetch=2,
            grid=(heads,),
            in_specs=[per_head(WIDE), whole(w_out.shape), per_head(listed)]
            + [pl.BlockSpec(memory_space=pl.ANY)] * len(parts),
            out_specs=[per_head(WIDE), per_head(listed)] + [whole((rows // 2, D))] * 2,
            scratch_shapes=[
                pltpu.VMEM((2, slots * rows, WIDE), bf16),
                pltpu.VMEM((heads, rows, WIDE), bf16),
                pltpu.VMEM((rows, listed), f32),
                pltpu.SemaphoreType.DMA((2, 2 * slots)),
            ],
        ),
        out_shape=[
            jax.ShapeDtypeStruct((heads, rows, WIDE), bf16),
            jax.ShapeDtypeStruct((heads, rows, listed), bf16),
        ]
        + [jax.ShapeDtypeStruct((rows // 2, D), bf16)] * 2,
        compiler_params=params(30 if len(parts) == 2 else 12),
        cost_estimate=cost(
            2 * rows * heads * WIDE * (D + 512), 2 * heads * WIDE * rows * (slots + 4)
        ),
        name="attend",
    )(place, starts, queries, w_out, mask, *parts)


def attend_back_kernel(place, starts, *refs, heads, count, blocks, parts):
    q_ref, probs_ref, w_ref = refs[:3]
    pieces = refs[3:5]
    kv_parts = refs[5 : 5 + parts]
    dq_ref, grad_ref = refs[5 + parts : 7 + parts]
    outs = refs[7 + parts : 7 + 2 * parts]
    keys, sums, mixed_ref, work, scores_ref, grads_ref, sems = refs[7 + 2 * parts :]
    rows = blocks * QB
    size = rows // 2
    head, buffer = bring_blocks(place, kv_parts, keys, sems, heads, rows)

    @pl.when(head == 0)
    def _():
        for k in range(2):
            grad_ref[half_rows(place, k, size), :] = pieces[k][...]

    sums[...] = jnp.zeros_like(sums)
    mixed_ref[...] = lax.dot_general(
        grad_ref[...], w_ref[...], ON_LANES, preferred_element_type=f32
    ).astype(bf16)
    blocks_at = [pl.ds(b * QB, QB) for b in range(blocks)]
    where = [listed_rows(place, starts, head, b, rows) for b in range(blocks)]
    for b, at in enumerate(blocks_at):
        kv = load_rows(keys, buffer, where[b])
        work[at, :] = lax.dot_general(
            mixed_ref[at, :], kv, ON_LANES, preferred_element_type=f32
        )
    weights = probs_ref[0].astype(f32)
    grad_probs = work[...]
    inner = jnp.sum(weights * grad_probs, axis=-1, keepdims=True)
    scores_ref[...] = (weights * (grad_probs - inner)).astype(bf16)
    for b, at in enumerate(blocks_at):
        kv = load_rows(keys, buffer, where[b])
        grad_q = jnp.dot(scores_ref[at, :], kv, preferred_element_type=f32)
        dq_ref[0, at, :] = (grad_q.astype(bf16).astype(f32) * scale).astype(bf16)
    for b, at in enumerate(blocks_at):
        grads_ref[b] = lax.dot_general(
            jnp.concatenate([scores_ref[at, :], probs_ref[0, at, :]], axis=0),
            jnp.concatenate([q_ref[0, at, :], mixed_ref[at, :]], axis=0),
            ON_ROWS,
            preferred_element_type=f32,
        )
    for b in range(blocks):
        done = 0
        for start, length in where[b]:
            sums[pl.ds(start, length), :] += grads_ref[b, done : done + length, :]
            done += length
    for i in range(2 * count if parts == 2 else parts):
        chunk = sums[chunk_rows(place, i // 2, i % 2, rows), :].astype(bf16)
        if parts == 2:
            outs[i % 2][i // 2, 0] = chunk
        else:
            outs[i][0] = chunk


def attend_back(place, starts, queries, probs, w_out, pieces, parts, count):
    heads, rows, _ = queries.shape
    listed = probs.shape[2]
    per_head = lambda columns: pl.BlockSpec((1, rows, columns), lambda h, *_: (h, 0, 0))
    slots = count if len(parts) == 2 else len(parts) // 2
    if len(parts) == 2:
        out_specs = [pl.BlockSpec((count, 1, rows // 2, WIDE), lambda h, *_: (0, h, 0, 0))] * 2
    else:
        out_specs = [pl.BlockSpec((1, rows // 2, WIDE), lambda h, *_: (h, 0, 0))] * len(parts)
    return pl.pallas_call(
        functools.partial(
            attend_back_kernel, heads=heads, count=count, blocks=rows // QB, parts=len(parts)
        ),
        grid_spec=pltpu.PrefetchScalarGridSpec(
            num_scalar_prefetch=2,
            grid=(heads,),
            in_specs=[
                per_head(WIDE),
                per_head(listed),
                pl.BlockSpec((WIDE, D), lambda h, *_: (h, 0)),
            ]
            + [whole((rows // 2, D))] * 2
            + [pl.BlockSpec(memory_space=pl.ANY)] * len(parts),
            out_specs=[per_head(WIDE), whole((rows, D))] + out_specs,
            scratch_shapes=[
                pltpu.VMEM((2, slots * rows, WIDE), bf16),
                pltpu.VMEM((slots * rows, WIDE), f32),
                pltpu.VMEM((rows, WIDE), bf16),
                pltpu.VMEM((rows, listed), f32),
                pltpu.VMEM((rows, listed), bf16),
                pltpu.VMEM((rows // QB, listed, WIDE), f32),
                pltpu.SemaphoreType.DMA((2, 2 * slots)),
            ],
        ),
        out_shape=[
            jax.ShapeDtypeStruct((heads, rows, WIDE), bf16),
            jax.ShapeDtypeStruct((rows, D), bf16),
        ]
        + [jax.ShapeDtypeStruct(part.shape, bf16) for part in parts],
        compiler_params=params(62 if len(parts) == 2 else 16),
        cost_estimate=cost(
            2 * rows * heads * WIDE * (D + 1536), 4 * heads * WIDE * rows * (slots + 4)
        ),
        name="attend_back",
    )(place, starts, queries, probs, w_out, *pieces, *parts)


def project_back_kernel(place, *refs, heads, terms, norm_row):
    dq_ref, w_ref, normed_ref, param = refs[:4]
    kv_refs = refs[4 : 4 + 2 * terms]
    dkv_ref, bias_ref, sums_ref = refs[4 + 2 * terms : 7 + 2 * terms]
    outs = refs[7 + 2 * terms :]
    gain, shift = row(param, GAIN + norm_row), row(param, SHIFT + norm_row)
    sums_ref[...] = jnp.zeros_like(sums_ref)
    rows = dq_ref.shape[1]
    size = rows // 2
    for h in range(heads):
        bias_ref[h : h + 1, :] = jnp.sum(dq_ref[h].astype(f32), axis=0, keepdims=True)
        over_rows = jnp.zeros((1, WIDE), f32)
        for k in range(2):
            total = kv_refs[k * terms][h].astype(f32)
            for term in kv_refs[k * terms + 1 : (k + 1) * terms]:
                total = total + term[h].astype(f32)
            low = total.astype(bf16)
            dkv_ref[h, half_rows(place, k, size), :] = low
            over_rows = over_rows + jnp.sum(low.astype(f32), axis=0, keepdims=True)
        bias_ref[heads + h : heads + h + 1, :] = over_rows
    for k in range(2):
        at = half_rows(place, k, size)
        grads = jnp.concatenate(
            [dq_ref[h, at, :] for h in range(heads)] + [dkv_ref[h, at, :] for h in range(heads)],
            axis=1,
        )
        grad_normed = jnp.dot(grads, w_ref[...], preferred_element_type=f32)
        outs[k][...] = grad_normed.astype(bf16)
        unit = (normed_ref[at, :].astype(f32) - shift) / gain
        sums_ref[0:1, :] += jnp.sum(grad_normed * unit, axis=0, keepdims=True)
        sums_ref[1:2, :] += jnp.sum(grad_normed, axis=0, keepdims=True)


def project_back(place, dq, w_all, normed, param, kv_terms, norm_row):
    heads, rows, _ = dq.shape
    half = rows // 2
    return pl.pallas_call(
        functools.partial(
            project_back_kernel, heads=heads, terms=len(kv_terms[0]), norm_row=norm_row
        ),
        grid_spec=pltpu.PrefetchScalarGridSpec(
            num_scalar_prefetch=1,
            grid=(1,),
            in_specs=[whole(array.shape) for array in (dq, w_all, normed, param)]
            + [whole((heads, half, WIDE))] * (2 * len(kv_terms[0])),
            out_specs=[whole(dq.shape), whole((2 * heads, WIDE)), whole((2, D))]
            + [whole((half, D))] * 2,
        ),
        out_shape=[
            jax.ShapeDtypeStruct(dq.shape, bf16),
            jax.ShapeDtypeStruct((2 * heads, WIDE), f32),
            jax.ShapeDtypeStruct((2, D), f32),
        ]
        + [jax.ShapeDtypeStruct((half, D), bf16)] * 2,
        compiler_params=params(12),
        cost_estimate=cost(4 * rows * D * heads * WIDE, 4 * D * heads * WIDE + 12 * rows * D),
        name="project_back",
    )(place, dq, w_all, normed, param, *kv_terms[0], *kv_terms[1])


def feed_kernel(place, *refs):
    pieces = refs[:2]
    up_ref, bias_ref, down_ref, kept_ref, slope_ref = refs[2:7]
    outs = refs[7:]
    size = pieces[0].shape[0]
    root = 0.7978845608028654
    cubic = 0.044715
    for k in range(2):
        at = pl.ds(k * size, size)
        normed = pieces[k][...]
        kept_ref[0, at, :] = normed
        inner = jnp.dot(normed, up_ref[...], preferred_element_type=f32) + bias_ref[...]
        square = inner * inner
        bend = jnp.tanh(root * inner * (1.0 + cubic * square))
        half = 0.5 * (1.0 + bend)
        hidden = (inner * half).astype(bf16)
        kept_ref[1, at, :] = hidden
        slope = half + 0.5 * inner * (1.0 - bend * bend) * (root * (1.0 + 3.0 * cubic * square))
        slope_ref[at, :] = slope.astype(bf16)
        outs[k][...] = jnp.dot(hidden, down_ref[...], preferred_element_type=f32).astype(bf16)


def feed(place, pieces, w_up, b_up, w_down):
    half = pieces[0].shape[0]
    rows = 2 * half
    units = w_up.shape[1]
    return pl.pallas_call(
        feed_kernel,
        grid_spec=pltpu.PrefetchScalarGridSpec(
            num_scalar_prefetch=1,
            grid=(1,),
            in_specs=[whole((half, D))] * 2
            + [whole(w_up.shape), whole(b_up.shape), whole(w_down.shape)],
            out_specs=[whole((2, rows, D)), whole((rows, units))] + [whole((half, D))] * 2,
        ),
        out_shape=[
            jax.ShapeDtypeStruct((2, rows, D), bf16),
            jax.ShapeDtypeStruct((rows, units), bf16),
        ]
        + [jax.ShapeDtypeStruct((half, D), bf16)] * 2,
        compiler_params=params(14),
        cost_estimate=cost(4 * rows * D * units, 4 * D * units + 10 * rows * D, rows * units),
        name="feed",
    )(place, *pieces, w_up, b_up, w_down)


def feed_back_kernel(place, *refs):
    pieces = refs[:2]
    down_ref, up_ref, slope_ref, inner_ref, bias_ref = refs[2:7]
    outs = refs[7:]
    size = pieces[0].shape[0]
    transposed = (((1,), (1,)), ((), ()))
    total = None
    for k in range(2):
        at = pl.ds(k * size, size)
        grad = pieces[k][...]
        hidden = lax.dot_general(grad, down_ref[...], transposed, preferred_element_type=f32)
        inner = (hidden * slope_ref[at, :].astype(f32)).astype(bf16)
        inner_ref[at, :] = inner
        part = jnp.sum(inner.astype(f32), axis=0, keepdims=True)
        total = part if total is None else total + part
        outs[k][...] = lax.dot_general(
            inner, up_ref[...], transposed, preferred_element_type=f32
        ).astype(bf16)
    bias_ref[...] = total


def halves_of(pieces, half):
    if len(pieces) == 2:
        return tuple(pieces), [whole((half, D))] * 2
    specs = [
        pl.BlockSpec((half, D), lambda i, place, k=k: ((place[0] & 1) ^ k, 0)) for k in range(2)
    ]
    return tuple(pieces) * 2, specs


def feed_back(place, pieces, w_up, w_down, slope):
    rows, units = slope.shape
    half = rows // 2
    arrays, specs = halves_of(pieces, half)
    return pl.pallas_call(
        feed_back_kernel,
        grid_spec=pltpu.PrefetchScalarGridSpec(
            num_scalar_prefetch=1,
            grid=(1,),
            in_specs=specs + [whole(w_down.shape), whole(w_up.shape), whole(slope.shape)],
            out_specs=[whole((rows, units)), whole((1, units))] + [whole((half, D))] * 2,
        ),
        out_shape=[
            jax.ShapeDtypeStruct((rows, units), bf16),
            jax.ShapeDtypeStruct((1, units), f32),
        ]
        + [jax.ShapeDtypeStruct((half, D), bf16)] * 2,
        compiler_params=params(14),
        cost_estimate=cost(4 * rows * D * units, 4 * D * units + 10 * rows * D),
        name="feed_back",
    )(place, *arrays, w_down, w_up, slope)


def add_norm_kernel(place, *refs, bias_row, norm_row):
    a, b, residual, param, valid = refs[:5]
    out_ref, low_ref, normed_ref, squares_ref = refs[5:]
    branch = a[...].astype(f32) + b[...].astype(f32) + row(param, bias_row)
    total = residual[...].astype(f32) + branch
    out_ref[...] = total
    low = total.astype(bf16)
    low_ref[...] = low
    if norm_row is not None:
        unit, _ = normalise(low.astype(f32))
        gain, shift = row(param, GAIN + norm_row), row(param, SHIFT + norm_row)
        normed_ref[...] = (unit * gain + shift).astype(bf16)
    else:
        normed_ref[...] = low
    weight = valid[...]
    squares_ref[0:1, :] = jnp.sum(weight * branch * branch, axis=0, keepdims=True)
    squares_ref[1:2, :] = jnp.sum(weight * total * total, axis=0, keepdims=True)


def own_half(half):
    return pl.BlockSpec((half, D), lambda i, place: (place[0] & 1, 0))


def add_norm(place, terms, residual, param, valid, rows, bias_row, norm_row):
    half = rows // 2
    spec = whole((half, D))
    return pl.pallas_call(
        functools.partial(add_norm_kernel, bias_row=bias_row, norm_row=norm_row),
        grid_spec=pltpu.PrefetchScalarGridSpec(
            num_scalar_prefetch=1,
            grid=(1,),
            in_specs=[spec] * 2
            + [
                spec,
                whole((PARAM_ROWS, D)),
                whole(valid.shape),
            ],
            out_specs=[spec, spec, spec, whole((2, D))],
        ),
        out_shape=[
            jax.ShapeDtypeStruct((half, D), f32),
            jax.ShapeDtypeStruct((half, D), bf16),
            jax.ShapeDtypeStruct((half, D), bf16),
            jax.ShapeDtypeStruct((2, D), f32),
        ],
        compiler_params=params(8),
        cost_estimate=cost(20 * half * D, 18 * half * D),
        name="add_norm",
    )(place, *terms, residual, param, valid)


def norm_back_kernel(place, *refs, norm_row):
    a, b, source, gradient, param = refs[:5]
    out_ref, low_ref, sums_ref = refs[5:]
    grad_normed = a[...].astype(f32) + b[...].astype(f32)
    unit, inverse = normalise(source[...].astype(f32))
    grad_unit = grad_normed * row(param, GAIN + norm_row)
    first = jnp.mean(grad_unit, axis=-1, keepdims=True)
    second = jnp.mean(grad_unit * unit, axis=-1, keepdims=True)
    total = gradient[...].astype(f32) + inverse * (grad_unit - first - unit * second)
    out_ref[...] = total
    low = total.astype(bf16)
    low_ref[...] = low
    sums_ref[0:1, :] = jnp.sum(grad_normed * unit, axis=0, keepdims=True)
    sums_ref[1:2, :] = jnp.sum(grad_normed, axis=0, keepdims=True)
    sums_ref[2:3, :] = jnp.sum(low.astype(f32), axis=0, keepdims=True)


def norm_back(place, terms, source, gradient, param, rows, norm_row):
    half = rows // 2
    spec = whole((half, D))
    pick = lambda array: spec if array.shape[0] == half else own_half(half)
    return pl.pallas_call(
        functools.partial(norm_back_kernel, norm_row=norm_row),
        grid_spec=pltpu.PrefetchScalarGridSpec(
            num_scalar_prefetch=1,
            grid=(1,),
            in_specs=[spec] * 2 + [pick(source), pick(gradient), whole((PARAM_ROWS, D))],
            out_specs=[spec, spec, whole((3, D))],
        ),
        out_shape=[
            jax.ShapeDtypeStruct((half, D), f32),
            jax.ShapeDtypeStruct((half, D), bf16),
            jax.ShapeDtypeStruct((3, D), f32),
        ],
        compiler_params=params(8),
        cost_estimate=cost(20 * half * D, 18 * half * D),
        name="norm_back",
    )(place, *terms, source, gradient, param)


def piece_slot(place, piece, order):
    away = piece ^ place[5]
    bit = lambda i: (away >> order[i]) & 1
    return bit(0), 2 * bit(1) + bit(2)


def put_piece(place, outs, order, part, piece, value):
    low = value.shape[0]
    at = slice(part * low, (part + 1) * low)
    sent, k = piece_slot(place, piece, order)

    @pl.when(sent == 0)
    def _():
        outs[0][k, at] = value

    @pl.when(sent == 1)
    def _():
        outs[1][k, at] = value


def take_pieces(place, refs, order, staged):
    for piece in range(8):
        sent, k = piece_slot(place, piece, order)

        @pl.when(sent == 0)
        def _():
            staged[piece] = refs[0][k]

        @pl.when(sent == 1)
        def _():
            staged[piece] = refs[1][k]


def square_grads_kernel(place, left_ref, *refs, order, terms):
    rights, outs = refs[:terms], refs[terms:]
    half = D // 2
    low = half // 2
    size = left_ref.shape[1] // terms
    for i in range(2):
        for j in range(2):
            value = sum(
                lax.dot_general(
                    left_ref[0, k * size : (k + 1) * size, i * half : (i + 1) * half],
                    right[:, j * half : (j + 1) * half],
                    ON_ROWS,
                    preferred_element_type=f32,
                )
                for k, right in enumerate(rights)
            ).astype(bf16)
            for part in range(2):
                piece = 4 * i + 2 * j + part
                put_piece(place, outs, order, 0, piece, value[part * low : (part + 1) * low])


def square_grads(place, fed, which, rights, order):
    rows = fed.shape[1]
    if which:
        arrays, specs = halves_of(rights, rows // 2)
    else:
        arrays, specs = tuple(rights), [whole(rights[0].shape)]
    left = pl.BlockSpec((1, rows, D), lambda *_: (which, 0, 0))
    return pieces_call(
        functools.partial(square_grads_kernel, order=order, terms=len(arrays)),
        "down_grads" if which else "up_grads",
        place,
        (fed, *arrays),
        (D // 4, D // 2),
        2 * rows * D * D,
        [left, *specs],
    )


def pieces_call(kernel, name, place, arrays, shape, flops, specs=None):
    return pl.pallas_call(
        kernel,
        grid_spec=pltpu.PrefetchScalarGridSpec(
            num_scalar_prefetch=1,
            grid=(1,),
            in_specs=specs or [whole(array.shape) for array in arrays],
            out_specs=[whole((4,) + shape)] * 2,
        ),
        out_shape=[jax.ShapeDtypeStruct((4,) + shape, bf16)] * 2,
        compiler_params=params(14),
        cost_estimate=cost(flops, 2 * sum(array.size for array in arrays)),
        name=name,
    )(place, *arrays)


def mix_grads_kernel(place, *refs, arrays, groups, order):
    sources, outs = refs[:arrays], refs[arrays:]
    half = D // 2
    parts = 8 // len(groups)
    for j in range(2):
        at = slice(j * half, (j + 1) * half)
        products = {}
        for g, (left, right, first) in enumerate(groups):
            if left not in products:
                heads = sources[left].shape[0]
                products[left] = [
                    lax.dot_general(
                        sources[left][h],
                        sources[right][:, at],
                        ON_ROWS,
                        preferred_element_type=f32,
                    ).astype(bf16)
                    for h in range(heads)
                ]
            value = jnp.concatenate(
                [product[first : first + HD] for product in products[left]], axis=0
            )
            low = value.shape[0] // parts
            for part in range(parts):
                piece = parts * g + part
                put_piece(place, outs, order, j, piece, value[part * low : (part + 1) * low])


def mix_grads(place, arrays, groups, order):
    heads, rows, _ = arrays[0].shape
    return pieces_call(
        functools.partial(mix_grads_kernel, arrays=len(arrays), groups=groups, order=order),
        "mix_grads",
        place,
        arrays,
        (heads * HD * len(groups) // 4, D // 2),
        2 * len(groups) * rows * D * heads * WIDE,
    )


def square_place_kernel(place, *refs, order):
    out, staged = refs[-2:]
    half = D // 2
    low = half // 2
    take_pieces(place, refs[:2], order, staged)
    for piece in range(8):
        i, j, part = piece // 4, (piece // 2) % 2, piece % 2
        top = i * half + part * low
        out[0, top : top + low, j * half : (j + 1) * half] = staged[piece].astype(f32)


def mix_place_kernel(place, *refs, bundles):
    first_staged = len(refs) - len(bundles)
    qkv_ref, out_ref = refs[first_staged - 2 : first_staged]
    half = D // 2
    for i, (order, groups) in enumerate(bundles):
        staged = refs[first_staged + i]
        take_pieces(place, refs[2 * i : 2 * i + 2], order, staged)
        parts = 8 // len(groups)
        low = staged.shape[1] // 2
        for j in range(2):
            columns_at = slice(j * half, (j + 1) * half)
            for piece in range(8):
                g, part = groups[piece // parts], piece % parts
                rows = slice(part * low, (part + 1) * low)
                value = staged[piece, j * low : (j + 1) * low].astype(f32)
                if g < 3:
                    qkv_ref[0, g, rows, columns_at] = value
                else:
                    out_ref[0, rows, columns_at] = value


def place_call(kernel, name, place, bundles, earlier, shapes, layer):
    arrays = [array for bundle in bundles for array in bundle]
    specs = [
        pl.BlockSpec((1,) + shape, lambda *_, rank=len(shape): (layer,) + (0,) * rank)
        for shape in shapes
    ]
    kept = [pl.BlockSpec(memory_space=pl.ANY)] * len(earlier)
    size = sum(array.size for array in arrays)
    return pl.pallas_call(
        kernel,
        grid_spec=pltpu.PrefetchScalarGridSpec(
            num_scalar_prefetch=1,
            grid=(1,),
            in_specs=[whole(array.shape) for array in arrays] + kept,
            out_specs=specs,
            scratch_shapes=[pltpu.VMEM((8,) + bundle[0].shape[1:], bf16) for bundle in bundles],
        ),
        out_shape=[jax.ShapeDtypeStruct((LAYERS,) + shape, f32) for shape in shapes],
        input_output_aliases={1 + len(arrays) + i: i for i in range(len(earlier))},
        compiler_params=params(18),
        cost_estimate=cost(size, 6 * size),
        name=name,
    )(place, *arrays, *earlier)


def columns_kernel(place, *refs):
    pieces, out = refs[:2], refs[2]
    size = pieces[0].shape[0]
    width = out.shape[0]
    for p in range(4):

        @pl.when(place[0] == p)
        def _():
            for k in range(2):
                part = pieces[k][:, p * width : (p + 1) * width].astype(f32)
                q = (p & 1) ^ k
                out[:, q * size : (q + 1) * size] = jnp.transpose(part).astype(bf16)


def columns(place, pieces):
    half = pieces[0].shape[0]
    return pl.pallas_call(
        columns_kernel,
        grid_spec=pltpu.PrefetchScalarGridSpec(
            num_scalar_prefetch=1,
            grid=(1,),
            in_specs=[whole((half, D))] * 2,
            out_specs=whole((D // 4, 2 * half)),
        ),
        out_shape=jax.ShapeDtypeStruct((D // 4, 2 * half), bf16),
        compiler_params=params(8),
        cost_estimate=cost(half * D, 8 * half * D),
        name="columns",
    )(place, *pieces)


def on_device(
    residual_in,
    cotangent,
    w_qkv,
    b_qv,
    w_out,
    b_out,
    w_up,
    b_up,
    w_down,
    b_down,
    ln_gain,
    ln_bias,
    selection,
    lengths,
    valid,
):
    rows = residual_in.shape[0]
    heads = selection.shape[0]
    blocks = rows // QB
    half = rows // 2
    count = lax.axis_size("tok")
    position = lax.axis_index("tok")
    member = lax.axis_index("head")
    width = D // 4
    first_row = position * rows
    chosen = lax.dynamic_slice_in_dim(selection, position * blocks, blocks, 1).reshape(heads, -1)
    per_device = rows // KB
    starts = slot_of(chosen // per_device, position, count) * rows + (chosen % per_device) * KB
    place = jnp.stack(
        [
            member,
            position,
            lengths[0],
            slot_of(position, position, count) * rows,
            slot_of(jnp.maximum(position - 1, 0), position, count) * rows,
            position if ring_form(count) else 0,
        ]
    ).astype(jnp.int32)

    first_pieces = share_features(residual_in.T)
    small = jnp.concatenate(
        [ln_gain.reshape(-1, width), ln_bias.reshape(-1, width), b_out, b_down], axis=0
    )
    small = jnp.pad(small, ((0, 128 - small.shape[0]), (0, 0)))
    param_pieces = share_features(small.T)

    split = jnp.transpose(w_qkv, (0, 2, 3, 1)).reshape(LAYERS, 3, heads, HD, D)
    w_all = jnp.concatenate(
        [
            jnp.pad(split[:, 0], ((0, 0), (0, 0), (0, WIDE - HD), (0, 0))),
            jnp.concatenate([split[:, 1], split[:, 2]], axis=2),
        ],
        axis=1,
    ).reshape(LAYERS, 2 * heads * WIDE, D)
    b_split = b_qv.reshape(LAYERS, 2, heads, HD)
    b_all = (
        jnp.concatenate(
            [
                jnp.pad(b_split[:, 0], ((0, 0), (0, 0), (0, HD))),
                jnp.pad(b_split[:, 1], ((0, 0), (0, 0), (HD, 0))),
            ],
            axis=1,
        )
        .reshape(LAYERS, 1, 2 * heads * WIDE)
        .astype(f32)
    )
    w_mix = jnp.pad(
        w_out.reshape(LAYERS, heads, HD, D), ((0, 0), (0, 0), (HD, 0), (0, 0))
    ).reshape(LAYERS, heads * WIDE, D)
    b_inner = b_up.astype(f32)

    far_valid = jnp.tile(valid.reshape(-1, KB), (1, SEL)).astype(f32)
    padded = jnp.concatenate([jnp.zeros((WINDOW,), jnp.int32), valid])
    near = lax.dynamic_slice_in_dim(padded, first_row, rows + WINDOW).reshape(-1, WINDOW)
    near_valid = jnp.concatenate([near[:-1], near[1:]], axis=1).astype(f32)
    own_valid = lax.dynamic_slice_in_dim(valid, first_row + (member & 1) * half, half)
    own_valid = own_valid.astype(f32)[:, None]
    mask = masks(place, chosen, near_valid, far_valid, heads, rows)

    pieces = first_pieces
    lows = []
    kept = []
    squares = []
    for l in range(LAYERS):
        normed, queries, *own_kv = project(
            place, pieces, None if l else param_pieces, w_all[l], b_all[l], rows, heads
        )
        if l == 0:
            own_kv, (low_first, param) = own_kv[:2], own_kv[2:]
            residual = low_first
        parts = gather_blocks(own_kv)
        mixed, probs, *pieces = attend(place, starts, queries, w_mix[l], mask, parts, count)
        residual, low_second, normed_own, branch_squares = add_norm(
            place, sum_rows(pieces), residual, param, own_valid, rows, B_OUT + l, 2 * l + 1
        )
        fed, slope, *pieces = feed(
            place, share_rows(normed_own), w_up[l], b_inner[l : l + 1], w_down[l]
        )
        residual, low_next, normed_own, second_squares = add_norm(
            place,
            sum_rows(pieces),
            residual,
            param,
            own_valid,
            rows,
            B_DOWN + l,
            2 * l + 2 if l + 1 < LAYERS else None,
        )
        squares.append((second_squares[1], branch_squares[0], second_squares[0]))
        kept.append((normed, queries, parts, mixed, probs, low_second, fed, slope))
        lows.append(low_next)
        if l + 1 < LAYERS:
            pieces = share_rows(normed_own)
    residual_out = columns(place, share_rows(lows[-1])).T

    gradient, sums_down = turn(place, share_features(cotangent.T))
    sums_down = sums_down[0]
    grad_pieces = (gradient,)
    grads = [None] * LAYERS
    placed_up = placed_down = placed_mix = ()
    shapes_mix = ((3, heads * HD, D), (heads * HD, D))
    for l in reversed(range(LAYERS)):
        last = l == 0
        normed, queries, parts, mixed, probs, low_second, fed, slope = kept[l]
        down = Bundle(square_grads(place, fed, 1, grad_pieces, COLUMN_FIRST), COLUMN_FIRST)
        down.send()
        inner, grad_b_up, *pieces = feed_back(place, grad_pieces, w_up[l], w_down[l], slope)
        up = Bundle(square_grads(place, fed, 0, (inner,), COLUMN_FIRST), COLUMN_FIRST)
        up.send()
        terms, _, _ = lax.optimization_barrier((sum_rows(pieces), up.out, down.out))
        terms = down.take(terms)
        if last:
            terms = mix_before.take(up_before.take(down_before.take(terms)))
            down_before.send()
            up_before.send()
        gradient, low, second_sums = norm_back(
            place, terms, low_second, gradient, param, rows, 2 * l + 1
        )
        pieces = share_rows(low)
        dq, branch_full, *kv_grads = attend_back(
            place, starts, queries, probs, w_mix[l], pieces, parts, count
        )
        kv_grads = up.take(kv_grads)
        if last:
            kv_grads = up_before.take(down_before.take(kv_grads))
        kv_terms = return_blocks(kv_grads, lambda other: other)
        if last:
            kv_terms, residual_out = lax.optimization_barrier((kv_terms, residual_out))
        dkv, bias_sums, first_sums, *pieces = project_back(
            place, dq, w_all[l], normed, param, kv_terms, 2 * l
        )
        if not last:
            down.send(dkv)
            up.send(dkv)
        groups = ((0, 3, 0), (1, 3, 0), (1, 3, HD), (2, 4, HD))
        mix_pieces = mix_grads(
            place, (dq, dkv, mixed, normed, branch_full), groups, COLUMN_FIRST
        )
        mix = Bundle(mix_pieces, COLUMN_FIRST)
        if last:
            finish_in_turn(dkv, down_before, up_before, mix_before, down, up, mix)
        else:
            mix.send()
        terms, _ = lax.optimization_barrier((sum_rows(pieces), mix_pieces))
        if not last:
            terms = up.take(down.take(terms))
            down.send()
            up.send()
            down_before, up_before, mix_before = down, up, mix
        gradient, low, low_sums = norm_back(
            place, terms, lows[l - 1] if l else low_first, gradient, param, rows, 2 * l
        )
        pieces = share_rows(low)
        if not last:
            pieces = mix.take(pieces)
            mix.send()
        grad_pieces = pieces
        grads[l] = (
            None,
            grad_b_up[0],
            jnp.concatenate(
                [
                    bias_sums[:heads, :HD].reshape(-1),
                    bias_sums[heads:, HD:].reshape(-1),
                    jnp.zeros((D - 2 * heads * HD,), f32),
                ]
            ),
            None,
            None,
            second_sums[2],
            sums_down,
            first_sums,
            second_sums,
        )
        sums_down = low_sums[2]
    grad_residual = columns(place, pieces).T
    for l, bundles in ((1, (down_before, up_before, mix_before)), (0, (down, up, mix))):
        placed_down, placed_up = [
            place_call(
                functools.partial(square_place_kernel, order=COLUMN_FIRST),
                name,
                place,
                [bundle.finish()],
                placed,
                ((D, D),),
                l,
            )
            for name, bundle, placed in (
                ("down_place", bundles[0], placed_down),
                ("up_place", bundles[1], placed_up),
            )
        ]
        done = bundles[2].finish()
        if l == 0:
            done, placed_down, placed_up, placed_mix = lax.optimization_barrier(
                (done, placed_down, placed_up, placed_mix)
            )
        placed_mix = place_call(
            functools.partial(mix_place_kernel, bundles=((COLUMN_FIRST, (0, 1, 2, 3)),)),
            "mix_place",
            place,
            [done],
            placed_mix,
            shapes_mix,
            l,
        )

    first = jnp.concatenate([grads[l][7] for l in range(LAYERS)], axis=0)
    first = first + swap(first, "head", 2)
    over_all = jnp.concatenate(
        [first]
        + [grads[l][8][:2] for l in range(LAYERS)]
        + [jnp.stack([grads[l][5] for l in range(LAYERS)])]
        + [jnp.stack([grads[l][6] for l in range(LAYERS)])]
        + [jnp.stack([vector for layer in squares for vector in layer])],
        axis=0,
    )
    over_tok = jnp.stack(
        [grads[l][1] for l in range(LAYERS)] + [grads[l][2] for l in range(LAYERS)]
    )
    packed = small_sum(
        jnp.concatenate([over_all + swap(over_all, "head", 1), over_tok], axis=0), "tok"
    )
    stat_row = 4 * LAYERS + 2 * LAYERS
    tok_row = stat_row + 3 * LAYERS
    mine = lax.dynamic_slice_in_dim(packed[:stat_row], member * width, width, 1)
    norms = mine[: 4 * LAYERS].reshape(2, LAYERS, 2, width)
    grad_ln_gain = jnp.stack([norms[0, :, 0], norms[1, :, 0]], axis=1)
    grad_ln_bias = jnp.stack([norms[0, :, 1], norms[1, :, 1]], axis=1)
    grad_b_out = mine[4 * LAYERS : 5 * LAYERS]
    grad_b_down = mine[5 * LAYERS : 6 * LAYERS]
    square_sums = jnp.sum(packed[stat_row:tok_row], axis=-1).reshape(LAYERS, 3)
    valid_count = jnp.maximum(jnp.sum(valid.astype(f32)), 1.0)
    statistics = jnp.sqrt(square_sums / (valid_count * D))
    grad_b_up = packed[tok_row : tok_row + LAYERS]
    grad_b_qv = packed[tok_row + LAYERS :, : 2 * heads * HD].reshape(LAYERS, 2, heads * HD)
    return (
        residual_out,
        grad_residual,
        jnp.transpose(placed_mix[0], (0, 3, 1, 2)),
        grad_b_qv,
        placed_mix[1],
        grad_b_out,
        placed_up[0],
        grad_b_up,
        placed_down[0],
        grad_b_down,
        grad_ln_gain,
        grad_ln_bias,
        statistics,
    )


def solution(mesh):
    in_specs = (
        P("tok", "head"),
        P("tok", "head"),
        P(None, None, None, "head"),
        P(None, None, "head"),
        P(None, "head", None),
        P(None, "head"),
        P(None, None, "head"),
        P(None, "head"),
        P(None, "head", None),
        P(None, "head"),
        P(None, None, "head"),
        P(None, None, "head"),
        P("head", None, None),
        P(),
        P(),
    )
    out_specs = (
        P("tok", "head"),
        P("tok", "head"),
        P(None, None, None, "head"),
        P(None, None, "head"),
        P(None, "head", None),
        P(None, "head"),
        P(None, None, "head"),
        P(None, "head"),
        P(None, "head", None),
        P(None, "head"),
        P(None, None, "head"),
        P(None, None, "head"),
        P(),
    )
    return jax.shard_map(
        on_device, mesh=mesh, in_specs=in_specs, out_specs=out_specs, check_vma=False
    )
```

time: 560 us -> 515 us (0.920)
  the two profiles are of different devices: /device:TPU:0 before, /device:TPU:7 now
where the time goes in v3:
time: 515 us; the launch traced here: 506 us
  waiting for transfers between devices  189 us (37%)
  starting transfers between devices  140 us (27%)
  Pallas kernels  118 us (23%)
  local copies, waits for them, and re-layouts  45.9 us (9%)
  other arithmetic  9.7 us (2%)
    ppermute x106, waiting for transfers between devices, swap(): lax.ppermute(value, axis, [(i, i ^ step) for i in range(lax.axis_size(axi...  162 us
    ppermute x106, starting transfers between devices, swap(): lax.ppermute(value, axis, [(i, i ^ step) for i in range(lax.axis_size(axi...  120 us
    unnamed x211, local copies, waits for them, and re-layouts  28.6 us
    ppermute x24, waiting for transfers between devices, rotate(): lax.ppermute(value, axis, [(i, (i + step) % count) for i in range(count)])  26.4 us
    ppermute x24, starting transfers between devices, rotate(): lax.ppermute(value, axis, [(i, (i + step) % count) for i in range(count)])  20.4 us
    pallas_call x2, Pallas kernels, attend_back(): pl.pallas_call(functools.partial(attend_back_kernel, heads=heads, count=c...  19.4 us
    pallas_call x6, Pallas kernels, place_call(): pl.pallas_call(kernel, grid_spec=pltpu.PrefetchScalarGridSpec(num_scalar_...  18.2 us
    pallas_call x6, Pallas kernels, pieces_call(): pl.pallas_call(kernel, grid_spec=pltpu.PrefetchScalarGridSpec(num_scalar_...  16.9 us
  transfers between devices with their start and end apart: 130, of which 67 were waited for; matrix products, arithmetic and copies ran while one was open for 5% of the time, Pallas kernels for 16%

profile of v3, /device:TPU:7, one launch (start us, length us, event | category | flops | bytes accessed | tf_op | source)
XLA Modules:
  0.0 505.9 jit_solution(14323446201554272903)
XLA Ops:
  46.3 5.1 %collective-permute-done.18.refs_17_.refs_19_ = bf16[3,256,128]{2,1,0:T(8,128)(2,1)S(1)} collective-permute-done((bf16[3,256,128]{2,1,0:T(8,128)(2,1)}, bf16[3,256,128]{2,1,0:T(8,128)(2,1)S(1)}, u32[]{:S(2)}, u32[]{:S(2)}) %collective-permute-start.18) | collective-permute-done | bytes 196640 | tf_op jit(solution)/shard_map/ppermute | solution.py:38
  54.3 6.6 %attend.2 = (bf16[3,512,128]{2,1,0:T(8,128)(2,1)S(1)}, bf16[3,512,192]{2,1,0:T(8,128)(2,1)S(1)}, bf16[256,768]{1,0:T(8,128)(2,1)S(1)}, bf16[256,768]{1,0:T(8,128)(2,1)S(1)}) custom-call(s32[6]{0:T(128)S(1)} %stack.29.place, s32[3,32]{1,0:T(4,128)S(1)} %fusion.7.starts, bf16[3,512,128]{2,1,0:T(8,128)(2,1)S(1)} %copy-done.8, bf16[384,768]{1,0:T(8,128)(2,1)S(1)} %bitcast.65, ...), custom_call_target="tpu_custom_call" | custom-call | flops 503316480 | bytes 4718592 | tf_op jit(solution)/shard_map/attend/pallas_call | solution.py:486
  68.3 8.8 %collective-permute-done.21.refs_1_ = bf16[256,768]{1,0:T(8,128)(2,1)} collective-permute-done((bf16[256,768]{1,0:T(8,128)(2,1)}, bf16[256,768]{1,0:T(8,128)(2,1)}, u32[]{:S(2)}, u32[]{:S(2)}) %collective-permute-start.21) | collective-permute-done | bytes 393248 | tf_op jit(solution)/shard_map/ppermute | solution.py:38
  88.3 10.2 %collective-permute-done.24.refs_1_ = bf16[256,768]{1,0:T(8,128)(2,1)S(1)} collective-permute-done((bf16[256,768]{1,0:T(8,128)(2,1)S(1)}, bf16[256,768]{1,0:T(8,128)(2,1)S(1)}, u32[]{:S(2)}, u32[]{:S(2)}) %collective-permute-start.24) | collective-permute-done | bytes 393248 | tf_op jit(solution)/shard_map/ppermute | solution.py:38
  105.2 4.5 collective-permute-done.28.refs_6_.refs_8_
  135.9 5.3 %collective-permute-done.38.refs_17_.refs_19_ = bf16[3,256,128]{2,1,0:T(8,128)(2,1)S(1)} collective-permute-done((bf16[3,256,128]{2,1,0:T(8,128)(2,1)S(1)}, bf16[3,256,128]{2,1,0:T(8,128)(2,1)S(1)}, u32[]{:S(2)}, u32[]{:S(2)}) %collective-permute-start.38) | collective-permute-done | bytes 196640 | tf_op jit(solution)/shard_map/ppermute | solution.py:38
  141.1 8.3 %attend.3 = (bf16[3,512,128]{2,1,0:T(8,128)(2,1)S(1)}, bf16[3,512,192]{2,1,0:T(8,128)(2,1)S(1)}, bf16[256,768]{1,0:T(8,128)(2,1)S(1)}, bf16[256,768]{1,0:T(8,128)(2,1)S(1)}) custom-call(s32[6]{0:T(128)S(1)} %stack.29.place, s32[3,32]{1,0:T(4,128)S(1)} %fusion.7.starts, bf16[3,512,128]{2,1,0:T(8,128)(2,1)S(1)} %get-tuple-element.412.refs_0_, ...), custom_call_target="tpu_custom_call" | custom-call | flops 503316480 | bytes 4718592 | tf_op jit(solution)/shard_map/attend/pallas_call | solution.py:486
  155.5 8.9 %collective-permute-done.41.refs_1_ = bf16[256,768]{1,0:T(8,128)(2,1)S(1)} collective-permute-done((bf16[256,768]{1,0:T(8,128)(2,1)S(1)}, bf16[256,768]{1,0:T(8,128)(2,1)S(1)}, u32[]{:S(2)}, u32[]{:S(2)}) %collective-permute-start.41) | collective-permute-done | bytes 393248 | tf_op jit(solution)/shard_map/ppermute | solution.py:38
  183.8 6.3 %collective-permute-done.49.refs_1_ = bf16[256,768]{1,0:T(8,128)(2,1)S(1)} collective-permute-done((bf16[256,768]{1,0:T(8,128)(2,1)S(1)}, bf16[256,768]{1,0:T(8,128)(2,1)S(1)}, u32[]{:S(2)}, u32[]{:S(2)}) %collective-permute-start.49) | collective-permute-done | bytes 393248 | tf_op jit(solution)/shard_map/ppermute | solution.py:38
  190.1 4.2 collective-permute-done.47.came
  198.5 10.5 %attend_back.2 = (bf16[3,512,128]{2,1,0:T(8,128)(2,1)S(1)}, bf16[512,768]{1,0:T(8,128)(2,1)S(1)}, bf16[3,256,128]{2,1,0:T(8,128)(2,1)S(1)}, bf16[3,256,128]{2,1,...) custom-call(s32[6]{0:T(128)S(1)} %stack.29.place, ...), custom_call_target="tpu_custom_call" | custom-call | flops 905969664 | bytes 9437184 | tf_op jit(solution)/shard_map/attend_back/pallas_call | solution.py:578
  210.5 4.6 collective-permute-done.58
  215.5 3.8 collective-permute-done.51
  219.9 3.7 collective-permute-done.59
  224.0 3.8 collective-permute-done.52
  228.2 3.8 collective-permute-done.60
  232.4 3.8 collective-permute-done.53
  254.8 4.6 collective-permute-done.68.refs_1_
  259.3 4.4 collective-permute-done.65.came
  278.1 11.7 %collective-permute-done.73.came = bf16[4,192,384]{2,1,0:T(8,128)(2,1)S(1)} collective-permute-done((bf16[4,192,384]{2,1,0:T(8,128)(2,1)S(1)}, bf16[4,192,384]{2,1,0:T(8,128)(2,1)S(1)}, u32[]{:S(2)}, u32[]{:S(2)}) %collective-permute-start.73) | collective-permute-done | bytes 589856 | tf_op jit(solution)/shard_map/ppermute | solution.py:38
  292.8 6.7 %collective-permute-done.69.came = bf16[1,192,384]{2,1,0:T(8,128)(2,1)S(1)} collective-permute-done((bf16[1,192,384]{2,1,0:T(8,128)(2,1)S(1)}, bf16[1,192,384]{2,1,0:T(8,128)(2,1)S(1)}, u32[]{:S(2)}, u32[]{:S(2)}) %collective-permute-start.69) | collective-permute-done | bytes 147488 | tf_op jit(solution)/shard_map/ppermute | solution.py:38
  306.2 8.9 %attend_back.3 = (bf16[3,512,128]{2,1,0:T(8,128)(2,1)S(1)}, bf16[512,768]{1,0:T(8,128)(2,1)S(1)}, bf16[3,256,128]{2,1,0:T(8,128)(2,1)S(1)}, bf16[3,256,128]{2,1,...) custom-call(s32[6]{0:T(128)S(1)} %stack.29.place, ...), custom_call_target="tpu_custom_call" | custom-call | flops 905969664 | bytes 9437184 | tf_op jit(solution)/shard_map/attend_back/pallas_call | solution.py:578
  367.6 4.3 mix_grads.3
  381.2 4.6 collective-permute-start.126
  385.8 3.4 collective-permute-done.112.came
  402.9 4.1 collective-permute-done.128
  409.7 3.6 collective-permute-start.98
  417.3 3.7 collective-permute-done.129
  430.9 6.6 %collective-permute-start.123 = (bf16[4,192,384]{2,1,0:T(8,128)(2,1)S(1)}, bf16[4,192,384]{2,1,0:T(8,128)(2,1)}, u32[]{:S(2)}, u32[]{:S(2)}) collective-permute-start(bf16[4,192,384]{2,1,0:T(8,128)(2,1)S(1)} %merge.58.refs_0_), channel_id=1, source_target_pairs={{0,1},{1,0},{2,3},{3,2},{4,5},{5,4},{6,7},{7,6},{8,9},{9,8},{10,11... | collective-permute-start | bytes 1769480 | tf_op jit(solution)/shard_map/ppermute | solution.py:38
  445.2 4.0 collective-permute-done.122.came
  462.9 17.1 %collective-permute-start.100 = (bf16[256,768]{1,0:T(8,128)(2,1)}, bf16[256,768]{1,0:T(8,128)(2,1)S(1)}, u32[]{:S(2)}, u32[]{:S(2)}) collective-permute-start(bf16[256,768]{1,0:T(8,128)(2,1)} %get-tuple-element.658.refs_0_), channel_id=1, source_target_pairs={{0,8},{8,0},{16,24},{24,16},{1,9},{9,1},{17,25},{25,17},{2,10},{10... | collective-permute-start | bytes 1179656 | tf_op jit(solution)/shard_map/ppermute | solution.py:38
  498.6 3.5 up_place.3
  (597 shorter events, 309.2 us)
Async XLA Ops:
  154.4 14.2 %collective-permute-start.43 = (bf16[192,512]{1,0:T(8,128)(2,1)S(1)}, bf16[192,512]{1,0:T(8,128)(2,1)S(1)}, u32[]{:S(2)}, u32[]{:S(2)}) collective-permute-start(bf16[192,512]{1,0:T(8,128)(2,1)S(1)} %bitcast.73), channel_id=1, source_target_pairs={{0,16},{8,24},{16,0},{24,8},{1,17},{9,25},{17,1},{25,9},{2,18},{10... | collective-permute-start | bytes 589832 | tf_op jit(solution)/shard_map/ppermute | solution.py:38
  179.4 14.8 %collective-permute-start.47 = (bf16[4,192,384]{2,1,0:T(8,128)(2,1)S(1)}, bf16[4,192,384]{2,1,0:T(8,128)(2,1)S(1)}, u32[]{:S(2)}, u32[]{:S(2)}) collective-permute-start(bf16[4,192,384]{2,1,0:T(8,128)(2,1)S(1)} %get-tuple-element.444), channel_id=1, source_target_pairs={{0,1},{1,0},{2,3},{3,2},{4,5},{5,4},{6,7},{7,6},{8,9},{9,8},{10,11... | collective-permute-start | bytes 1769480 | tf_op jit(solution)/shard_map/ppermute | solution.py:38
  182.4 26.5 %collective-permute-start.46 = (bf16[4,192,384]{2,1,0:T(8,128)(2,1)S(1)}, bf16[4,192,384]{2,1,0:T(8,128)(2,1)S(1)}, u32[]{:S(2)}, u32[]{:S(2)}) collective-permute-start(bf16[4,192,384]{2,1,0:T(8,128)(2,1)S(1)} %get-tuple-element.442), channel_id=1, source_target_pairs={{0,1},{1,0},{2,3},{3,2},{4,5},{5,4},{6,7},{7,6},{8,9},{9,8},{10,11... | collective-permute-start | bytes 1769480 | tf_op jit(solution)/shard_map/ppermute | solution.py:38
  249.8 14.0 %collective-permute-start.65 = (bf16[2,192,384]{2,1,0:T(8,128)(2,1)S(1)}, bf16[2,192,384]{2,1,0:T(8,128)(2,1)S(1)}, u32[]{:S(2)}, u32[]{:S(2)}) collective-permute-start(bf16[2,192,384]{2,1,0:T(8,128)(2,1)S(1)} %get-tuple-element.504), channel_id=1, source_target_pairs={{0,2},{1,3},{2,0},{3,1},{4,6},{5,7},{6,4},{7,5},{8,10},{9,11},{10,... | collective-permute-start | bytes 884744 | tf_op jit(solution)/shard_map/ppermute | solution.py:38
  274.8 15.0 %collective-permute-start.73 = (bf16[4,192,384]{2,1,0:T(8,128)(2,1)S(1)}, bf16[4,192,384]{2,1,0:T(8,128)(2,1)S(1)}, u32[]{:S(2)}, u32[]{:S(2)}) collective-permute-start(bf16[4,192,384]{2,1,0:T(8,128)(2,1)S(1)} %get-tuple-element.534), channel_id=1, source_target_pairs={{0,1},{1,0},{2,3},{3,2},{4,5},{5,4},{6,7},{7,6},{8,9},{9,8},{10,11... | collective-permute-start | bytes 1769480 | tf_op jit(solution)/shard_map/ppermute | solution.py:38
  275.2 17.3 %collective-permute-start.75 = (bf16[256,768]{1,0:T(8,128)(2,1)S(1)}, bf16[256,768]{1,0:T(8,128)(2,1)S(1)}, u32[]{:S(2)}, u32[]{:S(2)}) collective-permute-start(bf16[256,768]{1,0:T(8,128)(2,1)S(1)} %add_convert_fusion.2.refs_0_), channel_id=1, source_target_pairs={{0,16},{8,24},{16,0},{24,8},{1,17},{9,25},{17,1},{25,9},{2,18},{10... | collective-permute-start | bytes 1179656 | tf_op jit(solution)/shard_map/ppermute | solution.py:38
  276.4 25.8 %collective-permute-start.95 = (bf16[256,768]{1,0:T(8,128)(2,1)S(1)}, bf16[256,768]{1,0:T(8,128)(2,1)S(1)}, u32[]{:S(2)}, u32[]{:S(2)}) collective-permute-start(bf16[256,768]{1,0:T(8,128)(2,1)S(1)} %get-tuple-element.636), channel_id=1, source_target_pairs={{0,8},{8,0},{16,24},{24,16},{1,9},{9,1},{17,25},{25,17},{2,10},{10... | collective-permute-start | bytes 1179656 | tf_op jit(solution)/shard_map/ppermute | solution.py:38
  277.1 22.3 %collective-permute-start.79 = (bf16[2,192,384]{2,1,0:T(8,128)(2,1)S(1)}, bf16[2,192,384]{2,1,0:T(8,128)(2,1)S(1)}, u32[]{:S(2)}, u32[]{:S(2)}) collective-permute-start(bf16[2,192,384]{2,1,0:T(8,128)(2,1)S(1)} %get-tuple-element.551), channel_id=1, source_target_pairs={{0,2},{1,3},{2,0},{3,1},{4,6},{5,7},{6,4},{7,5},{8,10},{9,11},{10,... | collective-permute-start | bytes 884744 | tf_op jit(solution)/shard_map/ppermute | solution.py:38
  277.4 15.4 %collective-permute-start.70 = (bf16[1,192,384]{2,1,0:T(8,128)(2,1)S(1)}, bf16[1,192,384]{2,1,0:T(8,128)(2,1)S(1)}, u32[]{:S(2)}, u32[]{:S(2)}) collective-permute-start(bf16[1,192,384]{2,1,0:T(8,128)(2,1)S(1)} %get-tuple-element.525), channel_id=1, source_target_pairs={{0,4},{1,5},{2,6},{3,7},{4,0},{5,1},{6,2},{7,3},{8,12},{9,13},{10,... | collective-permute-start | bytes 442376 | tf_op jit(solution)/shard_map/ppermute | solution.py:38
  292.5 22.6 %collective-permute-start.78 = (bf16[4,192,384]{2,1,0:T(8,128)(2,1)S(1)}, bf16[4,192,384]{2,1,0:T(8,128)(2,1)S(1)}, u32[]{:S(2)}, u32[]{:S(2)}) collective-permute-start(bf16[4,192,384]{2,1,0:T(8,128)(2,1)S(1)} %get-tuple-element.539), channel_id=1, source_target_pairs={{0,1},{1,0},{2,3},{3,2},{4,5},{5,4},{6,7},{7,6},{8,9},{9,8},{10,11... | collective-permute-start | bytes 1769480 | tf_op jit(solution)/shard_map/ppermute | solution.py:38
  302.3 17.1 %collective-permute-start.96 = (bf16[256,768]{1,0:T(8,128)(2,1)S(1)}, bf16[256,768]{1,0:T(8,128)(2,1)S(1)}, u32[]{:S(2)}, u32[]{:S(2)}) collective-permute-start(bf16[256,768]{1,0:T(8,128)(2,1)S(1)} %add_convert_fusion.1.refs_0_), channel_id=1, source_target_pairs={{0,16},{8,24},{16,0},{24,8},{1,17},{9,25},{17,1},{25,9},{2,18},{10... | collective-permute-start | bytes 1179656 | tf_op jit(solution)/shard_map/ppermute | solution.py:38
  303.6 14.3 %collective-permute-start.76 = (bf16[1,192,384]{2,1,0:T(8,128)(2,1)S(1)}, bf16[1,192,384]{2,1,0:T(8,128)(2,1)S(1)}, u32[]{:S(2)}, u32[]{:S(2)}) collective-permute-start(bf16[1,192,384]{2,1,0:T(8,128)(2,1)S(1)} %merge.34.kept), channel_id=1, source_target_pairs={{0,4},{1,5},{2,6},{3,7},{4,0},{5,1},{6,2},{7,3},{8,12},{9,13},{10,... | collective-permute-start | bytes 442376 | tf_op jit(solution)/shard_map/ppermute | solution.py:38
  321.3 28.4 %collective-permute-start.97 = (bf16[256,768]{1,0:T(8,128)(2,1)S(1)}, bf16[256,768]{1,0:T(8,128)(2,1)S(1)}, u32[]{:S(2)}, u32[]{:S(2)}) collective-permute-start(bf16[256,768]{1,0:T(8,128)(2,1)S(1)} %get-tuple-element.638.refs_0_), channel_id=1, source_target_pairs={{0,8},{8,0},{16,24},{24,16},{1,9},{9,1},{17,25},{25,17},{2,10},{10... | collective-permute-start | bytes 1179656 | tf_op jit(solution)/shard_map/ppermute | solution.py:38
  356.1 17.2 %collective-permute-start.105 = (bf16[2,192,384]{2,1,0:T(8,128)(2,1)S(1)}, bf16[2,192,384]{2,1,0:T(8,128)(2,1)S(1)}, u32[]{:S(2)}, u32[]{:S(2)}) collective-permute-start(bf16[2,192,384]{2,1,0:T(8,128)(2,1)S(1)} %merge.40.kept), channel_id=1, source_target_pairs={{0,2},{1,3},{2,0},{3,1},{4,6},{5,7},{6,4},{7,5},{8,10},{9,11},{10,... | collective-permute-start | bytes 884744 | tf_op jit(solution)/shard_map/ppermute | solution.py:38
  358.7 21.6 %collective-permute-start.125 = (f32[4,768]{1,0:T(4,128)S(1)}, f32[4,768]{1,0:T(4,128)}, u32[]{:S(2)}, u32[]{:S(2)}) collective-permute-start(f32[4,768]{1,0:T(4,128)S(1)} %pad_maximum_fusion), channel_id=1, source_target_pairs={{0,16},{8,24},{16,0},{24,8},{1,17},{9,25},{17,1},{25,9},{2,18},{10... | collective-permute-start | bytes 36872 | tf_op jit(solution)/shard_map/ppermute | solution.py:38
  359.1 19.9 %collective-permute-start.111 = (bf16[2,192,384]{2,1,0:T(8,128)(2,1)S(1)}, bf16[2,192,384]{2,1,0:T(8,128)(2,1)}, u32[]{:S(2)}, u32[]{:S(2)}) collective-permute-start(bf16[2,192,384]{2,1,0:T(8,128)(2,1)S(1)} %merge.46.kept), channel_id=1, source_target_pairs={{0,2},{1,3},{2,0},{3,1},{4,6},{5,7},{6,4},{7,5},{8,10},{9,11},{10,... | collective-permute-start | bytes 884744 | tf_op jit(solution)/shard_map/ppermute | solution.py:38
  361.3 14.5 %collective-permute-start.102 = (bf16[1,192,384]{2,1,0:T(8,128)(2,1)}, bf16[1,192,384]{2,1,0:T(8,128)(2,1)S(1)}, u32[]{:S(2)}, u32[]{:S(2)}) collective-permute-start(bf16[1,192,384]{2,1,0:T(8,128)(2,1)} %get-tuple-element.665), channel_id=1, source_target_pairs={{0,4},{1,5},{2,6},{3,7},{4,0},{5,1},{6,2},{7,3},{8,12},{9,13},{10,... | collective-permute-start | bytes 442376 | tf_op jit(solution)/shard_map/ppermute | solution.py:38
  371.9 24.4 %collective-permute-start.101 = (bf16[4,192,384]{2,1,0:T(8,128)(2,1)}, bf16[4,192,384]{2,1,0:T(8,128)(2,1)}, u32[]{:S(2)}, u32[]{:S(2)}) collective-permute-start(bf16[4,192,384]{2,1,0:T(8,128)(2,1)} %get-tuple-element.654), channel_id=1, source_target_pairs={{0,1},{1,0},{2,3},{3,2},{4,5},{5,4},{6,7},{7,6},{8,9},{9,8},{10,11... | collective-permute-start | bytes 1769480 | tf_op jit(solution)/shard_map/ppermute | solution.py:38
  374.1 17.1 %collective-permute-start.106 = (bf16[2,192,384]{2,1,0:T(8,128)(2,1)}, bf16[2,192,384]{2,1,0:T(8,128)(2,1)S(1)}, u32[]{:S(2)}, u32[]{:S(2)}) collective-permute-start(bf16[2,192,384]{2,1,0:T(8,128)(2,1)} %get-tuple-element.681), channel_id=1, source_target_pairs={{0,2},{1,3},{2,0},{3,1},{4,6},{5,7},{6,4},{7,5},{8,10},{9,11},{10,... | collective-permute-start | bytes 884744 | tf_op jit(solution)/shard_map/ppermute | solution.py:38
  379.0 16.2 %collective-permute-start.103 = (bf16[2,192,384]{2,1,0:T(8,128)(2,1)}, bf16[2,192,384]{2,1,0:T(8,128)(2,1)S(1)}, u32[]{:S(2)}, u32[]{:S(2)}) collective-permute-start(bf16[2,192,384]{2,1,0:T(8,128)(2,1)} %get-tuple-element.668), channel_id=1, source_target_pairs={{0,2},{1,3},{2,0},{3,1},{4,6},{5,7},{6,4},{7,5},{8,10},{9,11},{10,... | collective-permute-start | bytes 884744 | tf_op jit(solution)/shard_map/ppermute | solution.py:38
  389.2 20.4 %collective-permute-start.113 = (bf16[2,192,384]{2,1,0:T(8,128)(2,1)S(1)}, bf16[2,192,384]{2,1,0:T(8,128)(2,1)}, u32[]{:S(2)}, u32[]{:S(2)}) collective-permute-start(bf16[2,192,384]{2,1,0:T(8,128)(2,1)S(1)} %merge.48.kept), channel_id=1, source_target_pairs={{0,2},{1,3},{2,0},{3,1},{4,6},{5,7},{6,4},{7,5},{8,10},{9,11},{10,... | collective-permute-start | bytes 884744 | tf_op jit(solution)/shard_map/ppermute | solution.py:38
  395.9 30.5 %collective-permute-start.121 = (bf16[4,192,384]{2,1,0:T(8,128)(2,1)S(1)}, bf16[4,192,384]{2,1,0:T(8,128)(2,1)S(1)}, u32[]{:S(2)}, u32[]{:S(2)}) collective-permute-start(bf16[4,192,384]{2,1,0:T(8,128)(2,1)S(1)} %merge.56.refs_0_), channel_id=1, source_target_pairs={{0,1},{1,0},{2,3},{3,2},{4,5},{5,4},{6,7},{7,6},{8,9},{9,8},{10,11... | collective-permute-start | bytes 1769480 | tf_op jit(solution)/shard_map/ppermute | solution.py:38
  397.6 18.2 %collective-permute-start.104 = (bf16[2,192,384]{2,1,0:T(8,128)(2,1)S(1)}, bf16[2,192,384]{2,1,0:T(8,128)(2,1)S(1)}, u32[]{:S(2)}, u32[]{:S(2)}) collective-permute-start(bf16[2,192,384]{2,1,0:T(8,128)(2,1)S(1)} %get-tuple-element.672), channel_id=1, source_target_pairs={{0,2},{1,3},{2,0},{3,1},{4,6},{5,7},{6,4},{7,5},{8,10},{9,11},{10,... | collective-permute-start | bytes 884744 | tf_op jit(solution)/shard_map/ppermute | solution.py:38
  400.1 39.4 %collective-permute-start.118 = (bf16[4,192,384]{2,1,0:T(8,128)(2,1)S(1)}, bf16[4,192,384]{2,1,0:T(8,128)(2,1)S(1)}, u32[]{:S(2)}, u32[]{:S(2)}) collective-permute-start(bf16[4,192,384]{2,1,0:T(8,128)(2,1)S(1)} %merge.53.refs_0_), channel_id=1, source_target_pairs={{0,1},{1,0},{2,3},{3,2},{4,5},{5,4},{6,7},{7,6},{8,9},{9,8},{10,11... | collective-permute-start | bytes 1769480 | tf_op jit(solution)/shard_map/ppermute | solution.py:38
  409.7 31.7 %collective-permute-start.98 = (bf16[256,768]{1,0:T(8,128)(2,1)}, bf16[256,768]{1,0:T(8,128)(2,1)}, u32[]{:S(2)}, u32[]{:S(2)}) collective-permute-start(bf16[256,768]{1,0:T(8,128)(2,1)} %copy-done.85), channel_id=1, source_target_pairs={{0,8},{8,0},{16,24},{24,16},{1,9},{9,1},{17,25},{25,17},{2,10},{10... | collective-permute-start | bytes 1179656 | tf_op jit(solution)/shard_map/ppermute | solution.py:38
  421.0 18.4 %collective-permute-start.117 = (bf16[2,192,384]{2,1,0:T(8,128)(2,1)S(1)}, bf16[2,192,384]{2,1,0:T(8,128)(2,1)}, u32[]{:S(2)}, u32[]{:S(2)}) collective-permute-start(bf16[2,192,384]{2,1,0:T(8,128)(2,1)S(1)} %merge.52.kept), channel_id=1, source_target_pairs={{0,2},{1,3},{2,0},{3,1},{4,6},{5,7},{6,4},{7,5},{8,10},{9,11},{10,... | collective-permute-start | bytes 884744 | tf_op jit(solution)/shard_map/ppermute | solution.py:38
  427.2 16.2 %collective-permute-start.115 = (bf16[1,192,384]{2,1,0:T(8,128)(2,1)S(1)}, bf16[1,192,384]{2,1,0:T(8,128)(2,1)S(1)}, u32[]{:S(2)}, u32[]{:S(2)}) collective-permute-start(bf16[1,192,384]{2,1,0:T(8,128)(2,1)S(1)} %merge.50.kept), channel_id=1, source_target_pairs={{0,4},{1,5},{2,6},{3,7},{4,0},{5,1},{6,2},{7,3},{8,12},{9,13},{10,... | collective-permute-start | bytes 442376 | tf_op jit(solution)/shard_map/ppermute | solution.py:38
  430.9 18.3 %collective-permute-start.123 = (bf16[4,192,384]{2,1,0:T(8,128)(2,1)S(1)}, bf16[4,192,384]{2,1,0:T(8,128)(2,1)}, u32[]{:S(2)}, u32[]{:S(2)}) collective-permute-start(bf16[4,192,384]{2,1,0:T(8,128)(2,1)S(1)} %merge.58.refs_0_), channel_id=1, source_target_pairs={{0,1},{1,0},{2,3},{3,2},{4,5},{5,4},{6,7},{7,6},{8,9},{9,8},{10,11... | collective-permute-start | bytes 1769480 | tf_op jit(solution)/shard_map/ppermute | solution.py:38
  443.4 16.0 %collective-permute-start.99 = (bf16[256,768]{1,0:T(8,128)(2,1)}, bf16[256,768]{1,0:T(8,128)(2,1)}, u32[]{:S(2)}, u32[]{:S(2)}) collective-permute-start(bf16[256,768]{1,0:T(8,128)(2,1)} %add_convert_fusion.refs_0_), channel_id=1, source_target_pairs={{0,16},{8,24},{16,0},{24,8},{1,17},{9,25},{17,1},{25,9},{2,18},{10... | collective-permute-start | bytes 1179656 | tf_op jit(solution)/shard_map/ppermute | solution.py:38
  451.0 47.6 %collective-permute-start.124 = (bf16[4,192,384]{2,1,0:T(8,128)(2,1)}, bf16[4,192,384]{2,1,0:T(8,128)(2,1)}, u32[]{:S(2)}, u32[]{:S(2)}) collective-permute-start(bf16[4,192,384]{2,1,0:T(8,128)(2,1)} %merge.59.refs_0_), channel_id=1, source_target_pairs={{0,1},{1,0},{2,3},{3,2},{4,5},{5,4},{6,7},{7,6},{8,9},{9,8},{10,11... | collective-permute-start | bytes 1769480 | tf_op jit(solution)/shard_map/ppermute | solution.py:38
  456.4 45.8 %collective-permute-start.120 = (bf16[4,192,384]{2,1,0:T(8,128)(2,1)S(1)}, bf16[4,192,384]{2,1,0:T(8,128)(2,1)}, u32[]{:S(2)}, u32[]{:S(2)}) collective-permute-start(bf16[4,192,384]{2,1,0:T(8,128)(2,1)S(1)} %merge.55.refs_0_), channel_id=1, source_target_pairs={{0,1},{1,0},{2,3},{3,2},{4,5},{5,4},{6,7},{7,6},{8,9},{9,8},{10,11... | collective-permute-start | bytes 1769480 | tf_op jit(solution)/shard_map/ppermute | solution.py:38
  462.9 24.3 %collective-permute-start.100 = (bf16[256,768]{1,0:T(8,128)(2,1)}, bf16[256,768]{1,0:T(8,128)(2,1)S(1)}, u32[]{:S(2)}, u32[]{:S(2)}) collective-permute-start(bf16[256,768]{1,0:T(8,128)(2,1)} %get-tuple-element.658.refs_0_), channel_id=1, source_target_pairs={{0,8},{8,0},{16,24},{24,16},{1,9},{9,1},{17,25},{25,17},{2,10},{10... | collective-permute-start | bytes 1179656 | tf_op jit(solution)/shard_map/ppermute | solution.py:38
  (202 other events, 1706.9 us)

commit v4 on v3

--- a/solution.py
+++ b/solution.py
@@ -72,6 +72,7 @@
     if not bundles[0].ring:
         return
     turns = {True: [], False: []}
+    started = []
     for index in TURNS:
         bundle = bundles[index]
         if bundle.step == 6:
@@ -79,8 +80,14 @@
         stage = bundle.step if bundle.step < 3 else 5 - bundle.step
         queue = turns[bundle.order[stage] == 0]
         depth = COLUMN_DEPTH if bundle.order[stage] == 0 else Z_DEPTH
-        bundle.send(queue[-depth] if len(queue) >= depth else other)
+        wait = [other]
+        if len(queue) >= depth:
+            wait.append(queue[-depth])
+        if len(started) >= LAG:
+            wait.append(started[-LAG])
+        bundle.send(wait)
         queue.append(bundle.coming)
+        started.append(bundle.coming)
 
 
 def ring_form(count):
@@ -89,8 +96,9 @@
 
 COLUMN_FIRST = (0, 1, 2)
 
-TURNS = (0, 1, 2, 5, 3, 0, 2, 4, 1, 3, 2, 5, 3, 2, 4, 3, 5, 3, 4, 4, 4, 5, 5, 5)
-COLUMN_DEPTH, Z_DEPTH = 2, 3
+TURNS = (0, 1, 2, 3, 0, 1, 2, 3, 1, 2, 1, 3, 2, 3, 2, 3, 3)
+COLUMN_DEPTH, Z_DEPTH = 3,4
+LAG = 4
 
 
 def after(value, other):
@@ -101,24 +109,36 @@
     def __init__(self, pieces, order):
         self.ring = ring_form(lax.axis_size("tok"))
         self.step, self.order = 0, order
-        self.kept, self.out = pieces
-        if not self.ring:
-            self.result = lax.psum(tuple(pieces), "tok")
+        self.parts = [tuple(pieces)]
+        self.coming = ()
+
+    def add(self, pieces):
+        self.parts.append(tuple(pieces))
+        if self.ring:
+            self.coming += (swap(pieces[1], "tok", 1 << self.order[0]),)
 
     def send(self, other=None):
         if not self.ring or self.step == 6:
             return
-        if self.step:
+        if self.step == 0:
+            out = self.parts[0][1]
+            self.kept = tuple(kept for kept, _ in self.parts)
+        else:
+            if self.step == 1:
+                self.kept = tuple(kept for kept, _ in self.parts)
             kept, came = self.kept, self.coming
             if other is not None:
                 kept, came = after((kept, came), other)
             if self.step < 3:
-                self.kept, self.out = merge("split", kept, came)
+                kept, out = merge("split", kept, came)
             else:
-                (self.kept,) = merge("add" if self.step == 3 else "join", kept, came)
-                self.out = self.kept
+                (kept,) = merge("add" if self.step == 3 else "join", kept, came)
+                out = kept
+            self.kept = (kept,)
+        if other is not None:
+            out = after(out, other)
         stage = self.step if self.step < 3 else 5 - self.step
-        self.coming = swap(self.out, "tok", 1 << self.order[stage])
+        self.coming = (swap(out, "tok", 1 << self.order[stage]),)
         self.step += 1
 
     def take(self, other):
@@ -131,8 +151,11 @@
         while self.ring and self.step < 6:
             self.send()
         if self.ring:
-            self.result = (self.kept, self.coming)
-        return self.result
+            return self.kept + self.coming
+        summed = lax.psum(self.parts, "tok")
+        return tuple(
+            jnp.concatenate([part[i] for part in summed], axis=1) for i in range(2)
+        )
 
 
 def gather_blocks(chunks):
@@ -314,32 +337,39 @@
     )(place, *pieces)
 
 
-def merge_kernel(kept, came, *outs, act):
-    count = kept.shape[0]
-    if act == "join":
-        outs[0][:count] = kept[...]
-        outs[0][count:] = came[...]
-        return
+def merge_kernel(*refs, act, parts):
+    count = refs[0].shape[0]
+    outs = refs[2 * parts :]
     each = count // len(outs)
-    for i, out in enumerate(outs):
-        at = slice(i * each, (i + 1) * each)
-        out[...] = (kept[at].astype(f32) + came[at].astype(f32)).astype(bf16)
+    for part in range(parts):
+        kept, came = refs[part], refs[parts + part]
+        size = kept.shape[1]
+        rows = slice(part * size, (part + 1) * size)
+        if act == "join":
+            outs[0][:count, rows] = kept[...]
+            outs[0][count:, rows] = came[...]
+            continue
+        for i, out in enumerate(outs):
+            at = slice(i * each, (i + 1) * each)
+            out[:, rows] = (kept[at].astype(f32) + came[at].astype(f32)).astype(bf16)
 
 
 def merge(act, kept, came):
-    count = kept.shape[0]
+    count, _, width = kept[0].shape
+    size = sum(array.shape[1] for array in kept)
     counts = {"add": [count], "split": [count // 2] * 2, "join": [2 * count]}[act]
-    shapes = [(n,) + kept.shape[1:] for n in counts]
+    shapes = [(n, size, width) for n in counts]
+    total = count * size * width
     return pl.pallas_call(
-        functools.partial(merge_kernel, act=act),
+        functools.partial(merge_kernel, act=act, parts=len(kept)),
         grid=(1,),
-        in_specs=[whole(kept.shape)] * 2,
+        in_specs=[whole(array.shape) for array in (*kept, *came)],
         out_specs=[whole(shape) for shape in shapes],
         out_shape=[jax.ShapeDtypeStruct(shape, bf16) for shape in shapes],
-        compiler_params=params(8),
-        cost_estimate=cost(kept.size, 8 * kept.size),
+        compiler_params=params(12),
+        cost_estimate=cost(total, 8 * total),
         name="merge",
-    )(kept, came)
+    )(*kept, *came)
 
 
 def chunk_rows(place, slot, k, rows):
@@ -991,15 +1021,17 @@
     )
 
 
-def square_place_kernel(place, *refs, order):
-    out, staged = refs[-2:]
+def feed_place_kernel(place, *refs, order):
+    outs, staged = refs[-3:-1], refs[-1]
     half = D // 2
     low = half // 2
     take_pieces(place, refs[:2], order, staged)
-    for piece in range(8):
-        i, j, part = piece // 4, (piece // 2) % 2, piece % 2
-        top = i * half + part * low
-        out[0, top : top + low, j * half : (j + 1) * half] = staged[piece].astype(f32)
+    for w, out in enumerate(outs):
+        for piece in range(8):
+            i, j, part = piece // 4, (piece // 2) % 2, piece % 2
+            top = i * half + part * low
+            value = staged[piece, w * low : (w + 1) * low]
+            out[0, top : top + low, j * half : (j + 1) * half] = value.astype(f32)
 
 
 def mix_place_kernel(place, *refs, bundles):
@@ -1199,22 +1231,22 @@
     sums_down = sums_down[0]
     grad_pieces = (gradient,)
     grads = [None] * LAYERS
-    placed_up = placed_down = placed_mix = ()
+    placed_feed = placed_mix = ()
     shapes_mix = ((3, heads * HD, D), (heads * HD, D))
     for l in reversed(range(LAYERS)):
         last = l == 0
         normed, queries, parts, mixed, probs, low_second, fed, slope = kept[l]
-        down = Bundle(square_grads(place, fed, 1, grad_pieces, COLUMN_FIRST), COLUMN_FIRST)
-        down.send()
+        down_pieces = square_grads(place, fed, 1, grad_pieces, COLUMN_FIRST)
+        feeding = Bundle(down_pieces, COLUMN_FIRST)
+        feeding.send()
         inner, grad_b_up, *pieces = feed_back(place, grad_pieces, w_up[l], w_down[l], slope)
-        up = Bundle(square_grads(place, fed, 0, (inner,), COLUMN_FIRST), COLUMN_FIRST)
-        up.send()
-        terms, _, _ = lax.optimization_barrier((sum_rows(pieces), up.out, down.out))
-        terms = down.take(terms)
+        up_pieces = square_grads(place, fed, 0, (inner,), COLUMN_FIRST)
+        terms, _ = lax.optimization_barrier((sum_rows(pieces), up_pieces))
+        terms = feeding.take(terms)
+        feeding.add(up_pieces)
         if last:
-            terms = mix_before.take(up_before.take(down_before.take(terms)))
-            down_before.send()
-            up_before.send()
+            terms = feed_before.take(terms)
+            feed_before.send()
         gradient, low, second_sums = norm_back(
             place, terms, low_second, gradient, param, rows, 2 * l + 1
         )
@@ -1222,9 +1254,9 @@
         dq, branch_full, *kv_grads = attend_back(
             place, starts, queries, probs, w_mix[l], pieces, parts, count
         )
-        kv_grads = up.take(kv_grads)
+        kv_grads = feeding.take(kv_grads)
         if last:
-            kv_grads = up_before.take(down_before.take(kv_grads))
+            kv_grads = mix_before.take(feed_before.take(kv_grads))
         kv_terms = return_blocks(kv_grads, lambda other: other)
         if last:
             kv_terms, residual_out = lax.optimization_barrier((kv_terms, residual_out))
@@ -1232,23 +1264,21 @@
             place, dq, w_all[l], normed, param, kv_terms, 2 * l
         )
         if not last:
-            down.send(dkv)
-            up.send(dkv)
+            feeding.send(dkv)
         groups = ((0, 3, 0), (1, 3, 0), (1, 3, HD), (2, 4, HD))
         mix_pieces = mix_grads(
             place, (dq, dkv, mixed, normed, branch_full), groups, COLUMN_FIRST
         )
         mix = Bundle(mix_pieces, COLUMN_FIRST)
         if last:
-            finish_in_turn(dkv, down_before, up_before, mix_before, down, up, mix)
+            finish_in_turn(dkv, feed_before, mix_before, feeding, mix)
         else:
             mix.send()
         terms, _ = lax.optimization_barrier((sum_rows(pieces), mix_pieces))
         if not last:
-            terms = up.take(down.take(terms))
-            down.send()
-            up.send()
-            down_before, up_before, mix_before = down, up, mix
+            terms = feeding.take(terms)
+            feeding.send()
+            feed_before, mix_before = feeding, mix
         gradient, low, low_sums = norm_back(
             place, terms, lows[l - 1] if l else low_first, gradient, param, rows, 2 * l
         )
@@ -1276,26 +1306,20 @@
         )
         sums_down = low_sums[2]
     grad_residual = columns(place, pieces).T
-    for l, bundles in ((1, (down_before, up_before, mix_before)), (0, (down, up, mix))):
-        placed_down, placed_up = [
-            place_call(
-                functools.partial(square_place_kernel, order=COLUMN_FIRST),
-                name,
-                place,
-                [bundle.finish()],
-                placed,
-                ((D, D),),
-                l,
-            )
-            for name, bundle, placed in (
-                ("down_place", bundles[0], placed_down),
-                ("up_place", bundles[1], placed_up),
-            )
-        ]
-        done = bundles[2].finish()
+    for l, bundles in ((1, (feed_before, mix_before)), (0, (feeding, mix))):
+        placed_feed = place_call(
+            functools.partial(feed_place_kernel, order=COLUMN_FIRST),
+            "feed_place",
+            place,
+            [bundles[0].finish()],
+            placed_feed,
+            ((D, D), (D, D)),
+            l,
+        )
+        done = bundles[1].finish()
         if l == 0:
-            done, placed_down, placed_up, placed_mix = lax.optimization_barrier(
-                (done, placed_down, placed_up, placed_mix)
+            done, placed_feed, placed_mix = lax.optimization_barrier(
+                (done, placed_feed, placed_mix)
             )
         placed_mix = place_call(
             functools.partial(mix_place_kernel, bundles=((COLUMN_FIRST, (0, 1, 2, 3)),)),
@@ -1343,9 +1367,9 @@
         grad_b_qv,
         placed_mix[1],
         grad_b_out,
-        placed_up[0],
+        placed_feed[1],
         grad_b_up,
-        placed_down[0],
+        placed_feed[0],
         grad_b_down,
         grad_ln_gain,
         grad_ln_bias,

time: 515 us -> 503 us (0.977)
  the two profiles are of different devices: /device:TPU:7 before, /device:TPU:0 now
where the time goes in v4:
time: 503 us; the launch traced here: 495 us
  waiting for transfers between devices  215 us (43%)
  starting transfers between devices  133 us (26%)
  Pallas kernels  102 us (20%)
  local copies, waits for them, and re-layouts  30.6 us (6%)
  other arithmetic  11.1 us (2%)
    ppermute x96, waiting for transfers between devices, swap(): lax.ppermute(value, axis, [(i, i ^ step) for i in range(lax.axis_size(axi...  186 us
    ppermute x96, starting transfers between devices, swap(): lax.ppermute(value, axis, [(i, i ^ step) for i in range(lax.axis_size(axi...  101 us
    ppermute x24, starting transfers between devices, rotate(): lax.ppermute(value, axis, [(i, (i + step) % count) for i in range(count)])  31.3 us
    ppermute x24, waiting for transfers between devices, rotate(): lax.ppermute(value, axis, [(i, (i + step) % count) for i in range(count)])  29.3 us
    pallas_call x2, Pallas kernels, attend_back(): pl.pallas_call(functools.partial(attend_back_kernel, heads=heads, count=c...  19.4 us
    pallas_call x6, Pallas kernels, pieces_call(): pl.pallas_call(kernel, grid_spec=pltpu.PrefetchScalarGridSpec(num_scalar_...  16.1 us
    pallas_call x2, Pallas kernels, attend(): pl.pallas_call(functools.partial(attend_kernel, heads=heads, blocks=rows...  14.9 us
    pallas_call x4, Pallas kernels, place_call(): pl.pallas_call(kernel, grid_spec=pltpu.PrefetchScalarGridSpec(num_scalar_...  13.2 us
  transfers between devices with their start and end apart: 120, of which 64 were waited for; matrix products, arithmetic and copies ran while one was open for 5% of the time, Pallas kernels for 13%

profile of v4, /device:TPU:0, one launch (start us, length us, event | category | flops | bytes accessed | tf_op | source)
XLA Modules:
  0.0 494.7 jit_solution(897968940008298185)
XLA Ops:
  24.8 3.6 collective-permute-done.7.refs_7_.refs_9_
  58.5 6.6 %attend.2 = (bf16[3,512,128]{2,1,0:T(8,128)(2,1)S(1)}, bf16[3,512,192]{2,1,0:T(8,128)(2,1)S(1)}, bf16[256,768]{1,0:T(8,128)(2,1)S(1)}, bf16[256,768]{1,0:T(8,128)(2,1)S(1)}) custom-call(s32[6]{0:T(128)S(1)} %stack.29.place, s32[3,32]{1,0:T(4,128)S(1)} %fusion.7.starts, bf16[3,512,128]{2,1,0:T(8,128)(2,1)S(1)} %copy-done.10, bf16[384,768]{1,0:T(8,128)(2,1)S(1)} %bitcast.65, ...), custom_call_target="tpu_custom_call" | custom-call | flops 503316480 | bytes 4718592 | tf_op jit(solution)/shard_map/attend/pallas_call | solution.py:516
  70.4 9.8 %collective-permute-done.21.refs_1_ = bf16[256,768]{1,0:T(8,128)(2,1)} collective-permute-done((bf16[256,768]{1,0:T(8,128)(2,1)}, bf16[256,768]{1,0:T(8,128)(2,1)}, u32[]{:S(2)}, u32[]{:S(2)}) %collective-permute-start.21) | collective-permute-done | bytes 393248 | tf_op jit(solution)/shard_map/ppermute | solution.py:38
  90.7 10.6 %collective-permute-done.24.refs_1_ = bf16[256,768]{1,0:T(8,128)(2,1)S(1)} collective-permute-done((bf16[256,768]{1,0:T(8,128)(2,1)S(1)}, bf16[256,768]{1,0:T(8,128)(2,1)S(1)}, u32[]{:S(2)}, u32[]{:S(2)}) %collective-permute-start.24) | collective-permute-done | bytes 393248 | tf_op jit(solution)/shard_map/ppermute | solution.py:38
  109.8 5.4 %collective-permute-done.27.refs_7_.refs_9_ = bf16[3,256,128]{2,1,0:T(8,128)(2,1)S(1)} collective-permute-done((bf16[3,256,128]{2,1,0:T(8,128)(2,1)S(1)}, bf16[3,256,128]{2,1,0:T(8,128)(2,1)S(1)}, u32[]{:S(2)}, u32[]{:S(2)}) %collective-permute-start.27) | collective-permute-done | bytes 196640 | tf_op jit(solution)/shard_map/ppermute | solution.py:43
  125.4 3.3 collective-permute-done.33.refs_12_.refs_14_
  142.9 8.3 %attend.3 = (bf16[3,512,128]{2,1,0:T(8,128)(2,1)S(1)}, bf16[3,512,192]{2,1,0:T(8,128)(2,1)S(1)}, bf16[256,768]{1,0:T(8,128)(2,1)S(1)}, bf16[256,768]{1,0:T(8,128)(2,1)S(1)}) custom-call(s32[6]{0:T(128)S(1)} %stack.29.place, s32[3,32]{1,0:T(4,128)S(1)} %fusion.7.starts, bf16[3,512,128]{2,1,0:T(8,128)(2,1)S(1)} %get-tuple-element.407.refs_0_, ...), custom_call_target="tpu_custom_call" | custom-call | flops 503316480 | bytes 4718592 | tf_op jit(solution)/shard_map/attend/pallas_call | solution.py:516
  155.1 9.9 %collective-permute-done.41.refs_1_ = bf16[256,768]{1,0:T(8,128)(2,1)S(1)} collective-permute-done((bf16[256,768]{1,0:T(8,128)(2,1)S(1)}, bf16[256,768]{1,0:T(8,128)(2,1)S(1)}, u32[]{:S(2)}, u32[]{:S(2)}) %collective-permute-start.41) | collective-permute-done | bytes 393248 | tf_op jit(solution)/shard_map/ppermute | solution.py:38
  183.6 7.6 %collective-permute-done.48.refs_1_ = bf16[256,768]{1,0:T(8,128)(2,1)S(1)} collective-permute-done((bf16[256,768]{1,0:T(8,128)(2,1)S(1)}, bf16[256,768]{1,0:T(8,128)(2,1)S(1)}, u32[]{:S(2)}, u32[]{:S(2)}) %collective-permute-start.48) | collective-permute-done | bytes 393248 | tf_op jit(solution)/shard_map/ppermute | solution.py:38
  191.2 3.2 collective-permute-done.46.refs_2_
  197.5 10.5 %attend_back.2 = (bf16[3,512,128]{2,1,0:T(8,128)(2,1)S(1)}, bf16[512,768]{1,0:T(8,128)(2,1)S(1)}, bf16[3,256,128]{2,1,0:T(8,128)(2,1)S(1)}, bf16[3,256,128]{2,1,...) custom-call(s32[6]{0:T(128)S(1)} %stack.29.place, ...), custom_call_target="tpu_custom_call" | custom-call | flops 905969664 | bytes 9437184 | tf_op jit(solution)/shard_map/attend_back/pallas_call | solution.py:608
  210.1 5.7 %collective-permute-done.51 = bf16[3,256,128]{2,1,0:T(8,128)(2,1)S(1)} collective-permute-done((bf16[3,256,128]{2,1,0:T(8,128)(2,1)S(1)}, bf16[3,256,128]{2,1,0:T(8,128)(2,1)S(1)}, u32[]{:S(2)}, u32[]{:S(2)}) %collective-permute-start.51) | collective-permute-done | bytes 196640 | tf_op jit(solution)/shard_map/ppermute | solution.py:38
  215.9 3.7 collective-permute-start.55
  255.7 6.8 %collective-permute-done.68.refs_1_ = bf16[256,768]{1,0:T(8,128)(2,1)S(1)} collective-permute-done((bf16[256,768]{1,0:T(8,128)(2,1)S(1)}, bf16[256,768]{1,0:T(8,128)(2,1)S(1)}, u32[]{:S(2)}, u32[]{:S(2)}) %collective-permute-start.68) | collective-permute-done | bytes 393248 | tf_op jit(solution)/shard_map/ppermute | solution.py:38
  267.0 3.5 collective-permute-done.65.refs_1_
  282.8 4.0 collective-permute-done.74.refs_1_
  286.9 4.4 collective-permute-done.72.refs_2_
  300.2 8.9 %attend_back.3 = (bf16[3,512,128]{2,1,0:T(8,128)(2,1)S(1)}, bf16[512,768]{1,0:T(8,128)(2,1)S(1)}, bf16[3,256,128]{2,1,0:T(8,128)(2,1)S(1)}, bf16[3,256,128]{2,1,...) custom-call(s32[6]{0:T(128)S(1)} %stack.29.place, ...), custom_call_target="tpu_custom_call" | custom-call | flops 905969664 | bytes 9437184 | tf_op jit(solution)/shard_map/attend_back/pallas_call | solution.py:608
  309.1 4.0 collective-permute-done.75.refs_1_
  352.9 11.9 %collective-permute-done.102.refs_1_ = bf16[2,384,384]{2,1,0:T(8,128)(2,1)S(1)} collective-permute-done((bf16[2,384,384]{2,1,0:T(8,128)(2,1)S(1)}, bf16[2,384,384]{2,1,0:T(8,128)(2,1)S(1)}, u32[]{:S(2)}, u32[]{:S(2)}) %collective-permute-start.102) | collective-permute-done | bytes 589856 | tf_op jit(solution)/shard_map/ppermute | solution.py:38
  367.4 3.5 mix_grads.3
  371.3 4.6 collective-permute-start.99
  375.9 8.1 %collective-permute-done.101.refs_1_ = bf16[2,384,384]{2,1,0:T(8,128)(2,1)S(1)} collective-permute-done((bf16[2,384,384]{2,1,0:T(8,128)(2,1)S(1)}, bf16[2,384,384]{2,1,0:T(8,128)(2,1)S(1)}, u32[]{:S(2)}, u32[]{:S(2)}) %collective-permute-start.101) | collective-permute-done | bytes 589856 | tf_op jit(solution)/shard_map/ppermute | solution.py:38
  387.4 15.1 %collective-permute-done.98.refs_1_ = bf16[4,192,384]{2,1,0:T(8,128)(2,1)S(1)} collective-permute-done((bf16[4,192,384]{2,1,0:T(8,128)(2,1)S(1)}, bf16[4,192,384]{2,1,0:T(8,128)(2,1)S(1)}, u32[]{:S(2)}, u32[]{:S(2)}) %collective-permute-start.98) | collective-permute-done | bytes 589856 | tf_op jit(solution)/shard_map/ppermute | solution.py:38
  404.1 4.3 collective-permute-start.108
  413.0 8.0 %collective-permute-done.107.refs_1_ = bf16[2,192,384]{2,1,0:T(8,128)(2,1)S(1)} collective-permute-done((bf16[2,192,384]{2,1,0:T(8,128)(2,1)S(1)}, bf16[2,192,384]{2,1,0:T(8,128)(2,1)S(1)}, u32[]{:S(2)}, u32[]{:S(2)}) %collective-permute-start.107) | collective-permute-done | bytes 294944 | tf_op jit(solution)/shard_map/ppermute | solution.py:38
  439.3 3.5 collective-permute-done.118
  447.9 3.6 collective-permute-done.119
  460.0 4.0 collective-permute-done.110.refs_1_
  469.1 3.3 norm_back.7
  483.5 4.4 feed_place.3
  490.9 3.3 mix_place.3
  (493 shorter events, 293.9 us)
Async XLA Ops:
  153.1 12.0 %collective-permute-start.41 = (bf16[256,768]{1,0:T(8,128)(2,1)S(1)}, bf16[256,768]{1,0:T(8,128)(2,1)S(1)}, u32[]{:S(2)}, u32[]{:S(2)}) collective-permute-start(bf16[256,768]{1,0:T(8,128)(2,1)S(1)} %add_convert_fusion.5.refs_0_), channel_id=1, source_target_pairs={{0,16},{8,24},{16,0},{24,8},{1,17},{9,25},{17,1},{25,9},{2,18},{10... | collective-permute-start | bytes 1179656 | tf_op jit(solution)/shard_map/ppermute | solution.py:38
  153.9 14.6 %collective-permute-start.43 = (bf16[192,512]{1,0:T(8,128)(2,1)S(1)}, bf16[192,512]{1,0:T(8,128)(2,1)S(1)}, u32[]{:S(2)}, u32[]{:S(2)}) collective-permute-start(bf16[192,512]{1,0:T(8,128)(2,1)S(1)} %bitcast.73), channel_id=1, source_target_pairs={{0,16},{8,24},{16,0},{24,8},{1,17},{9,25},{17,1},{25,9},{2,18},{10... | collective-permute-start | bytes 589832 | tf_op jit(solution)/shard_map/ppermute | solution.py:38
  178.2 16.2 %collective-permute-start.46 = (bf16[4,192,384]{2,1,0:T(8,128)(2,1)S(1)}, bf16[4,192,384]{2,1,0:T(8,128)(2,1)S(1)}, u32[]{:S(2)}, u32[]{:S(2)}) collective-permute-start(bf16[4,192,384]{2,1,0:T(8,128)(2,1)S(1)} %get-tuple-element.435), channel_id=1, source_target_pairs={{0,1},{1,0},{2,3},{3,2},{4,5},{5,4},{6,7},{7,6},{8,9},{9,8},{10,11... | collective-permute-start | bytes 1769480 | tf_op jit(solution)/shard_map/ppermute | solution.py:38
  183.2 24.8 %collective-permute-start.50 = (bf16[4,192,384]{2,1,0:T(8,128)(2,1)S(1)}, bf16[4,192,384]{2,1,0:T(8,128)(2,1)S(1)}, u32[]{:S(2)}, u32[]{:S(2)}) collective-permute-start(bf16[4,192,384]{2,1,0:T(8,128)(2,1)S(1)} %get-tuple-element.441), channel_id=1, source_target_pairs={{0,1},{1,0},{2,3},{3,2},{4,5},{5,4},{6,7},{7,6},{8,9},{9,8},{10,11... | collective-permute-start | bytes 1769480 | tf_op jit(solution)/shard_map/ppermute | solution.py:38
  221.4 12.2 %collective-permute-start.62 = (bf16[3,256,128]{2,1,0:T(8,128)(2,1)S(1)}, bf16[3,256,128]{2,1,0:T(8,128)(2,1)S(1)}, u32[]{:S(2)}, u32[]{:S(2)}) collective-permute-start(bf16[3,256,128]{2,1,0:T(8,128)(2,1)S(1)} %add_convert_fusion.16), channel_id=1, source_target_pairs={{0,6},{1,7},{2,0},{3,1},{4,2},{5,3},{6,4},{7,5},{8,14},{9,15},{10,... | collective-permute-start | bytes 589832 | tf_op jit(solution)/shard_map/ppermute | solution.py:43
  249.8 15.8 %collective-permute-start.66 = (bf16[2,384,384]{2,1,0:T(8,128)(2,1)S(1)}, bf16[2,384,384]{2,1,0:T(8,128)(2,1)S(1)}, u32[]{:S(2)}, u32[]{:S(2)}) collective-permute-start(bf16[2,384,384]{2,1,0:T(8,128)(2,1)S(1)} %get-tuple-element.508), channel_id=1, source_target_pairs={{0,2},{1,3},{2,0},{3,1},{4,6},{5,7},{6,4},{7,5},{8,10},{9,11},{10,... | collective-permute-start | bytes 1769480 | tf_op jit(solution)/shard_map/ppermute | solution.py:38
  255.4 15.2 %collective-permute-start.65 = (bf16[4,192,384]{2,1,0:T(8,128)(2,1)S(1)}, bf16[4,192,384]{2,1,0:T(8,128)(2,1)S(1)}, u32[]{:S(2)}, u32[]{:S(2)}) collective-permute-start(bf16[4,192,384]{2,1,0:T(8,128)(2,1)S(1)} %get-tuple-element.499), channel_id=1, source_target_pairs={{0,1},{1,0},{2,3},{3,2},{4,5},{5,4},{6,7},{7,6},{8,9},{9,8},{10,11... | collective-permute-start | bytes 1769480 | tf_op jit(solution)/shard_map/ppermute | solution.py:38
  275.1 16.2 %collective-permute-start.72 = (bf16[4,192,384]{2,1,0:T(8,128)(2,1)S(1)}, bf16[4,192,384]{2,1,0:T(8,128)(2,1)S(1)}, u32[]{:S(2)}, u32[]{:S(2)}) collective-permute-start(bf16[4,192,384]{2,1,0:T(8,128)(2,1)S(1)} %get-tuple-element.527), channel_id=1, source_target_pairs={{0,1},{1,0},{2,3},{3,2},{4,5},{5,4},{6,7},{7,6},{8,9},{9,8},{10,11... | collective-permute-start | bytes 1769480 | tf_op jit(solution)/shard_map/ppermute | solution.py:38
  276.9 22.3 %collective-permute-start.92 = (bf16[256,768]{1,0:T(8,128)(2,1)S(1)}, bf16[256,768]{1,0:T(8,128)(2,1)S(1)}, u32[]{:S(2)}, u32[]{:S(2)}) collective-permute-start(bf16[256,768]{1,0:T(8,128)(2,1)S(1)} %get-tuple-element.623), channel_id=1, source_target_pairs={{0,8},{8,0},{16,24},{24,16},{1,9},{9,1},{17,25},{25,17},{2,10},{10... | collective-permute-start | bytes 1179656 | tf_op jit(solution)/shard_map/ppermute | solution.py:38
  277.0 16.7 %collective-permute-start.71 = (bf16[1,384,384]{2,1,0:T(8,128)(2,1)S(1)}, bf16[1,384,384]{2,1,0:T(8,128)(2,1)S(1)}, u32[]{:S(2)}, u32[]{:S(2)}) collective-permute-start(bf16[1,384,384]{2,1,0:T(8,128)(2,1)S(1)} %get-tuple-element.523), channel_id=1, source_target_pairs={{0,4},{1,5},{2,6},{3,7},{4,0},{5,1},{6,2},{7,3},{8,12},{9,13},{10,... | collective-permute-start | bytes 884744 | tf_op jit(solution)/shard_map/ppermute | solution.py:38
  281.0 28.1 %collective-permute-start.76 = (bf16[4,192,384]{2,1,0:T(8,128)(2,1)S(1)}, bf16[4,192,384]{2,1,0:T(8,128)(2,1)S(1)}, u32[]{:S(2)}, u32[]{:S(2)}) collective-permute-start(bf16[4,192,384]{2,1,0:T(8,128)(2,1)S(1)} %get-tuple-element.533), channel_id=1, source_target_pairs={{0,1},{1,0},{2,3},{3,2},{4,5},{5,4},{6,7},{7,6},{8,9},{9,8},{10,11... | collective-permute-start | bytes 1769480 | tf_op jit(solution)/shard_map/ppermute | solution.py:38
  296.2 16.9 %collective-permute-start.70 = (bf16[2,192,384]{2,1,0:T(8,128)(2,1)S(1)}, bf16[2,192,384]{2,1,0:T(8,128)(2,1)S(1)}, u32[]{:S(2)}, u32[]{:S(2)}) collective-permute-start(bf16[2,192,384]{2,1,0:T(8,128)(2,1)S(1)} %get-tuple-element.519), channel_id=1, source_target_pairs={{0,2},{1,3},{2,0},{3,1},{4,6},{5,7},{6,4},{7,5},{8,10},{9,11},{10,... | collective-permute-start | bytes 884744 | tf_op jit(solution)/shard_map/ppermute | solution.py:38
  296.4 16.7 %collective-permute-start.75 = (bf16[1,384,384]{2,1,0:T(8,128)(2,1)S(1)}, bf16[1,384,384]{2,1,0:T(8,128)(2,1)S(1)}, u32[]{:S(2)}, u32[]{:S(2)}) collective-permute-start(bf16[1,384,384]{2,1,0:T(8,128)(2,1)S(1)} %merge.23.refs_0_), channel_id=1, source_target_pairs={{0,4},{1,5},{2,6},{3,7},{4,0},{5,1},{6,2},{7,3},{8,12},{9,13},{10,... | collective-permute-start | bytes 884744 | tf_op jit(solution)/shard_map/ppermute | solution.py:38
  299.2 15.7 %collective-permute-start.93 = (bf16[256,768]{1,0:T(8,128)(2,1)S(1)}, bf16[256,768]{1,0:T(8,128)(2,1)S(1)}, u32[]{:S(2)}, u32[]{:S(2)}) collective-permute-start(bf16[256,768]{1,0:T(8,128)(2,1)S(1)} %add_convert_fusion.1.refs_0_), channel_id=1, source_target_pairs={{0,16},{8,24},{16,0},{24,8},{1,17},{9,25},{17,1},{25,9},{2,18},{10... | collective-permute-start | bytes 1179656 | tf_op jit(solution)/shard_map/ppermute | solution.py:38
  316.7 29.9 %collective-permute-start.94 = (bf16[256,768]{1,0:T(8,128)(2,1)S(1)}, bf16[256,768]{1,0:T(8,128)(2,1)S(1)}, u32[]{:S(2)}, u32[]{:S(2)}) collective-permute-start(bf16[256,768]{1,0:T(8,128)(2,1)S(1)} %get-tuple-element.625.refs_0_), channel_id=1, source_target_pairs={{0,8},{8,0},{16,24},{24,16},{1,9},{9,1},{17,25},{25,17},{2,10},{10... | collective-permute-start | bytes 1179656 | tf_op jit(solution)/shard_map/ppermute | solution.py:38
  324.9 12.0 %collective-permute-start.89 = (bf16[3,256,128]{2,1,0:T(8,128)(2,1)S(1)}, bf16[3,256,128]{2,1,0:T(8,128)(2,1)S(1)}, u32[]{:S(2)}, u32[]{:S(2)}) collective-permute-start(bf16[3,256,128]{2,1,0:T(8,128)(2,1)S(1)} %add_convert_fusion.10), channel_id=1, source_target_pairs={{0,6},{1,7},{2,0},{3,1},{4,2},{5,3},{6,4},{7,5},{8,14},{9,15},{10,... | collective-permute-start | bytes 589832 | tf_op jit(solution)/shard_map/ppermute | solution.py:43
  364.9 43.5 %collective-permute-start.106 = (bf16[4,384,384]{2,1,0:T(8,128)(2,1)S(1)}, bf16[4,384,384]{2,1,0:T(8,128)(2,1)S(1)}, u32[]{:S(2)}, u32[]{:S(2)}) collective-permute-start(bf16[4,384,384]{2,1,0:T(8,128)(2,1)S(1)} %merge.31.refs_0_), channel_id=1, source_target_pairs={{0,1},{1,0},{2,3},{3,2},{4,5},{5,4},{6,7},{7,6},{8,9},{9,8},{10,11... | collective-permute-start | bytes 3538952 | tf_op jit(solution)/shard_map/ppermute | solution.py:38
  367.0 17.1 %collective-permute-start.101 = (bf16[2,384,384]{2,1,0:T(8,128)(2,1)S(1)}, bf16[2,384,384]{2,1,0:T(8,128)(2,1)S(1)}, u32[]{:S(2)}, u32[]{:S(2)}) collective-permute-start(bf16[2,384,384]{2,1,0:T(8,128)(2,1)S(1)} %get-tuple-element.667), channel_id=1, source_target_pairs={{0,2},{1,3},{2,0},{3,1},{4,6},{5,7},{6,4},{7,5},{8,10},{9,11},{10,... | collective-permute-start | bytes 1769480 | tf_op jit(solution)/shard_map/ppermute | solution.py:38
  370.9 31.6 %collective-permute-start.98 = (bf16[4,192,384]{2,1,0:T(8,128)(2,1)S(1)}, bf16[4,192,384]{2,1,0:T(8,128)(2,1)S(1)}, u32[]{:S(2)}, u32[]{:S(2)}) collective-permute-start(bf16[4,192,384]{2,1,0:T(8,128)(2,1)S(1)} %get-tuple-element.646), channel_id=1, source_target_pairs={{0,1},{1,0},{2,3},{3,2},{4,5},{5,4},{6,7},{7,6},{8,9},{9,8},{10,11... | collective-permute-start | bytes 1769480 | tf_op jit(solution)/shard_map/ppermute | solution.py:38
  371.3 13.1 %collective-permute-start.99 = (bf16[1,192,384]{2,1,0:T(8,128)(2,1)S(1)}, bf16[1,192,384]{2,1,0:T(8,128)(2,1)S(1)}, u32[]{:S(2)}, u32[]{:S(2)}) collective-permute-start(bf16[1,192,384]{2,1,0:T(8,128)(2,1)S(1)} %get-tuple-element.652), channel_id=1, source_target_pairs={{0,4},{1,5},{2,6},{3,7},{4,0},{5,1},{6,2},{7,3},{8,12},{9,13},{10,... | collective-permute-start | bytes 442376 | tf_op jit(solution)/shard_map/ppermute | solution.py:38
  384.2 19.8 %collective-permute-start.103 = (bf16[1,384,384]{2,1,0:T(8,128)(2,1)S(1)}, bf16[1,384,384]{2,1,0:T(8,128)(2,1)S(1)}, u32[]{:S(2)}, u32[]{:S(2)}) collective-permute-start(bf16[1,384,384]{2,1,0:T(8,128)(2,1)S(1)} %get-tuple-element.675), channel_id=1, source_target_pairs={{0,4},{1,5},{2,6},{3,7},{4,0},{5,1},{6,2},{7,3},{8,12},{9,13},{10,... | collective-permute-start | bytes 884744 | tf_op jit(solution)/shard_map/ppermute | solution.py:38
  384.4 19.6 %collective-permute-start.105 = (bf16[1,192,384]{2,1,0:T(8,128)(2,1)S(1)}, bf16[1,192,384]{2,1,0:T(8,128)(2,1)S(1)}, u32[]{:S(2)}, u32[]{:S(2)}) collective-permute-start(bf16[1,192,384]{2,1,0:T(8,128)(2,1)S(1)} %merge.30.refs_0_), channel_id=1, source_target_pairs={{0,4},{1,5},{2,6},{3,7},{4,0},{5,1},{6,2},{7,3},{8,12},{9,13},{10,... | collective-permute-start | bytes 442376 | tf_op jit(solution)/shard_map/ppermute | solution.py:38
  403.4 17.6 %collective-permute-start.100 = (bf16[2,192,384]{2,1,0:T(8,128)(2,1)S(1)}, bf16[2,192,384]{2,1,0:T(8,128)(2,1)S(1)}, u32[]{:S(2)}, u32[]{:S(2)}) collective-permute-start(bf16[2,192,384]{2,1,0:T(8,128)(2,1)S(1)} %get-tuple-element.657), channel_id=1, source_target_pairs={{0,2},{1,3},{2,0},{3,1},{4,6},{5,7},{6,4},{7,5},{8,10},{9,11},{10,... | collective-permute-start | bytes 884744 | tf_op jit(solution)/shard_map/ppermute | solution.py:38
  404.1 17.7 %collective-permute-start.108 = (bf16[1,384,384]{2,1,0:T(8,128)(2,1)S(1)}, bf16[1,384,384]{2,1,0:T(8,128)(2,1)S(1)}, u32[]{:S(2)}, u32[]{:S(2)}) collective-permute-start(bf16[1,384,384]{2,1,0:T(8,128)(2,1)S(1)} %merge.33.refs_0_), channel_id=1, source_target_pairs={{0,4},{1,5},{2,6},{3,7},{4,0},{5,1},{6,2},{7,3},{8,12},{9,13},{10,... | collective-permute-start | bytes 884744 | tf_op jit(solution)/shard_map/ppermute | solution.py:38
  412.2 13.8 %collective-permute-start.115 = (f32[4,768]{1,0:T(4,128)S(1)}, f32[4,768]{1,0:T(4,128)S(1)}, u32[]{:S(2)}, u32[]{:S(2)}) collective-permute-start(f32[4,768]{1,0:T(4,128)S(1)} %pad_maximum_fusion), channel_id=1, source_target_pairs={{0,16},{8,24},{16,0},{24,8},{1,17},{9,25},{17,1},{25,9},{2,18},{10... | collective-permute-start | bytes 36872 | tf_op jit(solution)/shard_map/ppermute | solution.py:38
  421.9 30.5 %collective-permute-start.113 = (bf16[4,192,384]{2,1,0:T(8,128)(2,1)S(1)}, bf16[4,192,384]{2,1,0:T(8,128)(2,1)S(1)}, u32[]{:S(2)}, u32[]{:S(2)}) collective-permute-start(bf16[4,192,384]{2,1,0:T(8,128)(2,1)S(1)} %merge.38.refs_0_), channel_id=1, source_target_pairs={{0,1},{1,0},{2,3},{3,2},{4,5},{5,4},{6,7},{7,6},{8,9},{9,8},{10,11... | collective-permute-start | bytes 1769480 | tf_op jit(solution)/shard_map/ppermute | solution.py:38
  423.7 29.5 %collective-permute-start.111 = (bf16[2,384,384]{2,1,0:T(8,128)(2,1)S(1)}, bf16[2,384,384]{2,1,0:T(8,128)(2,1)}, u32[]{:S(2)}, u32[]{:S(2)}) collective-permute-start(bf16[2,384,384]{2,1,0:T(8,128)(2,1)S(1)} %merge.36.refs_0_), channel_id=1, source_target_pairs={{0,2},{1,3},{2,0},{3,1},{4,6},{5,7},{6,4},{7,5},{8,10},{9,11},{10,... | collective-permute-start | bytes 1769480 | tf_op jit(solution)/shard_map/ppermute | solution.py:38
  426.0 31.2 %collective-permute-start.95 = (bf16[256,768]{1,0:T(8,128)(2,1)}, bf16[256,768]{1,0:T(8,128)(2,1)}, u32[]{:S(2)}, u32[]{:S(2)}) collective-permute-start(bf16[256,768]{1,0:T(8,128)(2,1)} %copy-done.62), channel_id=1, source_target_pairs={{0,8},{8,0},{16,24},{24,16},{1,9},{9,1},{17,25},{25,17},{2,10},{10... | collective-permute-start | bytes 1179656 | tf_op jit(solution)/shard_map/ppermute | solution.py:38
  428.7 14.3 %collective-permute-start.104 = (bf16[1,192,384]{2,1,0:T(8,128)(2,1)S(1)}, bf16[1,192,384]{2,1,0:T(8,128)(2,1)S(1)}, u32[]{:S(2)}, u32[]{:S(2)}) collective-permute-start(bf16[1,192,384]{2,1,0:T(8,128)(2,1)S(1)} %get-tuple-element.680), channel_id=1, source_target_pairs={{0,4},{1,5},{2,6},{3,7},{4,0},{5,1},{6,2},{7,3},{8,12},{9,13},{10,... | collective-permute-start | bytes 442376 | tf_op jit(solution)/shard_map/ppermute | solution.py:38
  443.1 13.1 %collective-permute-start.109 = (bf16[1,192,384]{2,1,0:T(8,128)(2,1)S(1)}, bf16[1,192,384]{2,1,0:T(8,128)(2,1)}, u32[]{:S(2)}, u32[]{:S(2)}) collective-permute-start(bf16[1,192,384]{2,1,0:T(8,128)(2,1)S(1)} %merge.34.refs_0_), channel_id=1, source_target_pairs={{0,4},{1,5},{2,6},{3,7},{4,0},{5,1},{6,2},{7,3},{8,12},{9,13},{10,... | collective-permute-start | bytes 442376 | tf_op jit(solution)/shard_map/ppermute | solution.py:38
  454.4 29.1 %collective-permute-start.114 = (bf16[4,384,384]{2,1,0:T(8,128)(2,1)S(1)}, bf16[4,384,384]{2,1,0:T(8,128)(2,1)}, u32[]{:S(2)}, u32[]{:S(2)}) collective-permute-start(bf16[4,384,384]{2,1,0:T(8,128)(2,1)S(1)} %merge.39.refs_0_), channel_id=1, source_target_pairs={{0,1},{1,0},{2,3},{3,2},{4,5},{5,4},{6,7},{7,6},{8,9},{9,8},{10,11... | collective-permute-start | bytes 3538952 | tf_op jit(solution)/shard_map/ppermute | solution.py:38
  464.0 26.9 %collective-permute-start.112 = (bf16[4,192,384]{2,1,0:T(8,128)(2,1)S(1)}, bf16[4,192,384]{2,1,0:T(8,128)(2,1)}, u32[]{:S(2)}, u32[]{:S(2)}) collective-permute-start(bf16[4,192,384]{2,1,0:T(8,128)(2,1)S(1)} %merge.37.refs_0_), channel_id=1, source_target_pairs={{0,1},{1,0},{2,3},{3,2},{4,5},{5,4},{6,7},{7,6},{8,9},{9,8},{10,11... | collective-permute-start | bytes 1769480 | tf_op jit(solution)/shard_map/ppermute | solution.py:38
  (156 other events, 1299.9 us)

commit v5 on v4

--- a/solution.py
+++ b/solution.py
@@ -110,7 +110,7 @@
         self.ring = ring_form(lax.axis_size("tok"))
         self.step, self.order = 0, order
         self.parts = [tuple(pieces)]
-        self.coming = ()
+        self.coming = self.kept = ()
 
     def add(self, pieces):
         self.parts.append(tuple(pieces))
@@ -1236,10 +1236,10 @@
     for l in reversed(range(LAYERS)):
         last = l == 0
         normed, queries, parts, mixed, probs, low_second, fed, slope = kept[l]
-        down_pieces = square_grads(place, fed, 1, grad_pieces, COLUMN_FIRST)
+        inner, grad_b_up, *pieces = feed_back(place, grad_pieces, w_up[l], w_down[l], slope)
+        down_pieces = square_grads(place, after(fed, pieces), 1, grad_pieces, COLUMN_FIRST)
         feeding = Bundle(down_pieces, COLUMN_FIRST)
         feeding.send()
-        inner, grad_b_up, *pieces = feed_back(place, grad_pieces, w_up[l], w_down[l], slope)
         up_pieces = square_grads(place, fed, 0, (inner,), COLUMN_FIRST)
         terms, _ = lax.optimization_barrier((sum_rows(pieces), up_pieces))
         terms = feeding.take(terms)
@@ -1332,6 +1332,7 @@
         )
 
     first = jnp.concatenate([grads[l][7] for l in range(LAYERS)], axis=0)
+    first = after(first, feeding.kept)
     first = first + swap(first, "head", 2)
     over_all = jnp.concatenate(
         [first]

time: 503 us -> 509 us (1.012)
  waiting for transfers between devices: 215 us -> 223 us
    ppermute x96, waiting for transfers between devices: 186 us -> 194 us  [swap(): lax.ppermute(value, axis, [(i, i ^ step) for i in range(lax.axis_size(axi...]
    unnamed x139 -> x127, local copies, waits for them, and re-layouts: 12.7 us -> 11.4 us
  transfers between devices with their start and end apart: 120 -> 120, of which waited for: 64 -> 65; matrix products, arithmetic and copies ran while one was open for 5% -> 4% of each run, Pallas kernels for 13% -> 14%
where the time goes in v5:
time: 509 us; the launch traced here: 500 us
  waiting for transfers between devices  223 us (44%)
  starting transfers between devices  134 us (26%)
  Pallas kernels  105 us (21%)
  local copies, waits for them, and re-layouts  28.3 us (6%)
  other arithmetic  6.94 us (1%)
    ppermute x96, waiting for transfers between devices, swap(): lax.ppermute(value, axis, [(i, i ^ step) for i in range(lax.axis_size(axi...  194 us
    ppermute x96, starting transfers between devices, swap(): lax.ppermute(value, axis, [(i, i ^ step) for i in range(lax.axis_size(axi...  102 us
    ppermute x24, starting transfers between devices, rotate(): lax.ppermute(value, axis, [(i, (i + step) % count) for i in range(count)])  31.3 us
    ppermute x24, waiting for transfers between devices, rotate(): lax.ppermute(value, axis, [(i, (i + step) % count) for i in range(count)])  29.2 us
    pallas_call x2, Pallas kernels, attend_back(): pl.pallas_call(functools.partial(attend_back_kernel, heads=heads, count=c...  19.4 us
    pallas_call x6, Pallas kernels, pieces_call(): pl.pallas_call(kernel, grid_spec=pltpu.PrefetchScalarGridSpec(num_scalar_...  16.1 us
    pallas_call x2, Pallas kernels, attend(): pl.pallas_call(functools.partial(attend_kernel, heads=heads, blocks=rows...  14.9 us
    pallas_call x4, Pallas kernels, place_call(): pl.pallas_call(kernel, grid_spec=pltpu.PrefetchScalarGridSpec(num_scalar_...  13.2 us
  transfers between devices with their start and end apart: 120, of which 65 were waited for; matrix products, arithmetic and copies ran while one was open for 4% of the time, Pallas kernels for 14%

profile of v5, /device:TPU:0, one launch (start us, length us, event | category | flops | bytes accessed | tf_op | source)
XLA Modules:
  0.0 500.0 jit_solution(17486718305360849065)
XLA Ops:
  24.8 3.6 collective-permute-done.7.refs_7_.refs_9_
  58.5 6.6 %attend.2 = (bf16[3,512,128]{2,1,0:T(8,128)(2,1)S(1)}, bf16[3,512,192]{2,1,0:T(8,128)(2,1)S(1)}, bf16[256,768]{1,0:T(8,128)(2,1)S(1)}, bf16[256,768]{1,0:T(8,128)(2,1)S(1)}) custom-call(s32[6]{0:T(128)S(1)} %stack.29.place, s32[3,32]{1,0:T(4,128)S(1)} %fusion.7.starts, bf16[3,512,128]{2,1,0:T(8,128)(2,1)S(1)} %copy-done.10, bf16[384,768]{1,0:T(8,128)(2,1)S(1)} %bitcast.65, ...), custom_call_target="tpu_custom_call" | custom-call | flops 503316480 | bytes 4718592 | tf_op jit(solution)/shard_map/attend/pallas_call | solution.py:516
  70.9 9.2 %collective-permute-done.21.refs_1_ = bf16[256,768]{1,0:T(8,128)(2,1)} collective-permute-done((bf16[256,768]{1,0:T(8,128)(2,1)}, bf16[256,768]{1,0:T(8,128)(2,1)}, u32[]{:S(2)}, u32[]{:S(2)}) %collective-permute-start.21) | collective-permute-done | bytes 393248 | tf_op jit(solution)/shard_map/ppermute | solution.py:38
  90.7 10.6 %collective-permute-done.24.refs_1_ = bf16[256,768]{1,0:T(8,128)(2,1)S(1)} collective-permute-done((bf16[256,768]{1,0:T(8,128)(2,1)S(1)}, bf16[256,768]{1,0:T(8,128)(2,1)S(1)}, u32[]{:S(2)}, u32[]{:S(2)}) %collective-permute-start.24) | collective-permute-done | bytes 393248 | tf_op jit(solution)/shard_map/ppermute | solution.py:38
  109.9 5.4 %collective-permute-done.27.refs_7_.refs_9_ = bf16[3,256,128]{2,1,0:T(8,128)(2,1)S(1)} collective-permute-done((bf16[3,256,128]{2,1,0:T(8,128)(2,1)S(1)}, bf16[3,256,128]{2,1,0:T(8,128)(2,1)S(1)}, u32[]{:S(2)}, u32[]{:S(2)}) %collective-permute-start.27) | collective-permute-done | bytes 196640 | tf_op jit(solution)/shard_map/ppermute | solution.py:43
  125.4 3.3 collective-permute-done.33.refs_12_.refs_14_
  142.9 8.3 %attend.3 = (bf16[3,512,128]{2,1,0:T(8,128)(2,1)S(1)}, bf16[3,512,192]{2,1,0:T(8,128)(2,1)S(1)}, bf16[256,768]{1,0:T(8,128)(2,1)S(1)}, bf16[256,768]{1,0:T(8,128)(2,1)S(1)}) custom-call(s32[6]{0:T(128)S(1)} %stack.29.place, s32[3,32]{1,0:T(4,128)S(1)} %fusion.7.starts, bf16[3,512,128]{2,1,0:T(8,128)(2,1)S(1)} %get-tuple-element.410.refs_0_, ...), custom_call_target="tpu_custom_call" | custom-call | flops 503316480 | bytes 4718592 | tf_op jit(solution)/shard_map/attend/pallas_call | solution.py:516
  155.1 9.9 %collective-permute-done.41.refs_1_ = bf16[256,768]{1,0:T(8,128)(2,1)S(1)} collective-permute-done((bf16[256,768]{1,0:T(8,128)(2,1)S(1)}, bf16[256,768]{1,0:T(8,128)(2,1)S(1)}, u32[]{:S(2)}, u32[]{:S(2)}) %collective-permute-start.41) | collective-permute-done | bytes 393248 | tf_op jit(solution)/shard_map/ppermute | solution.py:38
  183.7 7.6 %collective-permute-done.48.refs_1_ = bf16[256,768]{1,0:T(8,128)(2,1)S(1)} collective-permute-done((bf16[256,768]{1,0:T(8,128)(2,1)S(1)}, bf16[256,768]{1,0:T(8,128)(2,1)S(1)}, u32[]{:S(2)}, u32[]{:S(2)}) %collective-permute-start.48) | collective-permute-done | bytes 393248 | tf_op jit(solution)/shard_map/ppermute | solution.py:38
  197.5 10.5 %attend_back.2 = (bf16[3,512,128]{2,1,0:T(8,128)(2,1)S(1)}, bf16[512,768]{1,0:T(8,128)(2,1)S(1)}, bf16[3,256,128]{2,1,0:T(8,128)(2,1)S(1)}, bf16[3,256,128]{2,1,...) custom-call(s32[6]{0:T(128)S(1)} %stack.29.place, ...), custom_call_target="tpu_custom_call" | custom-call | flops 905969664 | bytes 9437184 | tf_op jit(solution)/shard_map/attend_back/pallas_call | solution.py:608
  210.1 5.7 %collective-permute-done.51 = bf16[3,256,128]{2,1,0:T(8,128)(2,1)S(1)} collective-permute-done((bf16[3,256,128]{2,1,0:T(8,128)(2,1)S(1)}, bf16[3,256,128]{2,1,0:T(8,128)(2,1)S(1)}, u32[]{:S(2)}, u32[]{:S(2)}) %collective-permute-start.51) | collective-permute-done | bytes 196640 | tf_op jit(solution)/shard_map/ppermute | solution.py:38
  215.9 3.7 collective-permute-start.55
  255.7 6.7 %collective-permute-done.68.refs_1_ = bf16[256,768]{1,0:T(8,128)(2,1)S(1)} collective-permute-done((bf16[256,768]{1,0:T(8,128)(2,1)S(1)}, bf16[256,768]{1,0:T(8,128)(2,1)S(1)}, u32[]{:S(2)}, u32[]{:S(2)}) %collective-permute-start.68) | collective-permute-done | bytes 393248 | tf_op jit(solution)/shard_map/ppermute | solution.py:38
  266.9 3.5 collective-permute-done.65.refs_1_
  282.7 4.1 collective-permute-done.74.refs_1_
  286.8 4.3 collective-permute-done.72.refs_2_
  300.1 8.9 %attend_back.3 = (bf16[3,512,128]{2,1,0:T(8,128)(2,1)S(1)}, bf16[512,768]{1,0:T(8,128)(2,1)S(1)}, bf16[3,256,128]{2,1,0:T(8,128)(2,1)S(1)}, bf16[3,256,128]{2,1,...) custom-call(s32[6]{0:T(128)S(1)} %stack.29.place, ...), custom_call_target="tpu_custom_call" | custom-call | flops 905969664 | bytes 9437184 | tf_op jit(solution)/shard_map/attend_back/pallas_call | solution.py:608
  309.1 4.0 collective-permute-done.75.refs_1_
  352.7 11.8 %collective-permute-done.102.refs_1_ = bf16[2,384,384]{2,1,0:T(8,128)(2,1)S(1)} collective-permute-done((bf16[2,384,384]{2,1,0:T(8,128)(2,1)S(1)}, bf16[2,384,384]{2,1,0:T(8,128)(2,1)S(1)}, u32[]{:S(2)}, u32[]{:S(2)}) %collective-permute-start.102) | collective-permute-done | bytes 589856 | tf_op jit(solution)/shard_map/ppermute | solution.py:38
  367.2 3.5 mix_grads.3
  371.1 4.2 collective-permute-start.99
  375.3 8.8 %collective-permute-done.101.refs_1_ = bf16[2,384,384]{2,1,0:T(8,128)(2,1)S(1)} collective-permute-done((bf16[2,384,384]{2,1,0:T(8,128)(2,1)S(1)}, bf16[2,384,384]{2,1,0:T(8,128)(2,1)S(1)}, u32[]{:S(2)}, u32[]{:S(2)}) %collective-permute-start.101) | collective-permute-done | bytes 589856 | tf_op jit(solution)/shard_map/ppermute | solution.py:38
  387.4 14.9 %collective-permute-done.98.refs_1_ = bf16[4,192,384]{2,1,0:T(8,128)(2,1)S(1)} collective-permute-done((bf16[4,192,384]{2,1,0:T(8,128)(2,1)S(1)}, bf16[4,192,384]{2,1,0:T(8,128)(2,1)S(1)}, u32[]{:S(2)}, u32[]{:S(2)}) %collective-permute-start.98) | collective-permute-done | bytes 589856 | tf_op jit(solution)/shard_map/ppermute | solution.py:38
  403.2 3.7 collective-permute-start.108
  407.6 8.6 %collective-permute-done.100.refs_1_ = bf16[2,192,384]{2,1,0:T(8,128)(2,1)S(1)} collective-permute-done((bf16[2,192,384]{2,1,0:T(8,128)(2,1)S(1)}, bf16[2,192,384]{2,1,0:T(8,128)(2,1)S(1)}, u32[]{:S(2)}, u32[]{:S(2)}) %collective-permute-start.100) | collective-permute-done | bytes 294944 | tf_op jit(solution)/shard_map/ppermute | solution.py:38
  416.2 4.1 collective-permute-done.107.refs_1_
  436.7 3.6 collective-permute-start.109
  451.9 4.3 collective-permute-done.117
  460.6 3.4 collective-permute-start.119
  481.0 5.6 %collective-permute-done.114.refs_1_ = bf16[4,384,384]{2,1,0:T(8,128)(2,1)} collective-permute-done((bf16[4,384,384]{2,1,0:T(8,128)(2,1)S(1)}, bf16[4,384,384]{2,1,0:T(8,128)(2,1)}, u32[]{:S(2)}, u32[]{:S(2)}) %collective-permute-start.114) | collective-permute-done | bytes 1179680 | tf_op jit(solution)/shard_map/ppermute | solution.py:38
  486.6 4.4 feed_place.3
  491.0 6.2 %collective-permute-done.112.refs_1_ = bf16[4,192,384]{2,1,0:T(8,128)(2,1)S(1)} collective-permute-done((bf16[4,192,384]{2,1,0:T(8,128)(2,1)S(1)}, bf16[4,192,384]{2,1,0:T(8,128)(2,1)S(1)}, u32[]{:S(2)}, u32[]{:S(2)}) %collective-permute-start.112) | collective-permute-done | bytes 589856 | tf_op jit(solution)/shard_map/ppermute | solution.py:38
  (481 shorter events, 293.6 us)
Async XLA Ops:
  153.0 12.0 %collective-permute-start.41 = (bf16[256,768]{1,0:T(8,128)(2,1)S(1)}, bf16[256,768]{1,0:T(8,128)(2,1)S(1)}, u32[]{:S(2)}, u32[]{:S(2)}) collective-permute-start(bf16[256,768]{1,0:T(8,128)(2,1)S(1)} %add_convert_fusion.5.refs_0_), channel_id=1, source_target_pairs={{0,16},{8,24},{16,0},{24,8},{1,17},{9,25},{17,1},{25,9},{2,18},{10... | collective-permute-start | bytes 1179656 | tf_op jit(solution)/shard_map/ppermute | solution.py:38
  153.9 14.5 %collective-permute-start.43 = (bf16[192,512]{1,0:T(8,128)(2,1)S(1)}, bf16[192,512]{1,0:T(8,128)(2,1)S(1)}, u32[]{:S(2)}, u32[]{:S(2)}) collective-permute-start(bf16[192,512]{1,0:T(8,128)(2,1)S(1)} %bitcast.73), channel_id=1, source_target_pairs={{0,16},{8,24},{16,0},{24,8},{1,17},{9,25},{17,1},{25,9},{2,18},{10... | collective-permute-start | bytes 589832 | tf_op jit(solution)/shard_map/ppermute | solution.py:38
  178.2 16.2 %collective-permute-start.46 = (bf16[4,192,384]{2,1,0:T(8,128)(2,1)S(1)}, bf16[4,192,384]{2,1,0:T(8,128)(2,1)S(1)}, u32[]{:S(2)}, u32[]{:S(2)}) collective-permute-start(bf16[4,192,384]{2,1,0:T(8,128)(2,1)S(1)} %get-tuple-element.442), channel_id=1, source_target_pairs={{0,1},{1,0},{2,3},{3,2},{4,5},{5,4},{6,7},{7,6},{8,9},{9,8},{10,11... | collective-permute-start | bytes 1769480 | tf_op jit(solution)/shard_map/ppermute | solution.py:38
  183.2 24.8 %collective-permute-start.50 = (bf16[4,192,384]{2,1,0:T(8,128)(2,1)S(1)}, bf16[4,192,384]{2,1,0:T(8,128)(2,1)S(1)}, u32[]{:S(2)}, u32[]{:S(2)}) collective-permute-start(bf16[4,192,384]{2,1,0:T(8,128)(2,1)S(1)} %get-tuple-element.445), channel_id=1, source_target_pairs={{0,1},{1,0},{2,3},{3,2},{4,5},{5,4},{6,7},{7,6},{8,9},{9,8},{10,11... | collective-permute-start | bytes 1769480 | tf_op jit(solution)/shard_map/ppermute | solution.py:38
  221.3 12.2 %collective-permute-start.62 = (bf16[3,256,128]{2,1,0:T(8,128)(2,1)S(1)}, bf16[3,256,128]{2,1,0:T(8,128)(2,1)S(1)}, u32[]{:S(2)}, u32[]{:S(2)}) collective-permute-start(bf16[3,256,128]{2,1,0:T(8,128)(2,1)S(1)} %add_convert_fusion.16), channel_id=1, source_target_pairs={{0,6},{1,7},{2,0},{3,1},{4,2},{5,3},{6,4},{7,5},{8,14},{9,15},{10,... | collective-permute-start | bytes 589832 | tf_op jit(solution)/shard_map/ppermute | solution.py:43
  249.7 15.8 %collective-permute-start.66 = (bf16[2,384,384]{2,1,0:T(8,128)(2,1)S(1)}, bf16[2,384,384]{2,1,0:T(8,128)(2,1)S(1)}, u32[]{:S(2)}, u32[]{:S(2)}) collective-permute-start(bf16[2,384,384]{2,1,0:T(8,128)(2,1)S(1)} %get-tuple-element.512), channel_id=1, source_target_pairs={{0,2},{1,3},{2,0},{3,1},{4,6},{5,7},{6,4},{7,5},{8,10},{9,11},{10,... | collective-permute-start | bytes 1769480 | tf_op jit(solution)/shard_map/ppermute | solution.py:38
  255.3 15.2 %collective-permute-start.65 = (bf16[4,192,384]{2,1,0:T(8,128)(2,1)S(1)}, bf16[4,192,384]{2,1,0:T(8,128)(2,1)S(1)}, u32[]{:S(2)}, u32[]{:S(2)}) collective-permute-start(bf16[4,192,384]{2,1,0:T(8,128)(2,1)S(1)} %get-tuple-element.503), channel_id=1, source_target_pairs={{0,1},{1,0},{2,3},{3,2},{4,5},{5,4},{6,7},{7,6},{8,9},{9,8},{10,11... | collective-permute-start | bytes 1769480 | tf_op jit(solution)/shard_map/ppermute | solution.py:38
  275.0 16.2 %collective-permute-start.72 = (bf16[4,192,384]{2,1,0:T(8,128)(2,1)S(1)}, bf16[4,192,384]{2,1,0:T(8,128)(2,1)S(1)}, u32[]{:S(2)}, u32[]{:S(2)}) collective-permute-start(bf16[4,192,384]{2,1,0:T(8,128)(2,1)S(1)} %get-tuple-element.535), channel_id=1, source_target_pairs={{0,1},{1,0},{2,3},{3,2},{4,5},{5,4},{6,7},{7,6},{8,9},{9,8},{10,11... | collective-permute-start | bytes 1769480 | tf_op jit(solution)/shard_map/ppermute | solution.py:38
  276.9 22.2 %collective-permute-start.92 = (bf16[256,768]{1,0:T(8,128)(2,1)S(1)}, bf16[256,768]{1,0:T(8,128)(2,1)S(1)}, u32[]{:S(2)}, u32[]{:S(2)}) collective-permute-start(bf16[256,768]{1,0:T(8,128)(2,1)S(1)} %get-tuple-element.628), channel_id=1, source_target_pairs={{0,8},{8,0},{16,24},{24,16},{1,9},{9,1},{17,25},{25,17},{2,10},{10... | collective-permute-start | bytes 1179656 | tf_op jit(solution)/shard_map/ppermute | solution.py:38
  277.0 16.7 %collective-permute-start.71 = (bf16[1,384,384]{2,1,0:T(8,128)(2,1)S(1)}, bf16[1,384,384]{2,1,0:T(8,128)(2,1)S(1)}, u32[]{:S(2)}, u32[]{:S(2)}) collective-permute-start(bf16[1,384,384]{2,1,0:T(8,128)(2,1)S(1)} %get-tuple-element.527), channel_id=1, source_target_pairs={{0,4},{1,5},{2,6},{3,7},{4,0},{5,1},{6,2},{7,3},{8,12},{9,13},{10,... | collective-permute-start | bytes 884744 | tf_op jit(solution)/shard_map/ppermute | solution.py:38
  281.0 28.1 %collective-permute-start.76 = (bf16[4,192,384]{2,1,0:T(8,128)(2,1)S(1)}, bf16[4,192,384]{2,1,0:T(8,128)(2,1)S(1)}, u32[]{:S(2)}, u32[]{:S(2)}) collective-permute-start(bf16[4,192,384]{2,1,0:T(8,128)(2,1)S(1)} %get-tuple-element.538), channel_id=1, source_target_pairs={{0,1},{1,0},{2,3},{3,2},{4,5},{5,4},{6,7},{7,6},{8,9},{9,8},{10,11... | collective-permute-start | bytes 1769480 | tf_op jit(solution)/shard_map/ppermute | solution.py:38
  296.2 16.9 %collective-permute-start.70 = (bf16[2,192,384]{2,1,0:T(8,128)(2,1)S(1)}, bf16[2,192,384]{2,1,0:T(8,128)(2,1)S(1)}, u32[]{:S(2)}, u32[]{:S(2)}) collective-permute-start(bf16[2,192,384]{2,1,0:T(8,128)(2,1)S(1)} %get-tuple-element.523), channel_id=1, source_target_pairs={{0,2},{1,3},{2,0},{3,1},{4,6},{5,7},{6,4},{7,5},{8,10},{9,11},{10,... | collective-permute-start | bytes 884744 | tf_op jit(solution)/shard_map/ppermute | solution.py:38
  296.4 16.7 %collective-permute-start.75 = (bf16[1,384,384]{2,1,0:T(8,128)(2,1)S(1)}, bf16[1,384,384]{2,1,0:T(8,128)(2,1)S(1)}, u32[]{:S(2)}, u32[]{:S(2)}) collective-permute-start(bf16[1,384,384]{2,1,0:T(8,128)(2,1)S(1)} %merge.23.refs_0_), channel_id=1, source_target_pairs={{0,4},{1,5},{2,6},{3,7},{4,0},{5,1},{6,2},{7,3},{8,12},{9,13},{10,... | collective-permute-start | bytes 884744 | tf_op jit(solution)/shard_map/ppermute | solution.py:38
  299.2 15.6 %collective-permute-start.93 = (bf16[256,768]{1,0:T(8,128)(2,1)S(1)}, bf16[256,768]{1,0:T(8,128)(2,1)S(1)}, u32[]{:S(2)}, u32[]{:S(2)}) collective-permute-start(bf16[256,768]{1,0:T(8,128)(2,1)S(1)} %add_convert_fusion.1.refs_0_), channel_id=1, source_target_pairs={{0,16},{8,24},{16,0},{24,8},{1,17},{9,25},{17,1},{25,9},{2,18},{10... | collective-permute-start | bytes 1179656 | tf_op jit(solution)/shard_map/ppermute | solution.py:38
  316.7 29.6 %collective-permute-start.94 = (bf16[256,768]{1,0:T(8,128)(2,1)S(1)}, bf16[256,768]{1,0:T(8,128)(2,1)S(1)}, u32[]{:S(2)}, u32[]{:S(2)}) collective-permute-start(bf16[256,768]{1,0:T(8,128)(2,1)S(1)} %get-tuple-element.630.refs_0_), channel_id=1, source_target_pairs={{0,8},{8,0},{16,24},{24,16},{1,9},{9,1},{17,25},{25,17},{2,10},{10... | collective-permute-start | bytes 1179656 | tf_op jit(solution)/shard_map/ppermute | solution.py:38
  364.6 42.3 %collective-permute-start.106 = (bf16[4,384,384]{2,1,0:T(8,128)(2,1)S(1)}, bf16[4,384,384]{2,1,0:T(8,128)(2,1)S(1)}, u32[]{:S(2)}, u32[]{:S(2)}) collective-permute-start(bf16[4,384,384]{2,1,0:T(8,128)(2,1)S(1)} %merge.31.refs_0_), channel_id=1, source_target_pairs={{0,1},{1,0},{2,3},{3,2},{4,5},{5,4},{6,7},{7,6},{8,9},{9,8},{10,11... | collective-permute-start | bytes 3538952 | tf_op jit(solution)/shard_map/ppermute | solution.py:38
  366.8 17.3 %collective-permute-start.101 = (bf16[2,384,384]{2,1,0:T(8,128)(2,1)S(1)}, bf16[2,384,384]{2,1,0:T(8,128)(2,1)S(1)}, u32[]{:S(2)}, u32[]{:S(2)}) collective-permute-start(bf16[2,384,384]{2,1,0:T(8,128)(2,1)S(1)} %get-tuple-element.672), channel_id=1, source_target_pairs={{0,2},{1,3},{2,0},{3,1},{4,6},{5,7},{6,4},{7,5},{8,10},{9,11},{10,... | collective-permute-start | bytes 1769480 | tf_op jit(solution)/shard_map/ppermute | solution.py:38
  370.6 31.7 %collective-permute-start.98 = (bf16[4,192,384]{2,1,0:T(8,128)(2,1)S(1)}, bf16[4,192,384]{2,1,0:T(8,128)(2,1)S(1)}, u32[]{:S(2)}, u32[]{:S(2)}) collective-permute-start(bf16[4,192,384]{2,1,0:T(8,128)(2,1)S(1)} %get-tuple-element.651), channel_id=1, source_target_pairs={{0,1},{1,0},{2,3},{3,2},{4,5},{5,4},{6,7},{7,6},{8,9},{9,8},{10,11... | collective-permute-start | bytes 1769480 | tf_op jit(solution)/shard_map/ppermute | solution.py:38
  371.1 13.3 %collective-permute-start.99 = (bf16[1,192,384]{2,1,0:T(8,128)(2,1)S(1)}, bf16[1,192,384]{2,1,0:T(8,128)(2,1)S(1)}, u32[]{:S(2)}, u32[]{:S(2)}) collective-permute-start(bf16[1,192,384]{2,1,0:T(8,128)(2,1)S(1)} %get-tuple-element.657), channel_id=1, source_target_pairs={{0,4},{1,5},{2,6},{3,7},{4,0},{5,1},{6,2},{7,3},{8,12},{9,13},{10,... | collective-permute-start | bytes 442376 | tf_op jit(solution)/shard_map/ppermute | solution.py:38
  384.3 18.8 %collective-permute-start.103 = (bf16[1,384,384]{2,1,0:T(8,128)(2,1)S(1)}, bf16[1,384,384]{2,1,0:T(8,128)(2,1)S(1)}, u32[]{:S(2)}, u32[]{:S(2)}) collective-permute-start(bf16[1,384,384]{2,1,0:T(8,128)(2,1)S(1)} %get-tuple-element.680), channel_id=1, source_target_pairs={{0,4},{1,5},{2,6},{3,7},{4,0},{5,1},{6,2},{7,3},{8,12},{9,13},{10,... | collective-permute-start | bytes 884744 | tf_op jit(solution)/shard_map/ppermute | solution.py:38
  384.4 18.7 %collective-permute-start.105 = (bf16[1,192,384]{2,1,0:T(8,128)(2,1)S(1)}, bf16[1,192,384]{2,1,0:T(8,128)(2,1)S(1)}, u32[]{:S(2)}, u32[]{:S(2)}) collective-permute-start(bf16[1,192,384]{2,1,0:T(8,128)(2,1)S(1)} %merge.30.refs_0_), channel_id=1, source_target_pairs={{0,4},{1,5},{2,6},{3,7},{4,0},{5,1},{6,2},{7,3},{8,12},{9,13},{10,... | collective-permute-start | bytes 442376 | tf_op jit(solution)/shard_map/ppermute | solution.py:38
  387.4 35.8 %collective-permute-start.95 = (bf16[256,768]{1,0:T(8,128)(2,1)S(1)}, bf16[256,768]{1,0:T(8,128)(2,1)S(1)}, u32[]{:S(2)}, u32[]{:S(2)}) collective-permute-start(bf16[256,768]{1,0:T(8,128)(2,1)S(1)} %get-tuple-element.641), channel_id=1, source_target_pairs={{0,8},{8,0},{16,24},{24,16},{1,9},{9,1},{17,25},{25,17},{2,10},{10... | collective-permute-start | bytes 1179656 | tf_op jit(solution)/shard_map/ppermute | solution.py:38
  402.4 13.7 %collective-permute-start.100 = (bf16[2,192,384]{2,1,0:T(8,128)(2,1)S(1)}, bf16[2,192,384]{2,1,0:T(8,128)(2,1)S(1)}, u32[]{:S(2)}, u32[]{:S(2)}) collective-permute-start(bf16[2,192,384]{2,1,0:T(8,128)(2,1)S(1)} %get-tuple-element.662), channel_id=1, source_target_pairs={{0,2},{1,3},{2,0},{3,1},{4,6},{5,7},{6,4},{7,5},{8,10},{9,11},{10,... | collective-permute-start | bytes 884744 | tf_op jit(solution)/shard_map/ppermute | solution.py:38
  403.2 13.0 %collective-permute-start.108 = (bf16[1,384,384]{2,1,0:T(8,128)(2,1)S(1)}, bf16[1,384,384]{2,1,0:T(8,128)(2,1)S(1)}, u32[]{:S(2)}, u32[]{:S(2)}) collective-permute-start(bf16[1,384,384]{2,1,0:T(8,128)(2,1)S(1)} %merge.33.refs_0_), channel_id=1, source_target_pairs={{0,4},{1,5},{2,6},{3,7},{4,0},{5,1},{6,2},{7,3},{8,12},{9,13},{10,... | collective-permute-start | bytes 884744 | tf_op jit(solution)/shard_map/ppermute | solution.py:38
  406.9 13.3 %collective-permute-start.107 = (bf16[2,192,384]{2,1,0:T(8,128)(2,1)S(1)}, bf16[2,192,384]{2,1,0:T(8,128)(2,1)S(1)}, u32[]{:S(2)}, u32[]{:S(2)}) collective-permute-start(bf16[2,192,384]{2,1,0:T(8,128)(2,1)S(1)} %merge.32.refs_0_), channel_id=1, source_target_pairs={{0,2},{1,3},{2,0},{3,1},{4,6},{5,7},{6,4},{7,5},{8,10},{9,11},{10,... | collective-permute-start | bytes 884744 | tf_op jit(solution)/shard_map/ppermute | solution.py:38
  420.4 19.8 %collective-permute-start.113 = (bf16[4,192,384]{2,1,0:T(8,128)(2,1)S(1)}, bf16[4,192,384]{2,1,0:T(8,128)(2,1)}, u32[]{:S(2)}, u32[]{:S(2)}) collective-permute-start(bf16[4,192,384]{2,1,0:T(8,128)(2,1)S(1)} %merge.38.refs_0_), channel_id=1, source_target_pairs={{0,1},{1,0},{2,3},{3,2},{4,5},{5,4},{6,7},{7,6},{8,9},{9,8},{10,11... | collective-permute-start | bytes 1769480 | tf_op jit(solution)/shard_map/ppermute | solution.py:38
  422.1 18.1 %collective-permute-start.111 = (bf16[2,384,384]{2,1,0:T(8,128)(2,1)S(1)}, bf16[2,384,384]{2,1,0:T(8,128)(2,1)}, u32[]{:S(2)}, u32[]{:S(2)}) collective-permute-start(bf16[2,384,384]{2,1,0:T(8,128)(2,1)S(1)} %merge.36.refs_0_), channel_id=1, source_target_pairs={{0,2},{1,3},{2,0},{3,1},{4,6},{5,7},{6,4},{7,5},{8,10},{9,11},{10,... | collective-permute-start | bytes 1769480 | tf_op jit(solution)/shard_map/ppermute | solution.py:38
  435.7 29.6 %collective-permute-start.97 = (bf16[256,768]{1,0:T(8,128)(2,1)}, bf16[256,768]{1,0:T(8,128)(2,1)}, u32[]{:S(2)}, u32[]{:S(2)}) collective-permute-start(bf16[256,768]{1,0:T(8,128)(2,1)} %get-tuple-element.650.refs_0_), channel_id=1, source_target_pairs={{0,8},{8,0},{16,24},{24,16},{1,9},{9,1},{17,25},{25,17},{2,10},{10... | collective-permute-start | bytes 1179656 | tf_op jit(solution)/shard_map/ppermute | solution.py:38
  449.5 22.8 %collective-permute-start.110 = (bf16[2,192,384]{2,1,0:T(8,128)(2,1)S(1)}, bf16[2,192,384]{2,1,0:T(8,128)(2,1)}, u32[]{:S(2)}, u32[]{:S(2)}) collective-permute-start(bf16[2,192,384]{2,1,0:T(8,128)(2,1)S(1)} %merge.35.refs_0_), channel_id=1, source_target_pairs={{0,2},{1,3},{2,0},{3,1},{4,6},{5,7},{6,4},{7,5},{8,10},{9,11},{10,... | collective-permute-start | bytes 884744 | tf_op jit(solution)/shard_map/ppermute | solution.py:38
  457.6 29.0 %collective-permute-start.114 = (bf16[4,384,384]{2,1,0:T(8,128)(2,1)S(1)}, bf16[4,384,384]{2,1,0:T(8,128)(2,1)}, u32[]{:S(2)}, u32[]{:S(2)}) collective-permute-start(bf16[4,384,384]{2,1,0:T(8,128)(2,1)S(1)} %merge.39.refs_0_), channel_id=1, source_target_pairs={{0,1},{1,0},{2,3},{3,2},{4,5},{5,4},{6,7},{7,6},{8,9},{9,8},{10,11... | collective-permute-start | bytes 3538952 | tf_op jit(solution)/shard_map/ppermute | solution.py:38
  460.6 16.3 %collective-permute-start.119 = (f32[22,768]{1,0:T(8,128)S(1)}, f32[22,768]{1,0:T(8,128)S(1)}, u32[]{:S(2)}, u32[]{:S(2)}) collective-permute-start(f32[22,768]{1,0:T(8,128)S(1)} %add.182), channel_id=1, source_target_pairs={{0,4},{1,5},{2,6},{3,7},{4,0},{5,1},{6,2},{7,3},{8,12},{9,13},{10,... | collective-permute-start | bytes 202760 | tf_op jit(solution)/shard_map/ppermute | solution.py:38
  473.3 24.0 %collective-permute-start.112 = (bf16[4,192,384]{2,1,0:T(8,128)(2,1)S(1)}, bf16[4,192,384]{2,1,0:T(8,128)(2,1)S(1)}, u32[]{:S(2)}, u32[]{:S(2)}) collective-permute-start(bf16[4,192,384]{2,1,0:T(8,128)(2,1)S(1)} %merge.37.refs_0_), channel_id=1, source_target_pairs={{0,1},{1,0},{2,3},{3,2},{4,5},{5,4},{6,7},{7,6},{8,9},{9,8},{10,11... | collective-permute-start | bytes 1769480 | tf_op jit(solution)/shard_map/ppermute | solution.py:38
  (150 other events, 1238.4 us)
